TPU v7x, 128 devices: a whole 4x4x4 slice. The times are simulated.
128 devices in a mesh: dp: 8 (over x, core), fsdp: 16 (over y, z).
Axes of the slice: x: 4, y: 4, z: 4, core: 2. Of those that a mesh axis runs over, the one named last changes fastest.
Arguments:
- queries: bfloat16 [24576, 4096], P(('dp', 'fsdp')), may hold values from -6 to 6
- passages: bfloat16 [24576, 4096], P(('dp', 'fsdp')), may hold values from -6 to 6
- head_weight: bfloat16 [4096, 2048], P('fsdp'), may hold values from -0.09375 to 0.09375
- send_lists: int32 [8, 16, 8, 48], P('dp', 'fsdp'), may hold values from 0 to 191
- neg_slots: int32 [24576, 16], P(('dp', 'fsdp')), may hold values from 0 to 383
Outputs:
- query_grads: bfloat16 [24576, 4096], P(('dp', 'fsdp'))
- passage_grads: bfloat16 [24576, 4096], P(('dp', 'fsdp'))
- head_grads: float32 [4096, 2048], P('fsdp', 'dp')
All inputs are finite; a program needn't handle non-finite values.
Results may differ from a plain program's by a relative error of at most 0.025.
Values may be sent and summed in bfloat16 or wider, within the bound.
No kernel may reach another device: no remote copies, remote signals or barrier semaphores. Data moves between devices by JAX's collectives and lax.ppermute only.
A program may use at most 128 MiB of HBM per device.

v0:
```python
import jax
import jax.numpy as jnp
from jax import lax
from jax.sharding import PartitionSpec as P

EPSILON = 1e-06


def rms_scale(values):
    return values * lax.rsqrt(jnp.mean(values * values, axis=-1, keepdims=True) + EPSILON)


def project(states, head):
    return jnp.dot(states, head, preferred_element_type=jnp.float32)


def per_device(queries, passages, head_weight, send_lists, neg_slots):
    head = lax.all_gather(head_weight, "fsdp", axis=0, tiled=True)
    rows_dev = queries.shape[0]
    width = head.shape[1]
    scale = 16.0 / width
    groups = send_lists.shape[2]
    capacity = send_lists.shape[3]
    slot_count = groups * capacity
    flat_lists = send_lists.reshape(slot_count)
    query_pre = project(queries, head)
    passage_pre = project(passages, head)
    query_emb = rms_scale(query_pre).astype(jnp.bfloat16)
    passage_emb = rms_scale(passage_pre).astype(jnp.bfloat16)
    picked = jnp.take(passages, flat_lists, axis=0).reshape(groups, capacity, passages.shape[1])
    arrived = lax.all_to_all(picked, "dp", split_axis=0, concat_axis=0, tiled=True)
    arrived_pre = project(arrived.reshape(slot_count, passages.shape[1]), head)
    fetched = rms_scale(arrived_pre).astype(jnp.bfloat16)
    positive = (
        jnp.einsum("qe,qe->q", query_emb, passage_emb, preferred_element_type=jnp.float32) * scale
    )
    table = (
        lax.dot_general(
            query_emb, fetched, (((1,), (1,)), ((), ())), preferred_element_type=jnp.float32
        )
        * scale
    )
    negative = jnp.take_along_axis(table, neg_slots, axis=1)
    logits = jnp.concatenate([positive[:, None], negative], axis=1)
    probs = jax.nn.softmax(logits, axis=-1)
    target = (jnp.arange(logits.shape[1]) == 0).astype(jnp.float32)
    weights = (probs - target).astype(jnp.bfloat16)
    selector = (
        neg_slots[:, :, None] == jnp.arange(slot_count, dtype=jnp.int32)[None, None, :]
    ).astype(jnp.bfloat16)
    mixing = jnp.einsum(
        "qn,qnr->qr", weights[:, 1:], selector, preferred_element_type=jnp.float32
    ).astype(jnp.bfloat16)
    first = weights[:, :1].astype(jnp.float32)
    query_emb_grad = first * passage_emb.astype(jnp.float32) + jnp.dot(
        mixing, fetched, preferred_element_type=jnp.float32
    )
    fetched_grad = lax.dot_general(
        mixing, query_emb, (((0,), (0,)), ((), ())), preferred_element_type=jnp.float32
    ).astype(jnp.bfloat16)
    returned = lax.all_to_all(
        fetched_grad.reshape(groups, capacity, width), "dp", split_axis=0, concat_axis=0, tiled=True
    )
    owner_matrix = (flat_lists[None, :] == jnp.arange(rows_dev, dtype=jnp.int32)[:, None]).astype(
        jnp.bfloat16
    )
    passage_emb_grad = first * query_emb.astype(jnp.float32) + jnp.dot(
        owner_matrix, returned.reshape(slot_count, width), preferred_element_type=jnp.float32
    )
    _, query_back = jax.vjp(rms_scale, query_pre)
    _, passage_back = jax.vjp(rms_scale, passage_pre)
    query_dy = query_back(query_emb_grad)[0].astype(jnp.bfloat16)
    passage_dy = passage_back(passage_emb_grad)[0].astype(jnp.bfloat16)
    contract = (((1,), (1,)), ((), ()))
    query_grads = lax.dot_general(
        query_dy, head, contract, preferred_element_type=jnp.float32
    ).astype(jnp.bfloat16)
    passage_grads = lax.dot_general(
        passage_dy, head, contract, preferred_element_type=jnp.float32
    ).astype(jnp.bfloat16)
    both_states = jnp.concatenate([queries, passages], axis=0)
    both_slopes = jnp.concatenate([query_dy, passage_dy], axis=0)
    rows_part = lax.psum_scatter(
        (
            lax.dot_general(
                both_states,
                both_slopes,
                (((0,), (0,)), ((), ())),
                preferred_element_type=jnp.float32,
            )
            / 128.0
        ).astype(jnp.bfloat16),
        "fsdp",
        scatter_dimension=0,
        tiled=True,
    )
    head_grads = lax.psum_scatter(rows_part, "dp", scatter_dimension=1, tiled=True).astype(
        jnp.float32
    )
    return (query_grads, passage_grads, head_grads)


def solution(mesh):
    return jax.shard_map(
        per_device,
        mesh=mesh,
        in_specs=(
            P(("dp", "fsdp"), None),
            P(("dp", "fsdp"), None),
            P("fsdp", None),
            P("dp", "fsdp", None, None),
            P(("dp", "fsdp"), None),
        ),
        out_specs=(P(("dp", "fsdp"), None), P(("dp", "fsdp"), None), P("fsdp", "dp")),
        check_vma=False,
    )
```

profile of v0, /device:TPU:0, one launch (start us, length us, event | category | flops | bytes accessed | tf_op | source)
XLA Modules:
  0.0 368.7 jit_solution(8756822943597860565)
XLA Ops:
  8.7 9.1 %gather_fusion = bf16[384,4096]{1,0:T(8,128)(2,1)S(1)} fusion(bf16[192,4096]{1,0:T(8,128)(2,1)} %param.6, s32[1024]{0:T(1024)S(1)} %pad_clamp_fusion), kind=kCustom, calls=%fused_computation | custom fusion | bytes 6292992 | tf_op jit(solution)/shard_map/jit(_take)/gather | solution.py:30
  17.9 2.0 broadcast_select_fusion
  19.9 4.5 %all-to-all-start = ((bf16[8,48,4096]{2,1,0:T(8,128)(2,1)}), bf16[8,48,4096]{2,1,0:T(8,128)(2,1)S(1)}, u32[]{:S(2)}, u32[]{:S(2)}) async-start(bf16[8,48,4096]{2,1,0:T(8,128)(2,1)} %broadcast_select_fusion), calls=%async_computation | async-start | bytes 6291456 | tf_op jit(solution)/shard_map/all_to_all | solution.py:31
  26.0 36.8 %all-to-all-done = bf16[8,48,4096]{2,1,0:T(8,128)(2,1)S(1)} async-done(((bf16[8,48,4096]{2,1,0:T(8,128)(2,1)}), bf16[8,48,4096]{2,1,0:T(8,128)(2,1)S(1)}, u32[]{:S(2)}, u32[]{:S(2)}) %all-to-all-start) | async-done | bytes 3145760 | tf_op jit(solution)/shard_map/all_to_all | solution.py:31
  62.8 61.3 %all-gather.2.cloned.1.call-done = bf16[4096,2048]{1,0:T(8,128)(2,1)} async-done(((bf16[256,2048]{1,0:T(8,128)(2,1)}), bf16[4096,2048]{1,0:T(8,128)(2,1)}) %all-gather.2.cloned.1.call-update) | async-done | bytes 16777232 | tf_op jit(solution)/shard_map/all_gather | solution.py:18
  124.1 11.4 %multiply_reduce_fusion = (f32[384]{0:T(512)S(1)}, f32[384,2048]{1,0:T(8,128)S(1)}) fusion(bf16[384,4096]{1,0:T(8,128)(2,1)} %bitcast.42, bf16[4096,2048]{1,0:T(8,128)(2,1)} %all-gather.2.cloned.1.call-done), kind=kOutput, calls=%fused_computation.11 | convolution fusion | flops 6444023296 | bytes 23070208 | tf_op jit(solution)/shard_map/dot_general | solution.py:14
  136.0 3.8 %multiply_reduce_fusion.3 = (f32[192]{0:T(256)S(1)}, f32[192,2048]{1,0:T(8,128)S(1)}) fusion(bf16[192,4096]{1,0:T(8,128)(2,1)S(1)} %copy-done, bf16[4096,2048]{1,0:T(8,128)(2,1)S(1)} %copy-done.22), kind=kOutput, calls=%fused_computation.31 | convolution fusion | flops 3222011648 | bytes 19923712 | tf_op jit(solution)/shard_map/dot_general | solution.py:14
  139.8 3.7 %multiply_reduce_fusion.4 = (f32[192]{0:T(256)S(1)}, f32[192,2048]{1,0:T(8,128)S(1)}) fusion(bf16[192,4096]{1,0:T(8,128)(2,1)S(1)} %copy-done.23, bf16[4096,2048]{1,0:T(8,128)(2,1)S(1)} %copy-done.22), kind=kOutput, calls=%fused_computation.33 | convolution fusion | flops 3222011648 | bytes 19923712 | tf_op jit(solution)/shard_map/dot_general | solution.py:14
  144.7 0.9 copy-done.4
  146.4 24.8 %gather_fusion.1 = f32[3072]{0:T(1024)S(1)} fusion(f32[192,384]{1,0:T(8,128)S(1)} %convolution_multiply_fusion, s32[3072]{0:T(1024)S(1)} %reshape.142), kind=kCustom, calls=%fused_computation.1 | custom fusion | bytes 49152 | tf_op jit(solution)/shard_map/jit(take_along_axis)/gather | solution.py:43
  171.6 2.1 fusion
  173.7 1.7 convolution_convert_fusion.2
  175.5 4.4 %all-to-all-start.1 = ((bf16[8,48,2048]{2,1,0:T(8,128)(2,1)}), bf16[8,48,2048]{2,1,0:T(8,128)(2,1)}, u32[]{:S(2)}, u32[]{:S(2)}) async-start(bf16[8,48,2048]{2,1,0:T(8,128)(2,1)} %bitcast.41), calls=%async_computation.1 | async-start | bytes 3145728 | tf_op jit(solution)/shard_map/all_to_all | solution.py:61
  180.2 3.3 multiply_reduce_fusion.2
  183.6 1.2 fusion.6
  184.8 16.7 %all-to-all-done.1 = bf16[8,48,2048]{2,1,0:T(8,128)(2,1)} async-done(((bf16[8,48,2048]{2,1,0:T(8,128)(2,1)}), bf16[8,48,2048]{2,1,0:T(8,128)(2,1)}, u32[]{:S(2)}, u32[]{:S(2)}) %all-to-all-start.1) | async-done | bytes 1572896 | tf_op jit(solution)/shard_map/all_to_all | solution.py:61
  201.5 2.4 multiply_reduce_fusion.1
  204.3 0.9 copy-done.9
  205.9 12.4 %multiply_convert_fusion = bf16[4096,2048]{1,0:T(8,128)(2,1)} fusion(bf16[192,4096]{1,0:T(8,128)(2,1)S(1)} %copy-done, bf16[192,4096]{1,0:T(8,128)(2,1)S(1)} %copy-done.24, bf16[192,2048]{1,0:T(8,128)(2,1)S(1)} %fusion.7, bf16[192,2048]{1,0:T(8,128)(2,1)S(1)} %copy-done.7), kind=kOutput, calls=%fused_computation.2 | convolution fusion | flops 6468665344 | bytes 21495808 | tf_op jit(solution)/shard_map/dot_general | solution.py:85
  218.6 108.4 %reduce-scatter.3.cloned.1.call-done = bf16[256,2048]{1,0:T(8,128)(2,1)} async-done(((bf16[4096,2048]{1,0:T(8,128)(2,1)}), bf16[256,2048]{1,0:T(8,128)(2,1)}) %reduce-scatter.3.cloned.1.call-update) | async-done | bytes 1048592 | tf_op jit(solution)/shard_map/reduce_scatter | solution.py:83
  327.0 12.6 %convolution_convert_fusion.1 = bf16[192,4096]{1,0:T(8,128)(2,1)} fusion(bf16[192,2048]{1,0:T(8,128)(2,1)S(1)} %copy-done.8, bf16[4096,2048]{1,0:T(8,128)(2,1)} %all-gather.2.cloned.1.call-done), kind=kOutput, calls=%fused_computation.4 | convolution fusion | flops 3222011904 | bytes 19136512 | tf_op jit(solution)/shard_map/dot_general | solution.py:75
  339.6 12.7 %convolution_convert_fusion = bf16[192,4096]{1,0:T(8,128)(2,1)} fusion(bf16[192,2048]{1,0:T(8,128)(2,1)S(1)} %copy-done.10, bf16[4096,2048]{1,0:T(8,128)(2,1)} %all-gather.2.cloned.1.call-done), kind=kOutput, calls=%fused_computation.3 | convolution fusion | flops 3222011904 | bytes 19136512 | tf_op jit(solution)/shard_map/dot_general | solution.py:78
  352.3 8.3 %reduce-scatter.5.cloned.1.call-done = bf16[256,256]{1,0:T(8,128)(2,1)} async-done(((bf16[256,2048]{1,0:T(8,128)(2,1)}), bf16[256,256]{1,0:T(8,128)(2,1)}) %reduce-scatter.5.cloned.1.call-update) | async-done | bytes 131088 | tf_op jit(solution)/shard_map/reduce_scatter | solution.py:97
  360.6 1.6 convert_element_type.66
  (80 shorter events, 7.6 us)
Async XLA Ops:
  7.2 116.9 %all-gather.2.cloned.1.call-start = ((), (), s32[]{:S(2)}) async-start(), calls=%async_computation.4 | async-start | bytes 17825792 | tf_op jit(solution)/shard_map/all_gather | solution.py:18
  8.7 9.1 %copy-start.12 = (s32[1,1,8,48]{3,2,1,0:T(8,128)S(1)}, s32[1,1,8,48]{3,2,1,0:T(8,128)}, u32[]{:S(2)}) copy-start(s32[1,1,8,48]{3,2,1,0:T(8,128)} %param.8) | copy-start | bytes 4612
  19.9 5.2 %copy-start.11 = (s32[192,16]{0,1:T(8,128)S(1)}, s32[192,16]{0,1:T(8,128)}, u32[]{:S(2)}) copy-start(s32[192,16]{0,1:T(8,128)} %param.9) | copy-start | bytes 36868
  19.9 43.0 %all-to-all-start = ((bf16[8,48,4096]{2,1,0:T(8,128)(2,1)}), bf16[8,48,4096]{2,1,0:T(8,128)(2,1)S(1)}, u32[]{:S(2)}, u32[]{:S(2)}) async-start(bf16[8,48,4096]{2,1,0:T(8,128)(2,1)} %broadcast_select_fusion), calls=%async_computation | async-start | bytes 6291456 | tf_op jit(solution)/shard_map/all_to_all | solution.py:31
  62.8 61.3 %copy-start.6 = (bf16[8,48,4096]{2,1,0:T(8,128)(2,1)}, bf16[8,48,4096]{2,1,0:T(8,128)(2,1)S(1)}, u32[]{:S(2)}) copy-start(bf16[8,48,4096]{2,1,0:T(8,128)(2,1)S(1)} %all-to-all-done) | copy-start | bytes 9437188
  124.1 11.5 %copy-start = (bf16[192,4096]{1,0:T(8,128)(2,1)S(1)}, bf16[192,4096]{1,0:T(8,128)(2,1)}, u32[]{:S(2)}) copy-start(bf16[192,4096]{1,0:T(8,128)(2,1)} %param.6) | copy-start | bytes 4718596
  124.1 11.9 %copy-start.22 = (bf16[4096,2048]{1,0:T(8,128)(2,1)S(1)}, bf16[4096,2048]{1,0:T(8,128)(2,1)}, u32[]{:S(2)}) copy-start(bf16[4096,2048]{1,0:T(8,128)(2,1)} %all-gather.2.cloned.1.call-done) | copy-start | bytes 50331652
  135.6 9.1 %copy-start.3 = (f32[384,2048]{1,0:T(8,128)}, f32[384,2048]{1,0:T(8,128)S(1)}, u32[]{:S(2)}) copy-start(f32[384,2048]{1,0:T(8,128)S(1)} %get-tuple-element.14) | copy-start | bytes 9437188
  136.0 3.8 %copy-start.23 = (bf16[192,4096]{1,0:T(8,128)(2,1)S(1)}, bf16[192,4096]{1,0:T(8,128)(2,1)}, u32[]{:S(2)}) copy-start(bf16[192,4096]{1,0:T(8,128)(2,1)} %param.5) | copy-start | bytes 4718596
  139.8 3.7 %copy-start.18 = (f32[192]{0:T(256)}, f32[192]{0:T(256)S(1)}, u32[]{:S(2)}) copy-start(f32[192]{0:T(256)S(1)} %get-tuple-element.9) | copy-start | bytes 2308
  171.6 2.1 copy-start.5
  175.5 4.7 %copy-start.14 = (f32[192]{0:T(256)S(1)}, f32[192]{0:T(256)}, u32[]{:S(2)}) copy-start(f32[192]{0:T(256)} %copy-done.13) | copy-start | bytes 2308
  175.5 26.1 %all-to-all-start.1 = ((bf16[8,48,2048]{2,1,0:T(8,128)(2,1)}), bf16[8,48,2048]{2,1,0:T(8,128)(2,1)}, u32[]{:S(2)}, u32[]{:S(2)}) async-start(bf16[8,48,2048]{2,1,0:T(8,128)(2,1)} %bitcast.41), calls=%async_computation.1 | async-start | bytes 3145728 | tf_op jit(solution)/shard_map/all_to_all | solution.py:61
  179.9 147.0 %reduce-scatter.3.cloned.1.call-start = ((), (), s32[]{:S(2)}) async-start(), calls=%async_computation.5 | async-start | bytes 17825792 | tf_op jit(solution)/shard_map/reduce_scatter | solution.py:83
  180.2 3.4 copy-start.21
  180.2 3.4 copy-start.2
  180.2 3.4 copy-start.16
  183.6 17.9 %copy-start.17 = (s32[384]{0:T(512)S(1)}, s32[384]{0:T(512)}, u32[]{:S(2)}) copy-start(s32[384]{0:T(512)} %reshape.130) | copy-start | bytes 4612
  201.5 2.4 copy-start.19
  203.9 1.3 copy-start.7
  203.9 1.9 copy-start.24
  218.2 108.7 %copy-start.8 = (bf16[192,2048]{1,0:T(8,128)(2,1)S(1)}, bf16[192,2048]{1,0:T(8,128)(2,1)}, u32[]{:S(2)}) copy-start(bf16[192,2048]{1,0:T(8,128)(2,1)} %fusion.6) | copy-start | bytes 2359300
  218.3 142.3 %reduce-scatter.5.cloned.1.call-start = ((), (), s32[]{:S(2)}) async-start(), calls=%async_computation.6 | async-start | bytes 1179648 | tf_op jit(solution)/shard_map/reduce_scatter | solution.py:97
  327.0 12.6 %copy-start.10 = (bf16[192,2048]{1,0:T(8,128)(2,1)S(1)}, bf16[192,2048]{1,0:T(8,128)(2,1)}, u32[]{:S(2)}) copy-start(bf16[192,2048]{1,0:T(8,128)(2,1)} %copy-done.9) | copy-start | bytes 2359300
  (6 other events, 6.3 us)
Sparse Core Ops, SparseCore 0:
  10.1 113.9 all-gather.1
  218.4 108.5 reduce-scatter.2
  329.3 31.2 reduce-scatter.4
where the time goes:
time: 369 us
  waiting for transfers between devices  232 us (63%)
  matrix products  66.9 us (18%)
  local copies, waits for them, and re-layouts  40.2 us (11%)
  between operations  14.1 us (4%)
  starting transfers between devices  9.55 us (3%)
  other arithmetic  5.75 us (2%)
    reduce_scatter x1, waiting for transfers between devices, per_device(): lax.psum_scatter((lax.dot_general(both_states, both_slopes, (((0,), (0,))...  108 us
    all_gather x1, waiting for transfers between devices, per_device(): head = lax.all_gather(head_weight, 'fsdp', axis=0, tiled=True)  61.3 us
    all_to_all x1, waiting for transfers between devices, per_device(): lax.all_to_all(picked, 'dp', split_axis=0, concat_axis=0, tiled=True)  36.8 us
    gather x5, local copies, waits for them, and re-layouts, per_device(): negative = jnp.take_along_axis(table, neg_slots, axis=1)  25.1 us
    dot_general x3, matrix products, project(): return jnp.dot(states, head, preferred_element_type=jnp.float32)  18.9 us
    all_to_all x1, waiting for transfers between devices, per_device(): lax.all_to_all(fetched_grad.reshape(groups, capacity, width), 'dp', split...  16.7 us
    dot_general x1, matrix products, per_device(): lax.dot_general(passage_dy, head, contract, preferred_element_type=jnp.fl...  12.7 us
    dot_general x1, matrix products, per_device(): lax.dot_general(query_dy, head, contract, preferred_element_type=jnp.floa...  12.6 us
  transfers between devices with their start and end apart: 5, of which 5 were waited for; matrix products, arithmetic and copies ran while one was open for 12% of the time, Pallas kernels for 0%

commit v1 on v0

v1 whole, which is shorter than its diff:
```python
import jax
import jax.numpy as jnp
from jax import lax
from jax.experimental import pallas as pl
from jax.experimental.pallas import tpu as pltpu
from jax.sharding import Mesh, PartitionSpec as P

EPSILON = 1e-06
BLOCK = 256
RING = 4
SWAP = [(0, 1), (1, 0)]
BF16 = jnp.bfloat16
F32 = jnp.float32


def shift(value, place, step):
    pairs = []
    for c in range(2):
        for y in range(RING):
            for z in range(RING):
                to_y, to_z = y, z
                if (place == 1) == (c == 0):
                    to_y = (y + step) % RING
                else:
                    to_z = (z + step) % RING
                pairs.append((c * 16 + y * 4 + z, c * 16 + to_y * 4 + to_z))
    return lax.ppermute(value, ("c", "y", "z"), pairs)


def swap(value):
    return lax.ppermute(value, "c", SWAP)


def block_at(core, d1, d2):
    y, z = lax.axis_index("y"), lax.axis_index("z")
    far_y = jnp.where(core == 0, d1, d2)
    far_z = jnp.where(core == 0, d2, d1)
    return ((y + far_y) % RING) * RING + (z + far_z) % RING


def gather_head(own):
    up = shift(own, 1, 1)
    down = shift(own, 1, -1)
    half = own.shape[0] // 2
    first = jnp.concatenate([own, up], axis=0)
    first_up = shift(first, 2, 1)
    first_down = shift(first, 2, -1)
    far_a = shift(up[:half], 1, 1)
    far_b = shift(down[half:], 1, -1)
    second = jnp.concatenate([down, far_a, far_b], axis=0)
    second_up = shift(second, 2, 1)
    second_down = shift(second, 2, -1)
    first_far = shift(first_up, 2, 1)
    second_far = shift(second_down, 2, -1)
    pieces = [first, second, first_up, first_down, second_up, second_down, first_far, second_far]
    a, b = (0, -1), (1, 2)
    places = [(a, 0), (b, 0), (a, -1), (a, 1), (b, -1), (b, 1), (a, 2), (b, 2)]
    return pieces, [(d1, d2) for d1s, d2 in places for d1 in d1s]


def place_kernel(at_ref, *refs):
    pieces, out_ref, sems = refs[:16], refs[16], refs[17]
    copies = []
    for i, piece in enumerate(pieces):
        for j in range(2):
            k = 2 * i + j
            row = pl.multiple_of(at_ref[0, k] * BLOCK, BLOCK)
            col = pl.multiple_of(at_ref[1, k] * 1024, 1024)
            copies.append(
                pltpu.make_async_copy(
                    piece.at[pl.ds(j * BLOCK, BLOCK), :],
                    out_ref.at[pl.ds(row, BLOCK), pl.ds(col, 1024)],
                    sems.at[k],
                )
            )
    for copy in copies:
        copy.start()
    for copy in copies:
        copy.wait()


def place_head(pieces, at):
    return pl.pallas_call(
        place_kernel,
        grid_spec=pltpu.PrefetchScalarGridSpec(
            num_scalar_prefetch=1,
            grid=(1,),
            in_specs=[pl.BlockSpec(memory_space=pl.ANY)] * 16,
            out_specs=pl.BlockSpec(memory_space=pl.ANY),
            scratch_shapes=[pltpu.SemaphoreType.DMA((32,))],
        ),
        out_shape=jax.ShapeDtypeStruct((4096, 2048), BF16),
        name="place_head",
    )(at, *pieces)


def partial_kernel(at_ref, states_ref, slopes_ref, *refs):
    out_ref = refs[-1]
    total = lax.dot_general(
        states_ref[...], slopes_ref[...], (((0,), (0,)), ((), ())), preferred_element_type=F32
    ) * (1.0 / 128.0)
    for ref in refs[:-1]:
        total = total + ref[...].astype(F32)
    out_ref[...] = total.astype(BF16)


def head_partial(states, slopes, at, adds=()):
    count = at.shape[0]
    rows, width = slopes.shape
    return pl.pallas_call(
        partial_kernel,
        grid_spec=pltpu.PrefetchScalarGridSpec(
            num_scalar_prefetch=1,
            grid=(count,),
            in_specs=[
                pl.BlockSpec((rows, BLOCK), lambda k, at: (0, at[k])),
                pl.BlockSpec((rows, width), lambda k, at: (0, 0)),
            ]
            + [pl.BlockSpec((BLOCK, width), lambda k, at: (k, 0))] * len(adds),
            out_specs=pl.BlockSpec((BLOCK, width), lambda k, at: (k, 0)),
        ),
        out_shape=jax.ShapeDtypeStruct((count * BLOCK, width), BF16),
        compiler_params=pltpu.CompilerParams(vmem_limit_bytes=32 * 1024 * 1024),
        name="head_partial",
    )(at, states, slopes, *adds)


def add(*values):
    total = values[0].astype(F32)
    for value in values[1:]:
        total = total + value.astype(F32)
    return total.astype(BF16)


def scatter_head(states, slopes, core):
    def part(d1, d2s, *adds):
        at = jnp.stack([block_at(core, d1, d2) for d2 in d2s]).astype(jnp.int32)
        return head_partial(states, slopes, at, adds)

    a, b = (2, 1), (-1, 0)
    far_a = shift(part(2, a), 1, 1)
    far_b = shift(part(2, b), 1, -1)
    up_b = shift(part(1, b), 1, 1)
    down_a = shift(part(-1, a), 1, -1)
    up_a = shift(part(1, a, far_a), 1, 1)
    down_b = shift(part(-1, b, far_b), 1, -1)
    mine_a = part(0, a, down_a, up_a)
    mine_b = part(0, b, up_b, down_b)
    far, up, down, mine = mine_a[:BLOCK], mine_a[BLOCK:], mine_b[:BLOCK], mine_b[BLOCK:]
    half = BLOCK // 2
    far_a = shift(far[:half], 2, 1)
    far_b = shift(far[half:], 2, -1)
    up_b = shift(up[half:], 2, 1)
    down_a = shift(down[:half], 2, -1)
    up_a = shift(add(up[:half], far_a), 2, 1)
    down_b = shift(add(down[half:], far_b), 2, -1)
    total = jnp.concatenate(
        [add(mine[:half], down_a, up_a), add(mine[half:], up_b, down_b)], axis=0
    )
    out = total[:, :BLOCK].astype(F32)
    for step in (1, 2, 3):
        sent = total[:, step * BLOCK : (step + 1) * BLOCK]
        out = out + lax.ppermute(
            sent, "x", [(i, (i + step) % RING) for i in range(RING)]
        ).astype(F32)
    return out


def inverse_rms(values):
    return lax.rsqrt(jnp.mean(values * values, axis=-1, keepdims=True) + EPSILON)


def rms_back(values, inverse, grad):
    along = jnp.mean(grad * values, axis=-1, keepdims=True)
    return (inverse * grad - values * (inverse * inverse * inverse * along)).astype(BF16)


def dot(a, b, contract=((1,), (0,))):
    return lax.dot_general(a, b, (contract, ((), ())), preferred_element_type=F32)


def per_device(queries, passages, head_weight, send_lists, neg_slots):
    core, x = lax.axis_index("c"), lax.axis_index("x")
    rows_dev, depth = queries.shape
    width = head_weight.shape[1]
    scale = 16.0 / width
    groups, capacity = send_lists.shape[2], send_lists.shape[3]
    slot_count = groups * capacity
    flat_lists = send_lists.reshape(slot_count)

    own_half = lax.dynamic_slice_in_dim(head_weight, core * (width // 2), width // 2, axis=1)
    pieces, places = gather_head(own_half)

    owner = (flat_lists[None, :] == jnp.arange(rows_dev, dtype=jnp.int32)[:, None]).astype(BF16)
    picked = dot(owner, passages, ((0,), (0,))).astype(BF16).reshape(groups, capacity, depth)
    arrived = lax.all_to_all(picked, ("x", "c"), split_axis=0, concat_axis=0, tiled=True)
    arrived = arrived.reshape(slot_count, depth)
    states = jnp.concatenate([queries, passages], axis=0)
    both_states = jnp.concatenate([states, swap(states)], axis=0)
    slot_ids = jnp.arange(slot_count, dtype=jnp.int32)[None, :]
    counts = jnp.zeros((rows_dev, slot_count), F32)
    for j in range(neg_slots.shape[1]):
        counts = counts + (neg_slots[:, j : j + 1] == slot_ids).astype(F32)

    at = jnp.stack(
        [block_at(core, d1, d2) for d1, d2 in places]
        + [block_at(1 - core, d1, d2) for d1, d2 in places]
    )
    side = jnp.concatenate([jnp.full((16,), core), jnp.full((16,), 1 - core)])
    head = place_head(pieces + [swap(piece) for piece in pieces], jnp.stack([at, side]).astype(jnp.int32))

    pre = dot(states, head)
    arrived_pre = dot(arrived, head)
    inverse = inverse_rms(pre)
    emb = (pre * inverse).astype(BF16)
    query_emb, passage_emb = emb[:rows_dev], emb[rows_dev:]
    fetched = (arrived_pre * inverse_rms(arrived_pre)).astype(BF16)

    positive = (
        jnp.sum(query_emb.astype(F32) * passage_emb.astype(F32), axis=1, keepdims=True) * scale
    )
    table = dot(query_emb, fetched, ((1,), (1,))) * scale
    top = jnp.maximum(
        positive, jnp.max(jnp.where(counts > 0, table, -jnp.inf), axis=1, keepdims=True)
    )
    raised = jnp.where(counts > 0, jnp.exp(table - top), 0.0)
    raised_positive = jnp.exp(positive - top)
    whole = raised_positive + jnp.sum(raised * counts, axis=1, keepdims=True)
    first = (raised_positive / whole - 1.0).astype(BF16).astype(F32)
    mixing = ((raised / whole).astype(BF16).astype(F32) * counts).astype(BF16)

    fetched_grad = dot(mixing, query_emb, ((0,), (0,))).astype(BF16)
    returned = lax.all_to_all(
        fetched_grad.reshape(groups, capacity, width),
        ("x", "c"),
        split_axis=0,
        concat_axis=0,
        tiled=True,
    ).reshape(slot_count, width)

    def split(slopes):
        cut = slopes.reshape(slopes.shape[0], RING, 2, BLOCK)
        cut = jnp.concatenate([cut, cut], axis=1)
        cut = lax.dynamic_slice_in_dim(cut, x, RING, axis=1)
        keep = lax.dynamic_index_in_dim(cut, core, 2, keepdims=False)
        send = lax.dynamic_index_in_dim(cut, 1 - core, 2, keepdims=False)
        shape = (slopes.shape[0], RING * BLOCK)
        return keep.reshape(shape), swap(send.reshape(shape))

    query_emb_grad = first * passage_emb.astype(F32) + dot(mixing, fetched)
    query_dy = rms_back(pre[:rows_dev], inverse[:rows_dev], query_emb_grad)
    query_keep, query_other = split(query_dy)
    query_grads = dot(query_dy, head, ((1,), (1,))).astype(BF16)

    passage_emb_grad = first * query_emb.astype(F32) + dot(owner, returned)
    passage_dy = rms_back(pre[rows_dev:], inverse[rows_dev:], passage_emb_grad)
    passage_keep, passage_other = split(passage_dy)
    slopes = jnp.concatenate([query_keep, passage_keep, query_other, passage_other], axis=0)
    head_grads = scatter_head(both_states, slopes, core)
    passage_grads = dot(passage_dy, head, ((1,), (1,))).astype(BF16)
    return (query_grads, passage_grads, head_grads)


def solution(mesh):
    fine = Mesh(mesh.devices.reshape(4, 2, 4, 4), ("x", "c", "y", "z"))
    every = ("x", "c", "y", "z")
    return jax.shard_map(
        per_device,
        mesh=fine,
        in_specs=(
            P(every, None),
            P(every, None),
            P(("y", "z"), None),
            P(("x", "c"), ("y", "z"), None, None),
            P(every, None),
        ),
        out_specs=(P(every, None), P(every, None), P(("y", "z"), ("x", "c"))),
        check_vma=False,
    )
```

time: 369 us -> 757 us (2.05)
  Pallas kernels: 0 us -> 526 us
  waiting for transfers between devices: 232 us -> 74.3 us
  starting transfers between devices: 9.55 us -> 54.3 us
  local copies, waits for them, and re-layouts: 40.2 us -> 22.8 us
  between operations: 14.1 us -> 1.38 us
    pallas_call x0 -> x9, Pallas kernels: none -> 526 us  [the longest x1 510 us: place_head(): pl.pallas_call(place_kernel, grid_spec=pltpu.PrefetchScalarGridSpec(num_s...]
    reduce_scatter x2 -> x0, waiting for transfers between devices: 117 us -> none  [the longest x1 108 us: per_device(): lax.psum_scatter((lax.dot_general(both_states, both_slopes, (((0,), (0,))...]
    all_gather x1 -> x0, waiting for transfers between devices: 61.3 us -> none  [per_device(): head = lax.all_gather(head_weight, 'fsdp', axis=0, tiled=True)]
    ppermute x0 -> x36, waiting for transfers between devices: none -> 57.8 us  [the longest x22 57.7 us: shift(): return lax.ppermute(value, ('c', 'y', 'z'), pairs)]
    ppermute x0 -> x36, starting transfers between devices: none -> 45.3 us  [the longest x22 39 us: shift(): return lax.ppermute(value, ('c', 'y', 'z'), pairs)]
    all_to_all x2, waiting for transfers between devices: 53.6 us -> 16.6 us  [the longest x1 16.6 us: per_device(): lax.all_to_all(fetched_grad.reshape(groups, capacity, width), ('x', 'c'),...]
    gather x6 -> x0, local copies, waits for them, and re-layouts: 34.2 us -> none  [the longest x5 25.1 us: per_device(): negative = jnp.take_along_axis(table, neg_slots, axis=1)]
    unnamed x51 -> x39, local copies, waits for them, and re-layouts: 4.45 us -> 13.9 us
  transfers between devices with their start and end apart: 5 -> 38, of which waited for: 5 -> 13; matrix products, arithmetic and copies ran while one was open for 12% -> 9% of each run, Pallas kernels for 0% -> 70%
where the time goes in v1:
time: 757 us; the launch traced here: 750 us
  Pallas kernels  526 us (69%)
  waiting for transfers between devices  74.3 us (10%)
  matrix products  63.5 us (8%)
  starting transfers between devices  54.3 us (7%)
  local copies, waits for them, and re-layouts  22.8 us (3%)
  other arithmetic  8.16 us (1%)
    pallas_call x1, Pallas kernels, place_head(): pl.pallas_call(place_kernel, grid_spec=pltpu.PrefetchScalarGridSpec(num_s...  510 us
    dot_general x9, matrix products, dot(): lax.dot_general(a, b, (contract, ((), ())), preferred_element_type=F32)  63.5 us
    ppermute x22, waiting for transfers between devices, shift(): return lax.ppermute(value, ('c', 'y', 'z'), pairs)  57.7 us
    ppermute x22, starting transfers between devices, shift(): return lax.ppermute(value, ('c', 'y', 'z'), pairs)  39 us
    all_to_all x1, waiting for transfers between devices, per_device(): lax.all_to_all(fetched_grad.reshape(groups, capacity, width), ('x', 'c'),...  16.6 us
    pallas_call x8, Pallas kernels, head_partial(): pl.pallas_call(partial_kernel, grid_spec=pltpu.PrefetchScalarGridSpec(num...  15.5 us
  transfers between devices with their start and end apart: 38, of which 13 were waited for; matrix products, arithmetic and copies ran while one was open for 9% of the time, Pallas kernels for 70%

profile of v1, /device:TPU:0, one launch (start us, length us, event | category | flops | bytes accessed | tf_op | source)
XLA Modules:
  0.0 750.3 jit_solution(7279119787401283917)
XLA Ops:
  5.2 7.2 collective-permute-done
  22.5 6.0 collective-permute-start.7
  28.5 4.5 collective-permute-done.4.refs_2_
  35.7 8.4 %collective-permute-done.7.refs_5_ = bf16[512,1024]{1,0:T(8,128)(2,1)} collective-permute-done((bf16[512,1024]{1,0:T(8,128)(2,1)}, bf16[512,1024]{1,0:T(8,128)(2,1)}, u32[]{:S(2)}, u32[]{:S(2)}) %collective-permute-start.7) | collective-permute-done | bytes 1048608 | tf_op jit(solution)/shard_map/ppermute | solution.py:27
  44.1 3.4 collective-permute-start.9
  50.4 4.6 all-to-all-start
  56.5 3.6 collective-permute-done.9.refs_7_
  60.3 3.5 constant_dynamic-update-slice_fusion.7
  66.6 510.4 %place_head.1 = bf16[4096,2048]{1,0:T(8,128)(2,1)} custom-call(s32[2,32]{1,0:T(2,128)} %pad_add_fusion.at_ref, bf16[512,1024]{1,0:T(8,128)(2,1)} %copy-done.7, bf16[512,1024]{1,0:T(8,128)(2,1)} %constant_dynamic-update-slice_fusion.2.refs_1_, bf16[512,1024]{1,0:T(8,128)(2,1)} %collective-permute-done.4.refs_2_, bf16[512,1024]{1,0:T(8,128)(2,1)} %copy-done.8, ...), custom_call_target="tpu_custom_call" | custom-call | tf_op jit(solution)/shard_map/place_head/pallas_call | solution.py:83
  577.0 12.4 %multiply_reduce_fusion.1 = (f32[384]{0:T(512)S(1)}, f32[384,2048]{1,0:T(8,128)}) fusion(bf16[384,4096]{1,0:T(8,128)(2,1)} %get-tuple-element.8, bf16[4096,2048]{1,0:T(8,128)(2,1)} %place_head.1), kind=kOutput, calls=%fused_computation.6 | convolution fusion | flops 6444023296 | bytes 23070208 | tf_op jit(solution)/shard_map/dot_general | solution.py:179
  589.4 11.4 %multiply_reduce_fusion = (f32[384]{0:T(512)S(1)}, f32[384,2048]{1,0:T(8,128)S(1)}) fusion(bf16[384,4096]{1,0:T(8,128)(2,1)} %bitcast.47, bf16[4096,2048]{1,0:T(8,128)(2,1)} %place_head.1), kind=kOutput, calls=%fused_computation.4 | convolution fusion | flops 6444023296 | bytes 23070208 | tf_op jit(solution)/shard_map/dot_general | solution.py:179
  607.1 4.4 all-to-all-start.1
  612.4 4.3 convolution_add_fusion.1
  616.7 16.6 %all-to-all-done.1 = bf16[8,48,2048]{2,1,0:T(8,128)(2,1)} async-done(((bf16[8,48,2048]{2,1,0:T(8,128)(2,1)}), bf16[8,48,2048]{2,1,0:T(8,128)(2,1)}, u32[]{:S(2)}, u32[]{:S(2)}) %all-to-all-start.1) | async-done | bytes 1572896 | tf_op jit(solution)/shard_map/all_to_all | solution.py:233
  633.2 3.8 multiply_reduce_fusion.2
  645.3 3.9 constant_dynamic-update-slice_fusion.5.states_ref
  656.3 3.3 collective-permute-start.22
  661.7 8.6 %collective-permute-done.26.refs_0_ = bf16[512,1024]{1,0:T(8,128)(2,1)S(1)} collective-permute-done((bf16[512,1024]{1,0:T(8,128)(2,1)S(1)}, bf16[512,1024]{1,0:T(8,128)(2,1)S(1)}, u32[]{:S(2)}, u32[]{:S(2)}) %collective-permute-start.26) | collective-permute-done | bytes 1048608 | tf_op jit(solution)/shard_map/ppermute | solution.py:27
  676.8 3.3 collective-permute-start.23
  683.2 5.6 collective-permute-done.27.refs_1_
  692.0 10.8 %collective-permute-done.21.refs_0_ = bf16[512,1024]{1,0:T(8,128)(2,1)S(1)} collective-permute-done((bf16[512,1024]{1,0:T(8,128)(2,1)S(1)}, bf16[512,1024]{1,0:T(8,128)(2,1)S(1)}, u32[]{:S(2)}, u32[]{:S(2)}) %collective-permute-start.21) | collective-permute-done | bytes 1048608 | tf_op jit(solution)/shard_map/ppermute | solution.py:27
  704.9 3.8 collective-permute-start.24
  719.3 12.6 %convolution_convert_fusion.1 = bf16[192,4096]{1,0:T(8,128)(2,1)} fusion(bf16[192,2048]{1,0:T(8,128)(2,1)S(1)} %get-tuple-element.5, bf16[4096,2048]{1,0:T(8,128)(2,1)} %place_head.1), kind=kOutput, calls=%fused_computation.1 | convolution fusion | flops 3222011904 | bytes 19136512 | tf_op jit(solution)/shard_map/dot_general | solution.py:179
  736.6 12.6 %convolution_convert_fusion.2 = bf16[192,4096]{1,0:T(8,128)(2,1)} fusion(bf16[192,2048]{1,0:T(8,128)(2,1)S(1)} %get-tuple-element.6, bf16[4096,2048]{1,0:T(8,128)(2,1)} %place_head.1), kind=kOutput, calls=%fused_computation.2 | convolution fusion | flops 3222011904 | bytes 19136512 | tf_op jit(solution)/shard_map/dot_general | solution.py:179
  (153 shorter events, 80.0 us)
Async XLA Ops:
  15.9 17.1 %collective-permute-start.4 = (bf16[512,1024]{1,0:T(8,128)(2,1)S(1)}, bf16[512,1024]{1,0:T(8,128)(2,1)}, u32[]{:S(2)}, u32[]{:S(2)}) collective-permute-start(bf16[512,1024]{1,0:T(8,128)(2,1)S(1)} %pad_maximum_fusion.refs_0_), channel_id=1, source_target_pairs={{0,1},{1,2},{2,3},{3,0},{4,5},{5,6},{6,7},{7,4},{8,9},{9,10},{10,1... | collective-permute-start | bytes 3145736 | tf_op jit(solution)/shard_map/ppermute | solution.py:27
  18.0 15.0 %collective-permute-start.5 = (bf16[512,1024]{1,0:T(8,128)(2,1)S(1)}, bf16[512,1024]{1,0:T(8,128)(2,1)S(1)}, u32[]{:S(2)}, u32[]{:S(2)}) collective-permute-start(bf16[512,1024]{1,0:T(8,128)(2,1)S(1)} %pad_maximum_fusion.refs_0_), channel_id=1, source_target_pairs={{0,3},{1,0},{2,1},{3,2},{4,7},{5,4},{6,5},{7,6},{8,11},{9,8},{10,9... | collective-permute-start | bytes 3145736 | tf_op jit(solution)/shard_map/ppermute | solution.py:27
  20.2 14.5 %collective-permute-start.10 = (bf16[512,1024]{1,0:T(8,128)(2,1)S(1)}, bf16[512,1024]{1,0:T(8,128)(2,1)S(1)}, u32[]{:S(2)}, u32[]{:S(2)}) collective-permute-start(bf16[512,1024]{1,0:T(8,128)(2,1)S(1)} %pad_maximum_fusion.refs_0_), channel_id=1, source_target_pairs={{0,16},{16,0},{1,17},{17,1},{2,18},{18,2},{3,19},{19,3},{4,20},{20... | collective-permute-start | bytes 3145736 | tf_op jit(solution)/shard_map/ppermute | solution.py:31
  22.5 21.7 %collective-permute-start.7 = (bf16[512,1024]{1,0:T(8,128)(2,1)}, bf16[512,1024]{1,0:T(8,128)(2,1)}, u32[]{:S(2)}, u32[]{:S(2)}) collective-permute-start(bf16[512,1024]{1,0:T(8,128)(2,1)} %constant_dynamic-update-slice_fusion.2.refs_1_), channel_id=1, source_target_pairs={{0,3},{1,0},{2,1},{3,2},{4,7},{5,4},{6,5},{7,6},{8,11},{9,8},{10,9... | collective-permute-start | bytes 3145736 | tf_op jit(solution)/shard_map/ppermute | solution.py:27
  28.5 26.5 %collective-permute-start.6 = (bf16[512,1024]{1,0:T(8,128)(2,1)}, bf16[512,1024]{1,0:T(8,128)(2,1)}, u32[]{:S(2)}, u32[]{:S(2)}) collective-permute-start(bf16[512,1024]{1,0:T(8,128)(2,1)} %constant_dynamic-update-slice_fusion.2.refs_1_), channel_id=1, source_target_pairs={{0,1},{1,2},{2,3},{3,0},{4,5},{5,6},{6,7},{7,4},{8,9},{9,10},{10,1... | collective-permute-start | bytes 3145736 | tf_op jit(solution)/shard_map/ppermute | solution.py:27
  33.0 22.5 %collective-permute-start.11 = (bf16[512,1024]{1,0:T(8,128)(2,1)}, bf16[512,1024]{1,0:T(8,128)(2,1)}, u32[]{:S(2)}, u32[]{:S(2)}) collective-permute-start(bf16[512,1024]{1,0:T(8,128)(2,1)} %constant_dynamic-update-slice_fusion.2.refs_1_), channel_id=1, source_target_pairs={{0,16},{16,0},{1,17},{17,1},{2,18},{18,2},{3,19},{19,3},{4,20},{20... | collective-permute-start | bytes 3145736 | tf_op jit(solution)/shard_map/ppermute | solution.py:31
  33.0 23.0 %collective-permute-start.8 = (bf16[512,1024]{1,0:T(8,128)(2,1)}, bf16[512,1024]{1,0:T(8,128)(2,1)}, u32[]{:S(2)}, u32[]{:S(2)}) collective-permute-start(bf16[512,1024]{1,0:T(8,128)(2,1)} %collective-permute-done.4.refs_2_), channel_id=1, source_target_pairs={{0,1},{1,2},{2,3},{3,0},{4,5},{5,6},{6,7},{7,4},{8,9},{9,10},{10,1... | collective-permute-start | bytes 3145736 | tf_op jit(solution)/shard_map/ppermute | solution.py:27
  34.7 21.3 %collective-permute-start.12 = (bf16[512,1024]{1,0:T(8,128)(2,1)}, bf16[512,1024]{1,0:T(8,128)(2,1)}, u32[]{:S(2)}, u32[]{:S(2)}) collective-permute-start(bf16[512,1024]{1,0:T(8,128)(2,1)} %collective-permute-done.4.refs_2_), channel_id=1, source_target_pairs={{0,16},{16,0},{1,17},{17,1},{2,18},{18,2},{3,19},{19,3},{4,20},{20... | collective-permute-start | bytes 3145736 | tf_op jit(solution)/shard_map/ppermute | solution.py:31
  44.1 16.0 %collective-permute-start.9 = (bf16[512,1024]{1,0:T(8,128)(2,1)}, bf16[512,1024]{1,0:T(8,128)(2,1)}, u32[]{:S(2)}, u32[]{:S(2)}) collective-permute-start(bf16[512,1024]{1,0:T(8,128)(2,1)} %collective-permute-done.7.refs_5_), channel_id=1, source_target_pairs={{0,3},{1,0},{2,1},{3,2},{4,7},{5,4},{6,5},{7,6},{8,11},{9,8},{10,9... | collective-permute-start | bytes 3145736 | tf_op jit(solution)/shard_map/ppermute | solution.py:27
  50.4 539.0 %all-to-all-start = ((bf16[8,48,4096]{2,1,0:T(8,128)(2,1)}), bf16[8,48,4096]{2,1,0:T(8,128)(2,1)}, u32[]{:S(2)}, u32[]{:S(2)}) async-start(bf16[8,48,4096]{2,1,0:T(8,128)(2,1)} %bitcast.85), calls=%async_computation | async-start | bytes 6291456 | tf_op jit(solution)/shard_map/all_to_all | solution.py:196
  607.1 26.1 %all-to-all-start.1 = ((bf16[8,48,2048]{2,1,0:T(8,128)(2,1)}), bf16[8,48,2048]{2,1,0:T(8,128)(2,1)}, u32[]{:S(2)}, u32[]{:S(2)}) async-start(bf16[8,48,2048]{2,1,0:T(8,128)(2,1)} %bitcast.86), calls=%async_computation.1 | async-start | bytes 3145728 | tf_op jit(solution)/shard_map/all_to_all | solution.py:233
  611.5 33.8 %collective-permute-start.18 = (bf16[384,4096]{1,0:T(8,128)(2,1)}, bf16[384,4096]{1,0:T(8,128)(2,1)}, u32[]{:S(2)}, u32[]{:S(2)}) collective-permute-start(bf16[384,4096]{1,0:T(8,128)(2,1)} %get-tuple-element.8), channel_id=1, source_target_pairs={{0,16},{16,0},{1,17},{17,1},{2,18},{18,2},{3,19},{19,3},{4,20},{20... | collective-permute-start | bytes 9437192 | tf_op jit(solution)/shard_map/ppermute | solution.py:31
  654.3 16.1 %collective-permute-start.26 = (bf16[512,1024]{1,0:T(8,128)(2,1)S(1)}, bf16[512,1024]{1,0:T(8,128)(2,1)S(1)}, u32[]{:S(2)}, u32[]{:S(2)}) collective-permute-start(bf16[512,1024]{1,0:T(8,128)(2,1)S(1)} %head_partial.13), channel_id=1, source_target_pairs={{0,4},{1,5},{2,6},{3,7},{4,8},{5,9},{6,10},{7,11},{8,12},{9,13},{1... | collective-permute-start | bytes 3145736 | tf_op jit(solution)/shard_map/ppermute | solution.py:27
  656.3 18.5 %collective-permute-start.22 = (bf16[512,1024]{1,0:T(8,128)(2,1)S(1)}, bf16[512,1024]{1,0:T(8,128)(2,1)S(1)}, u32[]{:S(2)}, u32[]{:S(2)}) collective-permute-start(bf16[512,1024]{1,0:T(8,128)(2,1)S(1)} %head_partial.9), channel_id=1, source_target_pairs={{0,12},{1,13},{2,14},{3,15},{4,0},{5,1},{6,2},{7,3},{8,4},{9,5},{1... | collective-permute-start | bytes 3145736 | tf_op jit(solution)/shard_map/ppermute | solution.py:27
  661.6 21.6 %collective-permute-start.25 = (bf16[512,1024]{1,0:T(8,128)(2,1)S(1)}, bf16[512,1024]{1,0:T(8,128)(2,1)S(1)}, u32[]{:S(2)}, u32[]{:S(2)}) collective-permute-start(bf16[512,1024]{1,0:T(8,128)(2,1)S(1)} %head_partial.12), channel_id=1, source_target_pairs={{0,12},{1,13},{2,14},{3,15},{4,0},{5,1},{6,2},{7,3},{8,4},{9,5},{1... | collective-permute-start | bytes 3145736 | tf_op jit(solution)/shard_map/ppermute | solution.py:27
  672.3 16.5 %collective-permute-start.27 = (bf16[512,1024]{1,0:T(8,128)(2,1)S(1)}, bf16[512,1024]{1,0:T(8,128)(2,1)S(1)}, u32[]{:S(2)}, u32[]{:S(2)}) collective-permute-start(bf16[512,1024]{1,0:T(8,128)(2,1)S(1)} %head_partial.14), channel_id=1, source_target_pairs={{0,4},{1,5},{2,6},{3,7},{4,8},{5,9},{6,10},{7,11},{8,12},{9,13},{1... | collective-permute-start | bytes 3145736 | tf_op jit(solution)/shard_map/ppermute | solution.py:27
  674.7 28.0 %collective-permute-start.21 = (bf16[512,1024]{1,0:T(8,128)(2,1)S(1)}, bf16[512,1024]{1,0:T(8,128)(2,1)S(1)}, u32[]{:S(2)}, u32[]{:S(2)}) collective-permute-start(bf16[512,1024]{1,0:T(8,128)(2,1)S(1)} %head_partial.8), channel_id=1, source_target_pairs={{0,4},{1,5},{2,6},{3,7},{4,8},{5,9},{6,10},{7,11},{8,12},{9,13},{1... | collective-permute-start | bytes 3145736 | tf_op jit(solution)/shard_map/ppermute | solution.py:27
  676.8 26.0 %collective-permute-start.23 = (bf16[512,1024]{1,0:T(8,128)(2,1)S(1)}, bf16[512,1024]{1,0:T(8,128)(2,1)S(1)}, u32[]{:S(2)}, u32[]{:S(2)}) collective-permute-start(bf16[512,1024]{1,0:T(8,128)(2,1)S(1)} %head_partial.10), channel_id=1, source_target_pairs={{0,12},{1,13},{2,14},{3,15},{4,0},{5,1},{6,2},{7,3},{8,4},{9,5},{1... | collective-permute-start | bytes 3145736 | tf_op jit(solution)/shard_map/ppermute | solution.py:27
  690.9 17.9 %collective-permute-start.28 = (bf16[128,1024]{1,0:T(8,128)(2,1)S(1)}, bf16[128,1024]{1,0:T(8,128)(2,1)S(1)}, u32[]{:S(2)}, u32[]{:S(2)}) collective-permute-start(bf16[128,1024]{1,0:T(8,128)(2,1)S(1)} %get-tuple-element.13), channel_id=1, source_target_pairs={{0,1},{1,2},{2,3},{3,0},{4,5},{5,6},{6,7},{7,4},{8,9},{9,10},{10,1... | collective-permute-start | bytes 786440 | tf_op jit(solution)/shard_map/ppermute | solution.py:27
  710.8 21.1 %collective-permute-start.30 = (bf16[128,1024]{1,0:T(8,128)(2,1)S(1)}, bf16[128,1024]{1,0:T(8,128)(2,1)}, u32[]{:S(2)}, u32[]{:S(2)}) collective-permute-start(bf16[128,1024]{1,0:T(8,128)(2,1)S(1)} %get-tuple-element.15), channel_id=1, source_target_pairs={{0,1},{1,2},{2,3},{3,0},{4,5},{5,6},{6,7},{7,4},{8,9},{9,10},{10,1... | collective-permute-start | bytes 786440 | tf_op jit(solution)/shard_map/ppermute | solution.py:27
  716.7 15.2 %collective-permute-start.32 = (bf16[128,1024]{1,0:T(8,128)(2,1)S(1)}, bf16[128,1024]{1,0:T(8,128)(2,1)}, u32[]{:S(2)}, u32[]{:S(2)}) collective-permute-start(bf16[128,1024]{1,0:T(8,128)(2,1)S(1)} %get-tuple-element.12), channel_id=1, source_target_pairs={{0,3},{1,0},{2,1},{3,2},{4,7},{5,4},{6,5},{7,6},{8,11},{9,8},{10,9... | collective-permute-start | bytes 786440 | tf_op jit(solution)/shard_map/ppermute | solution.py:27
  733.1 16.2 %collective-permute-start.33 = (bf16[256,256]{1,0:T(8,128)(2,1)S(1)}, bf16[256,256]{1,0:T(8,128)(2,1)S(1)}, u32[]{:S(2)}, u32[]{:S(2)}) collective-permute-start(bf16[256,256]{1,0:T(8,128)(2,1)S(1)} %get-tuple-element.20), channel_id=1, source_target_pairs={{0,32},{32,64},{64,96},{96,0},{1,33},{33,65},{65,97},{97,1},{2,34}... | collective-permute-start | bytes 393224 | tf_op jit(solution)/shard_map/ppermute | solution.py:163
  733.7 15.6 %collective-permute-start.34 = (bf16[256,256]{1,0:T(8,128)(2,1)S(1)}, bf16[256,256]{1,0:T(8,128)(2,1)S(1)}, u32[]{:S(2)}, u32[]{:S(2)}) collective-permute-start(bf16[256,256]{1,0:T(8,128)(2,1)S(1)} %get-tuple-element.22), channel_id=1, source_target_pairs={{0,64},{32,96},{64,0},{96,32},{1,65},{33,97},{65,1},{97,33},{2,66}... | collective-permute-start | bytes 393224 | tf_op jit(solution)/shard_map/ppermute | solution.py:163
  735.8 13.5 %collective-permute-start.35 = (bf16[256,256]{1,0:T(8,128)(2,1)S(1)}, bf16[256,256]{1,0:T(8,128)(2,1)S(1)}, u32[]{:S(2)}, u32[]{:S(2)}) collective-permute-start(bf16[256,256]{1,0:T(8,128)(2,1)S(1)} %get-tuple-element.21), channel_id=1, source_target_pairs={{0,96},{32,0},{64,32},{96,64},{1,97},{33,1},{65,33},{97,65},{2,98}... | collective-permute-start | bytes 393224 | tf_op jit(solution)/shard_map/ppermute | solution.py:163
  (28 other events, 265.2 us)

commit v2 on v1

--- a/solution.py
+++ b/solution.py
@@ -58,40 +58,270 @@
     return pieces, [(d1, d2) for d1s, d2 in places for d1 in d1s]
 
 
-def place_kernel(at_ref, *refs):
-    pieces, out_ref, sems = refs[:16], refs[16], refs[17]
-    copies = []
-    for i, piece in enumerate(pieces):
-        for j in range(2):
-            k = 2 * i + j
-            row = pl.multiple_of(at_ref[0, k] * BLOCK, BLOCK)
-            col = pl.multiple_of(at_ref[1, k] * 1024, 1024)
-            copies.append(
-                pltpu.make_async_copy(
-                    piece.at[pl.ds(j * BLOCK, BLOCK), :],
-                    out_ref.at[pl.ds(row, BLOCK), pl.ds(col, 1024)],
-                    sems.at[k],
-                )
-            )
-    for copy in copies:
-        copy.start()
-    for copy in copies:
-        copy.wait()
-
-
-def place_head(pieces, at):
+def project_kernel(count, last, at_ref, *refs):
+    own_ref, arrived_ref = refs[:2]
+    pieces = refs[2 : 2 + count]
+    rest = refs[2 + count :]
+    if last:
+        base_ref, counts_ref, _, head_ref, pre_out, inverse_ref, emb_ref, mixing_ref, first_ref, grad_ref = rest[:10]
+        held, states, loaded, stored, pre_ref = rest[10:]
+    else:
+        head_ref, pre_ref, held, states, loaded, stored = rest
+    step = pl.program_id(0)
+    half = count // 2
+    blocks = 2 * half
+    rows = own_ref.shape[0]
+    width = 1024
+
+    def load(i):
+        return pltpu.make_async_copy(
+            pieces[i], held.at[i // half, pl.ds((i % half) * 512, 512), :], loaded.at[i]
+        )
+
+    def store(k):
+        row = pl.multiple_of(at_ref[0, k] * BLOCK, BLOCK)
+        col = pl.multiple_of(at_ref[1, k] * width, width)
+        return pltpu.make_async_copy(
+            held.at[k // blocks, pl.ds((k % blocks) * BLOCK, BLOCK), :],
+            head_ref.at[pl.ds(row, BLOCK), pl.ds(col, width)],
+            stored.at[k],
+        )
+
+    @pl.when(step == 0)
+    def _():
+        for i in range(count):
+            load(i).start()
+
+    for side in range(2):
+
+        @pl.when(step == 4 * side)
+        def _(side=side):
+            for k in range(blocks):
+                col = pl.multiple_of(at_ref[0, side * blocks + k] * BLOCK, BLOCK)
+                states[pl.ds(0, rows), pl.ds(k * BLOCK, BLOCK)] = own_ref[:, pl.ds(col, BLOCK)]
+                states[pl.ds(rows, rows), pl.ds(k * BLOCK, BLOCK)] = arrived_ref[:, pl.ds(col, BLOCK)]
+            for i in range(side * half, (side + 1) * half):
+                load(i).wait()
+            for k in range(side * blocks, (side + 1) * blocks):
+                store(k).start()
+
+    at_col = pl.multiple_of((step % 4) * BLOCK, BLOCK)
+    product = jnp.dot(
+        states[...], held[step // 4, :, pl.ds(at_col, BLOCK)], preferred_element_type=F32
+    )
+    if not last:
+        pre_ref[...] = product
+    else:
+        out_col = pl.multiple_of(at_ref[1, (step // 4) * blocks] * width + at_col, BLOCK)
+        pre_ref[:, pl.ds(out_col, BLOCK)] = base_ref[...] + product
+
+    @pl.when(step == 7)
+    def _():
+        if last:
+            contrast(counts_ref, pre_ref, pre_out, inverse_ref, emb_ref, mixing_ref, first_ref, grad_ref)
+        for k in range(2 * blocks):
+            store(k).wait()
+
+
+def contrast(counts_ref, pre_ref, pre_out, inverse_ref, emb_ref, mixing_ref, first_ref, grad_ref):
+    rows = counts_ref.shape[0]
+    width = pre_ref.shape[1]
+    scale = 16.0 / width
+    chunk = 32
+
+    def normalize(i, _):
+        at = pl.ds(pl.multiple_of(i * chunk, chunk), chunk)
+        values = pre_ref[at, :]
+        inverse = lax.rsqrt(jnp.mean(values * values, axis=-1, keepdims=True) + EPSILON)
+        emb_ref[at, :] = (values * inverse).astype(BF16)
+
+        @pl.when(i < 2 * rows // chunk)
+        def _():
+            pre_out[at, :] = values
+            inverse_ref[at, :] = jnp.broadcast_to(inverse, (chunk, 128))
+
+        return 0
+
+    lax.fori_loop(0, pre_ref.shape[0] // chunk, normalize, 0)
+    query = emb_ref[pl.ds(0, rows), :]
+    passage = emb_ref[pl.ds(rows, rows), :]
+    fetched = emb_ref[pl.ds(2 * rows, 2 * rows), :]
+    positive = (
+        jnp.sum(query.astype(F32) * passage.astype(F32), axis=1, keepdims=True) * scale
+    )
+    table = dot(query, fetched, ((1,), (1,))) * scale
+    counts = counts_ref[...]
+    top = jnp.maximum(
+        positive, jnp.max(jnp.where(counts > 0, table, -1e30), axis=1, keepdims=True)
+    )
+    raised = jnp.where(counts > 0, jnp.exp(jnp.where(counts > 0, table - top, 0.0)), 0.0)
+    raised_positive = jnp.exp(positive - top)
+    whole = raised_positive + jnp.sum(raised * counts, axis=1, keepdims=True)
+    first = (raised_positive / whole - 1.0).astype(BF16).astype(F32)
+    mixing = ((raised / whole).astype(BF16).astype(F32) * counts).astype(BF16)
+    first_ref[...] = jnp.broadcast_to(first, (rows, 128))
+    mixing_ref[...] = mixing
+    grad_ref[...] = dot(mixing, query, ((0,), (0,))).astype(BF16)
+
+
+def project_first(at, both_states, arrived, pieces):
+    count = len(pieces)
+    rows = arrived.shape[0]
     return pl.pallas_call(
-        place_kernel,
+        lambda *refs: project_kernel(count, False, *refs),
+        grid_spec=pltpu.PrefetchScalarGridSpec(
+            num_scalar_prefetch=1,
+            grid=(8,),
+            in_specs=[
+                pl.BlockSpec((rows, 4096), lambda g, at: (0, 0)),
+                pl.BlockSpec((rows, 4096), lambda g, at: (0, 0)),
+            ]
+            + [pl.BlockSpec(memory_space=pl.ANY)] * count,
+            out_specs=[
+                pl.BlockSpec(memory_space=pl.ANY),
+                pl.BlockSpec((2 * rows, BLOCK), lambda g, at: (0, at[1, (g // 4) * count] * 4 + g % 4)),
+            ],
+            scratch_shapes=[
+                pltpu.VMEM((2, count // 2 * 512, 1024), BF16),
+                pltpu.VMEM((2 * rows, count // 2 * 512), BF16),
+                pltpu.SemaphoreType.DMA((count,)),
+                pltpu.SemaphoreType.DMA((2 * count,)),
+            ],
+        ),
+        out_shape=[
+            jax.ShapeDtypeStruct((4096, 2048), BF16),
+            jax.ShapeDtypeStruct((2 * rows, 2048), F32),
+        ],
+        compiler_params=pltpu.CompilerParams(vmem_limit_bytes=48 * 1024 * 1024),
+        name="project_first",
+    )(at, both_states, arrived, *pieces)
+
+
+def project_last(at, both_states, arrived, pieces, base, counts, head):
+    count = len(pieces)
+    rows = arrived.shape[0]
+    half = rows // 2
+
+    def whole(shape):
+        return pl.BlockSpec(shape, lambda g, at: (0,) * len(shape))
+
+    return pl.pallas_call(
+        lambda *refs: project_kernel(count, True, *refs),
+        grid_spec=pltpu.PrefetchScalarGridSpec(
+            num_scalar_prefetch=1,
+            grid=(8,),
+            in_specs=[whole((rows, 4096)), whole((rows, 4096))]
+            + [pl.BlockSpec(memory_space=pl.ANY)] * count
+            + [
+                pl.BlockSpec((2 * rows, BLOCK), lambda g, at: (0, at[1, (g // 4) * count] * 4 + g % 4)),
+                whole((half, rows)),
+                pl.BlockSpec(memory_space=pl.ANY),
+            ],
+            out_specs=[
+                pl.BlockSpec(memory_space=pl.ANY),
+                whole((rows, 2048)),
+                whole((rows, 128)),
+                whole((2 * rows, 2048)),
+                whole((half, rows)),
+                whole((half, 128)),
+                whole((rows, 2048)),
+            ],
+            scratch_shapes=[
+                pltpu.VMEM((2, count // 2 * 512, 1024), BF16),
+                pltpu.VMEM((2 * rows, count // 2 * 512), BF16),
+                pltpu.SemaphoreType.DMA((count,)),
+                pltpu.SemaphoreType.DMA((2 * count,)),
+                pltpu.VMEM((2 * rows, 2048), F32),
+            ],
+        ),
+        out_shape=[
+            jax.ShapeDtypeStruct((4096, 2048), BF16),
+            jax.ShapeDtypeStruct((rows, 2048), F32),
+            jax.ShapeDtypeStruct((rows, 128), F32),
+            jax.ShapeDtypeStruct((2 * rows, 2048), BF16),
+            jax.ShapeDtypeStruct((half, rows), BF16),
+            jax.ShapeDtypeStruct((half, 128), F32),
+            jax.ShapeDtypeStruct((rows, 2048), BF16),
+        ],
+        input_output_aliases={5 + count: 0},
+        compiler_params=pltpu.CompilerParams(vmem_limit_bytes=56 * 1024 * 1024),
+        name="project_last",
+    )(at, both_states, arrived, *pieces, base, counts, head)
+
+
+def slopes_kernel(cols_ref, pre_ref, inverse_ref, first_ref, other_ref, left_ref, right_ref, out_ref, keep_ref, send_ref, grad_ref):
+    chunk = 32
+    width = pre_ref.shape[1]
+    grad_ref[...] = jnp.dot(left_ref[...], right_ref[...], preferred_element_type=F32)
+
+    def some(i, _):
+        at = pl.ds(pl.multiple_of(i * chunk, chunk), chunk)
+        grad = first_ref[at, :1] * other_ref[at, :].astype(F32) + grad_ref[at, :]
+        values = pre_ref[at, :]
+        inverse = inverse_ref[at, :1]
+        along = jnp.mean(grad * values, axis=-1, keepdims=True)
+        out_ref[at, :] = (inverse * grad - values * (inverse * inverse * inverse * along)).astype(BF16)
+        return 0
+
+    lax.fori_loop(0, pre_ref.shape[0] // chunk, some, 0)
+    for k in range(width // BLOCK // 2):
+        for row, ref in ((0, keep_ref), (1, send_ref)):
+            col = pl.multiple_of(cols_ref[row, k] * BLOCK, BLOCK)
+            ref[:, pl.ds(k * BLOCK, BLOCK)] = out_ref[:, pl.ds(col, BLOCK)]
+
+
+def slopes_of(cols, pre, part, inverse, first, emb, other, left, right):
+    rows = first.shape[0]
+    width = pre.shape[1]
+
+    def whole(shape, at=0):
+        return pl.BlockSpec(shape, lambda g, cols: (at, 0))
+
+    return pl.pallas_call(
+        slopes_kernel,
         grid_spec=pltpu.PrefetchScalarGridSpec(
             num_scalar_prefetch=1,
             grid=(1,),
-            in_specs=[pl.BlockSpec(memory_space=pl.ANY)] * 16,
-            out_specs=pl.BlockSpec(memory_space=pl.ANY),
-            scratch_shapes=[pltpu.SemaphoreType.DMA((32,))],
+            in_specs=[
+                whole((rows, width), part),
+                whole((rows, 128), part),
+                whole((rows, 128)),
+                whole((rows, width), other),
+                whole(left.shape),
+                whole((left.shape[1], width), right[1]),
+            ],
+            out_specs=[whole((rows, width)), whole((rows, width // 2)), whole((rows, width // 2))],
+            scratch_shapes=[pltpu.VMEM((rows, width), F32)],
         ),
-        out_shape=jax.ShapeDtypeStruct((4096, 2048), BF16),
-        name="place_head",
-    )(at, *pieces)
+        out_shape=[
+            jax.ShapeDtypeStruct((rows, width), BF16),
+            jax.ShapeDtypeStruct((rows, width // 2), BF16),
+            jax.ShapeDtypeStruct((rows, width // 2), BF16),
+        ],
+        compiler_params=pltpu.CompilerParams(vmem_limit_bytes=32 * 1024 * 1024),
+        name="slopes_of",
+    )(cols, pre, inverse, first, emb, left, right[0])
+
+
+def input_grad_kernel(slopes_ref, head_ref, out_ref):
+    out_ref[...] = dot(slopes_ref[...], head_ref[...], ((1,), (1,))).astype(BF16)
+
+
+def input_grad(slopes, head):
+    rows, width = slopes.shape
+    depth = head.shape[0]
+    return pl.pallas_call(
+        input_grad_kernel,
+        grid=(depth // 512,),
+        in_specs=[
+            pl.BlockSpec((rows, width), lambda k: (0, 0)),
+            pl.BlockSpec((512, width), lambda k: (k, 0)),
+        ],
+        out_specs=pl.BlockSpec((rows, 512), lambda k: (0, k)),
+        out_shape=jax.ShapeDtypeStruct((rows, depth), BF16),
+        compiler_params=pltpu.CompilerParams(vmem_limit_bytes=32 * 1024 * 1024),
+        name="input_grad",
+    )(slopes, head)
 
 
 def partial_kernel(at_ref, states_ref, slopes_ref, *refs):
@@ -132,7 +362,7 @@
     return total.astype(BF16)
 
 
-def scatter_head(states, slopes, core):
+def scatter_head(states, slopes, core, beside):
     def part(d1, d2s, *adds):
         at = jnp.stack([block_at(core, d1, d2) for d2 in d2s]).astype(jnp.int32)
         return head_partial(states, slopes, at, adds)
@@ -142,6 +372,7 @@
     far_b = shift(part(2, b), 1, -1)
     up_b = shift(part(1, b), 1, 1)
     down_a = shift(part(-1, a), 1, -1)
+    extra, far_a, far_b = lax.optimization_barrier((beside(), far_a, far_b))
     up_a = shift(part(1, a, far_a), 1, 1)
     down_b = shift(part(-1, b, far_b), 1, -1)
     mine_a = part(0, a, down_a, up_a)
@@ -163,16 +394,7 @@
         out = out + lax.ppermute(
             sent, "x", [(i, (i + step) % RING) for i in range(RING)]
         ).astype(F32)
-    return out
-
-
-def inverse_rms(values):
-    return lax.rsqrt(jnp.mean(values * values, axis=-1, keepdims=True) + EPSILON)
-
-
-def rms_back(values, inverse, grad):
-    along = jnp.mean(grad * values, axis=-1, keepdims=True)
-    return (inverse * grad - values * (inverse * inverse * inverse * along)).astype(BF16)
+    return out, extra
 
 
 def dot(a, b, contract=((1,), (0,))):
@@ -183,7 +405,6 @@
     core, x = lax.axis_index("c"), lax.axis_index("x")
     rows_dev, depth = queries.shape
     width = head_weight.shape[1]
-    scale = 16.0 / width
     groups, capacity = send_lists.shape[2], send_lists.shape[3]
     slot_count = groups * capacity
     flat_lists = send_lists.reshape(slot_count)
@@ -202,34 +423,18 @@
     for j in range(neg_slots.shape[1]):
         counts = counts + (neg_slots[:, j : j + 1] == slot_ids).astype(F32)
 
-    at = jnp.stack(
-        [block_at(core, d1, d2) for d1, d2 in places]
-        + [block_at(1 - core, d1, d2) for d1, d2 in places]
-    )
-    side = jnp.concatenate([jnp.full((16,), core), jnp.full((16,), 1 - core)])
-    head = place_head(pieces + [swap(piece) for piece in pieces], jnp.stack([at, side]).astype(jnp.int32))
-
-    pre = dot(states, head)
-    arrived_pre = dot(arrived, head)
-    inverse = inverse_rms(pre)
-    emb = (pre * inverse).astype(BF16)
-    query_emb, passage_emb = emb[:rows_dev], emb[rows_dev:]
-    fetched = (arrived_pre * inverse_rms(arrived_pre)).astype(BF16)
-
-    positive = (
-        jnp.sum(query_emb.astype(F32) * passage_emb.astype(F32), axis=1, keepdims=True) * scale
-    )
-    table = dot(query_emb, fetched, ((1,), (1,))) * scale
-    top = jnp.maximum(
-        positive, jnp.max(jnp.where(counts > 0, table, -jnp.inf), axis=1, keepdims=True)
-    )
-    raised = jnp.where(counts > 0, jnp.exp(table - top), 0.0)
-    raised_positive = jnp.exp(positive - top)
-    whole = raised_positive + jnp.sum(raised * counts, axis=1, keepdims=True)
-    first = (raised_positive / whole - 1.0).astype(BF16).astype(F32)
-    mixing = ((raised / whole).astype(BF16).astype(F32) * counts).astype(BF16)
-
-    fetched_grad = dot(mixing, query_emb, ((0,), (0,))).astype(BF16)
+    def places_of(some):
+        at = [block_at(core, d1, d2) for d1, d2 in some] + [block_at(1 - core, d1, d2) for d1, d2 in some]
+        side = [core] * len(some) + [1 - core] * len(some)
+        return jnp.stack([jnp.stack(at), jnp.stack(side)]).astype(jnp.int32)
+
+    early, late = pieces[:6], pieces[6:]
+    early = early + [swap(piece) for piece in early]
+    head, base = project_first(places_of(places[:12]), both_states, arrived, early)
+    late = late + [swap(piece) for piece in late]
+    head, pre, inverse, emb, mixing, first, fetched_grad = project_last(
+        places_of(places[12:]), both_states, arrived, late, base, counts, head
+    )
     returned = lax.all_to_all(
         fetched_grad.reshape(groups, capacity, width),
         ("x", "c"),
@@ -238,26 +443,23 @@
         tiled=True,
     ).reshape(slot_count, width)
 
-    def split(slopes):
-        cut = slopes.reshape(slopes.shape[0], RING, 2, BLOCK)
-        cut = jnp.concatenate([cut, cut], axis=1)
-        cut = lax.dynamic_slice_in_dim(cut, x, RING, axis=1)
-        keep = lax.dynamic_index_in_dim(cut, core, 2, keepdims=False)
-        send = lax.dynamic_index_in_dim(cut, 1 - core, 2, keepdims=False)
-        shape = (slopes.shape[0], RING * BLOCK)
-        return keep.reshape(shape), swap(send.reshape(shape))
-
-    query_emb_grad = first * passage_emb.astype(F32) + dot(mixing, fetched)
-    query_dy = rms_back(pre[:rows_dev], inverse[:rows_dev], query_emb_grad)
-    query_keep, query_other = split(query_dy)
-    query_grads = dot(query_dy, head, ((1,), (1,))).astype(BF16)
-
-    passage_emb_grad = first * query_emb.astype(F32) + dot(owner, returned)
-    passage_dy = rms_back(pre[rows_dev:], inverse[rows_dev:], passage_emb_grad)
-    passage_keep, passage_other = split(passage_dy)
+    to_x = [(x + step) % RING for step in range(RING)]
+    cols = jnp.stack(
+        [jnp.stack([2 * to + core for to in to_x]), jnp.stack([2 * to + 1 - core for to in to_x])]
+    ).astype(jnp.int32)
+    query_dy, query_keep, query_send = slopes_of(cols, pre, 0, inverse, first, emb, 1, mixing, (emb, 1))
+    query_other = swap(query_send)
+    query_grads = input_grad(query_dy, head)
+    returned, query_grads, query_other = lax.optimization_barrier((returned, query_grads, query_other))
+
+    passage_dy, passage_keep, passage_send = slopes_of(
+        cols, pre, 1, inverse, first, emb, 0, owner, (returned, 0)
+    )
+    passage_other = swap(passage_send)
     slopes = jnp.concatenate([query_keep, passage_keep, query_other, passage_other], axis=0)
-    head_grads = scatter_head(both_states, slopes, core)
-    passage_grads = dot(passage_dy, head, ((1,), (1,))).astype(BF16)
+    head_grads, passage_grads = scatter_head(
+        both_states, slopes, core, lambda: input_grad(passage_dy, head)
+    )
     return (query_grads, passage_grads, head_grads)
 
 

time: 757 us -> 255 us (0.34)
  Pallas kernels: 526 us -> 85.2 us
  matrix products: 63.5 us -> 4.13 us
    pallas_call x1 -> x6, Pallas kernels: 510 us -> 62.6 us  [the longest x1 20.6 us: project_last(): pl.pallas_call(lambda *refs: project_kernel(count, True, *refs), grid_spe...]
    dot_general x9 -> x1, matrix products: 63.5 us -> 4.13 us  [dot(): lax.dot_general(a, b, (contract, ((), ())), preferred_element_type=F32)]
    all_to_all x1, waiting for transfers between devices: 16.6 us -> 0.31 us  [per_device(): lax.all_to_all(fetched_grad.reshape(groups, capacity, width), ('x', 'c'),...]
    unnamed x39 -> x49, local copies, waits for them, and re-layouts: 13.9 us -> 25.3 us
  transfers between devices with their start and end apart: 38 -> 38, of which waited for: 13 -> 19; matrix products, arithmetic and copies ran while one was open for 9% -> 7% of each run, Pallas kernels for 70% -> 23%
where the time goes in v2:
time: 255 us; the launch traced here: 254 us
  Pallas kernels  85.2 us (33%)
  waiting for transfers between devices  72.5 us (28%)
  starting transfers between devices  54.3 us (21%)
  local copies, waits for them, and re-layouts  29.9 us (12%)
  other arithmetic  5.98 us (2%)
  matrix products  4.13 us (2%)
    ppermute x22, waiting for transfers between devices, shift(): return lax.ppermute(value, ('c', 'y', 'z'), pairs)  61.5 us
    ppermute x22, starting transfers between devices, shift(): return lax.ppermute(value, ('c', 'y', 'z'), pairs)  37.2 us
    unnamed x49, local copies, waits for them, and re-layouts  25.3 us
    pallas_call x8, Pallas kernels, head_partial(): pl.pallas_call(partial_kernel, grid_spec=pltpu.PrefetchScalarGridSpec(num...  22.5 us
    pallas_call x1, Pallas kernels, project_last(): pl.pallas_call(lambda *refs: project_kernel(count, True, *refs), grid_spe...  20.6 us
    pallas_call x1, Pallas kernels, project_first(): pl.pallas_call(lambda *refs: project_kernel(count, False, *refs), grid_sp...  19.9 us
    pallas_call x2, Pallas kernels, input_grad(): pl.pallas_call(input_grad_kernel, grid=(depth // 512,), in_specs=[pl.Bloc...  15.1 us
    pallas_call x2, Pallas kernels, slopes_of(): pl.pallas_call(slopes_kernel, grid_spec=pltpu.PrefetchScalarGridSpec(num_...  7.08 us
  transfers between devices with their start and end apart: 38, of which 19 were waited for; matrix products, arithmetic and copies ran while one was open for 7% of the time, Pallas kernels for 23%

profile of v2, /device:TPU:0, one launch (start us, length us, event | category | flops | bytes accessed | tf_op | source)
XLA Modules:
  0.0 254.3 jit_solution(16518610601562194935)
XLA Ops:
  3.6 8.7 %collective-permute-done.1 = bf16[256,1024]{1,0:T(8,128)(2,1)S(1)} collective-permute-done((bf16[256,1024]{1,0:T(8,128)(2,1)S(1)}, bf16[256,1024]{1,0:T(8,128)(2,1)S(1)}, u32[]{:S(2)}, u32[]{:S(2)}) %collective-permute-start.1) | collective-permute-done | bytes 524320 | tf_op jit(solution)/shard_map/ppermute | solution.py:27
  18.7 7.1 %collective-permute-done.4 = bf16[256,1024]{1,0:T(8,128)(2,1)S(1)} collective-permute-done((bf16[256,1024]{1,0:T(8,128)(2,1)S(1)}, bf16[256,1024]{1,0:T(8,128)(2,1)S(1)}, u32[]{:S(2)}, u32[]{:S(2)}) %collective-permute-start.4) | collective-permute-done | bytes 524320 | tf_op jit(solution)/shard_map/ppermute | solution.py:27
  31.2 3.9 %collective-permute-done.6 = bf16[128,1024]{1,0:T(8,128)(2,1)S(1)} collective-permute-done((bf16[128,1024]{1,0:T(8,128)(2,1)S(1)}, bf16[128,1024]{1,0:T(8,128)(2,1)S(1)}, u32[]{:S(2)}, u32[]{:S(2)}) %collective-permute-start.6) | collective-permute-done | bytes 262176 | tf_op jit(solution)/shard_map/ppermute | solution.py:27
  37.9 4.1 %convolution_convert_fusion = bf16[384,4096]{1,0:T(8,128)(2,1)} fusion(bf16[192,4096]{1,0:T(8,128)(2,1)} %param.6, s32[384]{0:T(512)S(1)} %eq.458), kind=kOutput, calls=%fused_computation | convolution fusion | flops 605626368 | bytes 4720128 | tf_op jit(solution)/shard_map/dot_general | solution.py:401
  42.0 4.6 %all-to-all-start = ((bf16[8,48,4096]{2,1,0:T(8,128)(2,1)}), bf16[8,48,4096]{2,1,0:T(8,128)(2,1)}, u32[]{:S(2)}, u32[]{:S(2)}) async-start(bf16[8,48,4096]{2,1,0:T(8,128)(2,1)} %bitcast.69), calls=%async_computation | async-start | bytes 6291456 | tf_op jit(solution)/shard_map/all_to_all | solution.py:417
  48.8 6.2 %collective-permute-done.7.refs_8_ = bf16[512,1024]{1,0:T(8,128)(2,1)} collective-permute-done((bf16[512,1024]{1,0:T(8,128)(2,1)S(1)}, bf16[512,1024]{1,0:T(8,128)(2,1)}, u32[]{:S(2)}, u32[]{:S(2)}) %collective-permute-start.7) | collective-permute-done | bytes 1048608 | tf_op jit(solution)/shard_map/ppermute | solution.py:27
  63.1 8.1 %collective-permute-done.3.refs_3_ = bf16[512,1024]{1,0:T(8,128)(2,1)} collective-permute-done((bf16[512,1024]{1,0:T(8,128)(2,1)S(1)}, bf16[512,1024]{1,0:T(8,128)(2,1)}, u32[]{:S(2)}, u32[]{:S(2)}) %collective-permute-start.3) | collective-permute-done | bytes 1048608 | tf_op jit(solution)/shard_map/ppermute | solution.py:27
  74.4 4.0 %constant_dynamic-update-slice_fusion.refs_1_.states_ref = bf16[768,4096]{1,0:T(8,128)(2,1)} fusion(bf16[768,4096]{1,0:T(8,128)(2,1)} %constant_dynamic-update-slice_fusion.1, bf16[384,4096]{1,0:T(8,128)(2,1)} %collective-permute-done), kind=kLoop, calls=%fused_computation.38 | loop fusion | bytes 6291456 | tf_op jit(solution)/shard_map/concatenate | solution.py:420
  78.4 6.6 %all-to-all-done = bf16[8,48,4096]{2,1,0:T(8,128)(2,1)} async-done(((bf16[8,48,4096]{2,1,0:T(8,128)(2,1)}), bf16[8,48,4096]{2,1,0:T(8,128)(2,1)}, u32[]{:S(2)}, u32[]{:S(2)}) %all-to-all-start) | async-done | bytes 3145760 | tf_op jit(solution)/shard_map/all_to_all | solution.py:417
  85.0 19.9 %project_first.1 = (bf16[4096,2048]{1,0:T(8,128)(2,1)}, f32[768,2048]{1,0:T(8,128)}) custom-call(s32[2,24]{1,0:T(2,128)S(1)} %pad_add_fusion.1.refs_0_, bf16[768,4096]{1,0:T(8,128)(2,1)} %constant_dynamic-update-slice_fusion.refs_1_.states_ref, bf16[384,4096]{1,0:T(8,128)(2,1)} %bitcast.12.refs_2_, bf16[512,1024]{1,0:T(8,128)(2,1)S(1)} %pad_maximum_fusion.1.refs_3_, ...), custom_call_target="tpu_custom_call" | custom-call | tf_op jit(solution)/shard_map/project_first/pallas_call | solution.py:170
  104.9 20.6 %project_last.1 = (bf16[4096,2048]{1,0:T(8,128)(2,1)}, f32[384,2048]{1,0:T(8,128)}, f32[384,128]{1,0:T(8,128)}, bf16[768,2048]{1,0:T(8,128)(2,1)}, bf16[192,384]...) custom-call(s32[2,8]{1,0:T(2,128)} %pad_add_fusion.refs_0_, ...), custom_call_target="tpu_custom_call", output_to_operand_aliasing={{0}: (9, {})} | custom-call | tf_op jit(solution)/shard_map/project_last/pallas_call | solution.py:208
  125.5 4.6 %all-to-all-start.1 = ((bf16[8,48,2048]{2,1,0:T(8,128)(2,1)}), bf16[8,48,2048]{2,1,0:T(8,128)(2,1)}, u32[]{:S(2)}, u32[]{:S(2)}) async-start(bf16[8,48,2048]{2,1,0:T(8,128)(2,1)} %bitcast.70), calls=%async_computation.1 | async-start | bytes 3145728 | tf_op jit(solution)/shard_map/all_to_all | solution.py:438
  138.1 5.8 %copy-done.2 = bf16[4096,2048]{1,0:T(8,128)(2,1)S(1)} copy-done((bf16[4096,2048]{1,0:T(8,128)(2,1)S(1)}, bf16[4096,2048]{1,0:T(8,128)(2,1)}, u32[]{:S(2)}) %copy-start.2) | copy-done | bytes 16777240
  143.9 7.5 %input_grad.2 = bf16[192,4096]{1,0:T(8,128)(2,1)} custom-call(bf16[192,2048]{1,0:T(8,128)(2,1)S(1)} %get-tuple-element.32.slopes_ref, bf16[4096,2048]{1,0:T(8,128)(2,1)S(1)} %copy-done.2), custom_call_target="tpu_custom_call" | custom-call | tf_op jit(solution)/shard_map/input_grad/pallas_call | solution.py:313
  154.5 4.2 %slopes_of.3 = (bf16[192,2048]{1,0:T(8,128)(2,1)S(1)}, bf16[192,1024]{1,0:T(8,128)(2,1)S(1)}, bf16[192,1024]{1,0:T(8,128)(2,1)S(1)}) custom-call(s32[2,4]{1,0:T(2,128)S(1)} %pad_add_fusion.2.cols_ref, f32[384,2048]{1,0:T(8,128)S(1)} %copy-done.6, f32[384,128]{1,0:T(8,128)S(1)} %copy-done.8, f32[192,128]{1,0:T(8,128)S(1)} %copy-done.10, ...), custom_call_target="tpu_custom_call" | custom-call | tf_op jit(solution)/shard_map/slopes_of/pallas_call | solution.py:280
  163.4 3.8 %collective-permute-start.22 = (bf16[512,1024]{1,0:T(8,128)(2,1)S(1)}, bf16[512,1024]{1,0:T(8,128)(2,1)S(1)}, u32[]{:S(2)}, u32[]{:S(2)}) collective-permute-start(bf16[512,1024]{1,0:T(8,128)(2,1)S(1)} %head_partial.9), channel_id=1, source_target_pairs={{0,12},{1,13},{2,14},{3,15},{4,0},{5,1},{6,2},{7,3},{8,4},{9,5},{1... | collective-permute-start | bytes 3145736 | tf_op jit(solution)/shard_map/ppermute | solution.py:27
  170.2 5.8 %copy-done.3 = bf16[4096,2048]{1,0:T(8,128)(2,1)S(1)} copy-done((bf16[4096,2048]{1,0:T(8,128)(2,1)S(1)}, bf16[4096,2048]{1,0:T(8,128)(2,1)}, u32[]{:S(2)}) %copy-start.3) | copy-done | bytes 16777240
  175.9 7.5 %input_grad.3 = bf16[192,4096]{1,0:T(8,128)(2,1)} custom-call(bf16[192,2048]{1,0:T(8,128)(2,1)S(1)} %get-tuple-element.37.slopes_ref, bf16[4096,2048]{1,0:T(8,128)(2,1)S(1)} %copy-done.3), custom_call_target="tpu_custom_call" | custom-call | tf_op jit(solution)/shard_map/input_grad/pallas_call | solution.py:313
  186.3 3.3 %collective-permute-start.26 = (bf16[512,1024]{1,0:T(8,128)(2,1)S(1)}, bf16[512,1024]{1,0:T(8,128)(2,1)S(1)}, u32[]{:S(2)}, u32[]{:S(2)}) collective-permute-start(bf16[512,1024]{1,0:T(8,128)(2,1)S(1)} %head_partial.13), channel_id=1, source_target_pairs={{0,12},{1,13},{2,14},{3,15},{4,0},{5,1},{6,2},{7,3},{8,4},{9,5},{1... | collective-permute-start | bytes 3145736 | tf_op jit(solution)/shard_map/ppermute | solution.py:27
  198.5 3.3 %collective-permute-start.24 = (bf16[512,1024]{1,0:T(8,128)(2,1)S(1)}, bf16[512,1024]{1,0:T(8,128)(2,1)S(1)}, u32[]{:S(2)}, u32[]{:S(2)}) collective-permute-start(bf16[512,1024]{1,0:T(8,128)(2,1)S(1)} %head_partial.11), channel_id=1, source_target_pairs={{0,12},{1,13},{2,14},{3,15},{4,0},{5,1},{6,2},{7,3},{8,4},{9,5},{1... | collective-permute-start | bytes 3145736 | tf_op jit(solution)/shard_map/ppermute | solution.py:27
  201.9 6.8 %collective-permute-done.27.refs_1_ = bf16[512,1024]{1,0:T(8,128)(2,1)S(1)} collective-permute-done((bf16[512,1024]{1,0:T(8,128)(2,1)S(1)}, bf16[512,1024]{1,0:T(8,128)(2,1)S(1)}, u32[]{:S(2)}, u32[]{:S(2)}) %collective-permute-start.27) | collective-permute-done | bytes 1048608 | tf_op jit(solution)/shard_map/ppermute | solution.py:27
  213.7 9.0 %collective-permute-done.23.refs_0_ = bf16[512,1024]{1,0:T(8,128)(2,1)S(1)} collective-permute-done((bf16[512,1024]{1,0:T(8,128)(2,1)S(1)}, bf16[512,1024]{1,0:T(8,128)(2,1)S(1)}, u32[]{:S(2)}, u32[]{:S(2)}) %collective-permute-start.23) | collective-permute-done | bytes 1048608 | tf_op jit(solution)/shard_map/ppermute | solution.py:27
  225.7 3.2 %collective-permute-start.25 = (bf16[128,1024]{1,0:T(8,128)(2,1)S(1)}, bf16[128,1024]{1,0:T(8,128)(2,1)S(1)}, u32[]{:S(2)}, u32[]{:S(2)}) collective-permute-start(bf16[128,1024]{1,0:T(8,128)(2,1)S(1)} %slice.135), channel_id=1, source_target_pairs={{0,3},{1,0},{2,1},{3,2},{4,7},{5,4},{6,5},{7,6},{8,11},{9,8},{10,9... | collective-permute-start | bytes 786440 | tf_op jit(solution)/shard_map/ppermute | solution.py:27
  240.4 3.9 %collective-permute-done.32 = bf16[128,1024]{1,0:T(8,128)(2,1)S(1)} collective-permute-done((bf16[128,1024]{1,0:T(8,128)(2,1)S(1)}, bf16[128,1024]{1,0:T(8,128)(2,1)S(1)}, u32[]{:S(2)}, u32[]{:S(2)}) %collective-permute-start.32) | collective-permute-done | bytes 262176 | tf_op jit(solution)/shard_map/ppermute | solution.py:27
  (151 shorter events, 89.5 us)
Async XLA Ops:
  12.4 25.3 %collective-permute-start.2 = (bf16[512,1024]{1,0:T(8,128)(2,1)S(1)}, bf16[512,1024]{1,0:T(8,128)(2,1)S(1)}, u32[]{:S(2)}, u32[]{:S(2)}) collective-permute-start(bf16[512,1024]{1,0:T(8,128)(2,1)S(1)} %pad_maximum_fusion.1.refs_3_), channel_id=1, source_target_pairs={{0,1},{1,2},{2,3},{3,0},{4,5},{5,6},{6,7},{7,4},{8,9},{9,10},{10,1... | collective-permute-start | bytes 3145736 | tf_op jit(solution)/shard_map/ppermute | solution.py:27
  16.6 55.5 %collective-permute-start = (bf16[384,4096]{1,0:T(8,128)(2,1)}, bf16[384,4096]{1,0:T(8,128)(2,1)}, u32[]{:S(2)}, u32[]{:S(2)}) collective-permute-start(bf16[384,4096]{1,0:T(8,128)(2,1)} %pad_maximum_fusion), channel_id=1, source_target_pairs={{0,16},{16,0},{1,17},{17,1},{2,18},{18,2},{3,19},{19,3},{4,20},{20... | collective-permute-start | bytes 9437192 | tf_op jit(solution)/shard_map/ppermute | solution.py:31
  28.9 19.3 %collective-permute-start.11 = (bf16[512,1024]{1,0:T(8,128)(2,1)S(1)}, bf16[512,1024]{1,0:T(8,128)(2,1)}, u32[]{:S(2)}, u32[]{:S(2)}) collective-permute-start(bf16[512,1024]{1,0:T(8,128)(2,1)S(1)} %pad_maximum_fusion.1.refs_3_), channel_id=1, source_target_pairs={{0,3},{1,0},{2,1},{3,2},{4,7},{5,4},{6,5},{7,6},{8,11},{9,8},{10,9... | collective-permute-start | bytes 3145736 | tf_op jit(solution)/shard_map/ppermute | solution.py:27
  31.1 17.2 %collective-permute-start.13 = (bf16[512,1024]{1,0:T(8,128)(2,1)S(1)}, bf16[512,1024]{1,0:T(8,128)(2,1)}, u32[]{:S(2)}, u32[]{:S(2)}) collective-permute-start(bf16[512,1024]{1,0:T(8,128)(2,1)S(1)} %pad_maximum_fusion.1.refs_3_), channel_id=1, source_target_pairs={{0,16},{16,0},{1,17},{17,1},{2,18},{18,2},{3,19},{19,3},{4,20},{20... | collective-permute-start | bytes 3145736 | tf_op jit(solution)/shard_map/ppermute | solution.py:31
  35.1 19.9 %collective-permute-start.7 = (bf16[512,1024]{1,0:T(8,128)(2,1)S(1)}, bf16[512,1024]{1,0:T(8,128)(2,1)}, u32[]{:S(2)}, u32[]{:S(2)}) collective-permute-start(bf16[512,1024]{1,0:T(8,128)(2,1)S(1)} %constant_dynamic-update-slice_fusion.3.refs_4_), channel_id=1, source_target_pairs={{0,3},{1,0},{2,1},{3,2},{4,7},{5,4},{6,5},{7,6},{8,11},{9,8},{10,9... | collective-permute-start | bytes 3145736 | tf_op jit(solution)/shard_map/ppermute | solution.py:27
  37.8 19.2 %collective-permute-start.12 = (bf16[512,1024]{1,0:T(8,128)(2,1)S(1)}, bf16[512,1024]{1,0:T(8,128)(2,1)}, u32[]{:S(2)}, u32[]{:S(2)}) collective-permute-start(bf16[512,1024]{1,0:T(8,128)(2,1)S(1)} %constant_dynamic-update-slice_fusion.3.refs_4_), channel_id=1, source_target_pairs={{0,1},{1,2},{2,3},{3,0},{4,5},{5,6},{6,7},{7,4},{8,9},{9,10},{10,1... | collective-permute-start | bytes 3145736 | tf_op jit(solution)/shard_map/ppermute | solution.py:27
  42.0 43.0 %all-to-all-start = ((bf16[8,48,4096]{2,1,0:T(8,128)(2,1)}), bf16[8,48,4096]{2,1,0:T(8,128)(2,1)}, u32[]{:S(2)}, u32[]{:S(2)}) async-start(bf16[8,48,4096]{2,1,0:T(8,128)(2,1)} %bitcast.69), calls=%async_computation | async-start | bytes 6291456 | tf_op jit(solution)/shard_map/all_to_all | solution.py:417
  48.2 14.3 %collective-permute-start.14 = (bf16[512,1024]{1,0:T(8,128)(2,1)S(1)}, bf16[512,1024]{1,0:T(8,128)(2,1)S(1)}, u32[]{:S(2)}, u32[]{:S(2)}) collective-permute-start(bf16[512,1024]{1,0:T(8,128)(2,1)S(1)} %constant_dynamic-update-slice_fusion.3.refs_4_), channel_id=1, source_target_pairs={{0,16},{16,0},{1,17},{17,1},{2,18},{18,2},{3,19},{19,3},{4,20},{20... | collective-permute-start | bytes 3145736 | tf_op jit(solution)/shard_map/ppermute | solution.py:31
  48.3 14.7 %collective-permute-start.15 = (bf16[512,1024]{1,0:T(8,128)(2,1)S(1)}, bf16[512,1024]{1,0:T(8,128)(2,1)S(1)}, u32[]{:S(2)}, u32[]{:S(2)}) collective-permute-start(bf16[512,1024]{1,0:T(8,128)(2,1)S(1)} %collective-permute-done.2.refs_5_), channel_id=1, source_target_pairs={{0,16},{16,0},{1,17},{17,1},{2,18},{18,2},{3,19},{19,3},{4,20},{20... | collective-permute-start | bytes 3145736 | tf_op jit(solution)/shard_map/ppermute | solution.py:31
  55.0 16.2 %collective-permute-start.3 = (bf16[512,1024]{1,0:T(8,128)(2,1)S(1)}, bf16[512,1024]{1,0:T(8,128)(2,1)}, u32[]{:S(2)}, u32[]{:S(2)}) collective-permute-start(bf16[512,1024]{1,0:T(8,128)(2,1)S(1)} %collective-permute-done.2.refs_5_), channel_id=1, source_target_pairs={{0,1},{1,2},{2,3},{3,0},{4,5},{5,6},{6,7},{7,4},{8,9},{9,10},{10,1... | collective-permute-start | bytes 3145736 | tf_op jit(solution)/shard_map/ppermute | solution.py:27
  56.9 15.1 %collective-permute-start.8 = (bf16[512,1024]{1,0:T(8,128)(2,1)}, bf16[512,1024]{1,0:T(8,128)(2,1)}, u32[]{:S(2)}, u32[]{:S(2)}) collective-permute-start(bf16[512,1024]{1,0:T(8,128)(2,1)} %collective-permute-done.7.refs_8_), channel_id=1, source_target_pairs={{0,3},{1,0},{2,1},{3,2},{4,7},{5,4},{6,5},{7,6},{8,11},{9,8},{10,9... | collective-permute-start | bytes 3145736 | tf_op jit(solution)/shard_map/ppermute | solution.py:27
  62.5 15.9 %collective-permute-start.16 = (bf16[512,1024]{1,0:T(8,128)(2,1)}, bf16[512,1024]{1,0:T(8,128)(2,1)}, u32[]{:S(2)}, u32[]{:S(2)}) collective-permute-start(bf16[512,1024]{1,0:T(8,128)(2,1)} %collective-permute-done.11.refs_6_), channel_id=1, source_target_pairs={{0,16},{16,0},{1,17},{17,1},{2,18},{18,2},{3,19},{19,3},{4,20},{20... | collective-permute-start | bytes 3145736 | tf_op jit(solution)/shard_map/ppermute | solution.py:31
  63.0 22.0 %collective-permute-start.18 = (bf16[512,1024]{1,0:T(8,128)(2,1)}, bf16[512,1024]{1,0:T(8,128)(2,1)}, u32[]{:S(2)}, u32[]{:S(2)}) collective-permute-start(bf16[512,1024]{1,0:T(8,128)(2,1)} %collective-permute-done.7.refs_8_), channel_id=1, source_target_pairs={{0,16},{16,0},{1,17},{17,1},{2,18},{18,2},{3,19},{19,3},{4,20},{20... | collective-permute-start | bytes 3145736 | tf_op jit(solution)/shard_map/ppermute | solution.py:31
  72.1 32.8 %collective-permute-start.9 = (bf16[512,1024]{1,0:T(8,128)(2,1)}, bf16[512,1024]{1,0:T(8,128)(2,1)}, u32[]{:S(2)}, u32[]{:S(2)}) collective-permute-start(bf16[512,1024]{1,0:T(8,128)(2,1)} %collective-permute-done.3.refs_3_), channel_id=1, source_target_pairs={{0,16},{16,0},{1,17},{17,1},{2,18},{18,2},{3,19},{19,3},{4,20},{20... | collective-permute-start | bytes 3145736 | tf_op jit(solution)/shard_map/ppermute | solution.py:31
  72.1 32.8 %collective-permute-start.10 = (bf16[512,1024]{1,0:T(8,128)(2,1)}, bf16[512,1024]{1,0:T(8,128)(2,1)}, u32[]{:S(2)}, u32[]{:S(2)}) collective-permute-start(bf16[512,1024]{1,0:T(8,128)(2,1)} %collective-permute-done.8.refs_4_), channel_id=1, source_target_pairs={{0,16},{16,0},{1,17},{17,1},{2,18},{18,2},{3,19},{19,3},{4,20},{20... | collective-permute-start | bytes 3145736 | tf_op jit(solution)/shard_map/ppermute | solution.py:31
  125.5 26.2 %all-to-all-start.1 = ((bf16[8,48,2048]{2,1,0:T(8,128)(2,1)}), bf16[8,48,2048]{2,1,0:T(8,128)(2,1)}, u32[]{:S(2)}, u32[]{:S(2)}) async-start(bf16[8,48,2048]{2,1,0:T(8,128)(2,1)} %bitcast.70), calls=%async_computation.1 | async-start | bytes 3145728 | tf_op jit(solution)/shard_map/all_to_all | solution.py:438
  137.6 13.8 %collective-permute-start.19 = (bf16[192,1024]{1,0:T(8,128)(2,1)S(1)}, bf16[192,1024]{1,0:T(8,128)(2,1)}, u32[]{:S(2)}, u32[]{:S(2)}) collective-permute-start(bf16[192,1024]{1,0:T(8,128)(2,1)S(1)} %get-tuple-element.34), channel_id=1, source_target_pairs={{0,16},{16,0},{1,17},{17,1},{2,18},{18,2},{3,19},{19,3},{4,20},{20... | collective-permute-start | bytes 1179656 | tf_op jit(solution)/shard_map/ppermute | solution.py:31
  163.4 26.2 %collective-permute-start.22 = (bf16[512,1024]{1,0:T(8,128)(2,1)S(1)}, bf16[512,1024]{1,0:T(8,128)(2,1)S(1)}, u32[]{:S(2)}, u32[]{:S(2)}) collective-permute-start(bf16[512,1024]{1,0:T(8,128)(2,1)S(1)} %head_partial.9), channel_id=1, source_target_pairs={{0,12},{1,13},{2,14},{3,15},{4,0},{5,1},{6,2},{7,3},{8,4},{9,5},{1... | collective-permute-start | bytes 3145736 | tf_op jit(solution)/shard_map/ppermute | solution.py:27
  169.9 19.6 %collective-permute-start.21 = (bf16[512,1024]{1,0:T(8,128)(2,1)S(1)}, bf16[512,1024]{1,0:T(8,128)(2,1)S(1)}, u32[]{:S(2)}, u32[]{:S(2)}) collective-permute-start(bf16[512,1024]{1,0:T(8,128)(2,1)S(1)} %head_partial.8), channel_id=1, source_target_pairs={{0,4},{1,5},{2,6},{3,7},{4,8},{5,9},{6,10},{7,11},{8,12},{9,13},{1... | collective-permute-start | bytes 3145736 | tf_op jit(solution)/shard_map/ppermute | solution.py:27
  186.3 15.6 %collective-permute-start.26 = (bf16[512,1024]{1,0:T(8,128)(2,1)S(1)}, bf16[512,1024]{1,0:T(8,128)(2,1)S(1)}, u32[]{:S(2)}, u32[]{:S(2)}) collective-permute-start(bf16[512,1024]{1,0:T(8,128)(2,1)S(1)} %head_partial.13), channel_id=1, source_target_pairs={{0,12},{1,13},{2,14},{3,15},{4,0},{5,1},{6,2},{7,3},{8,4},{9,5},{1... | collective-permute-start | bytes 3145736 | tf_op jit(solution)/shard_map/ppermute | solution.py:27
  192.4 16.3 %collective-permute-start.27 = (bf16[512,1024]{1,0:T(8,128)(2,1)S(1)}, bf16[512,1024]{1,0:T(8,128)(2,1)S(1)}, u32[]{:S(2)}, u32[]{:S(2)}) collective-permute-start(bf16[512,1024]{1,0:T(8,128)(2,1)S(1)} %head_partial.14), channel_id=1, source_target_pairs={{0,4},{1,5},{2,6},{3,7},{4,8},{5,9},{6,10},{7,11},{8,12},{9,13},{1... | collective-permute-start | bytes 3145736 | tf_op jit(solution)/shard_map/ppermute | solution.py:27
  195.6 27.1 %collective-permute-start.23 = (bf16[512,1024]{1,0:T(8,128)(2,1)S(1)}, bf16[512,1024]{1,0:T(8,128)(2,1)S(1)}, u32[]{:S(2)}, u32[]{:S(2)}) collective-permute-start(bf16[512,1024]{1,0:T(8,128)(2,1)S(1)} %head_partial.10), channel_id=1, source_target_pairs={{0,4},{1,5},{2,6},{3,7},{4,8},{5,9},{6,10},{7,11},{8,12},{9,13},{1... | collective-permute-start | bytes 3145736 | tf_op jit(solution)/shard_map/ppermute | solution.py:27
  198.5 24.2 %collective-permute-start.24 = (bf16[512,1024]{1,0:T(8,128)(2,1)S(1)}, bf16[512,1024]{1,0:T(8,128)(2,1)S(1)}, u32[]{:S(2)}, u32[]{:S(2)}) collective-permute-start(bf16[512,1024]{1,0:T(8,128)(2,1)S(1)} %head_partial.11), channel_id=1, source_target_pairs={{0,12},{1,13},{2,14},{3,15},{4,0},{5,1},{6,2},{7,3},{8,4},{9,5},{1... | collective-permute-start | bytes 3145736 | tf_op jit(solution)/shard_map/ppermute | solution.py:27
  211.6 18.2 %collective-permute-start.28 = (bf16[128,1024]{1,0:T(8,128)(2,1)S(1)}, bf16[128,1024]{1,0:T(8,128)(2,1)S(1)}, u32[]{:S(2)}, u32[]{:S(2)}) collective-permute-start(bf16[128,1024]{1,0:T(8,128)(2,1)S(1)} %get-tuple-element.47), channel_id=1, source_target_pairs={{0,1},{1,2},{2,3},{3,0},{4,5},{5,6},{6,7},{7,4},{8,9},{9,10},{10,1... | collective-permute-start | bytes 786440 | tf_op jit(solution)/shard_map/ppermute | solution.py:27
  (35 other events, 282.7 us)

commit v3 on v2

v3 whole, which is shorter than its diff:
```python
import jax
import jax.numpy as jnp
from jax import lax
from jax.experimental import pallas as pl
from jax.experimental.pallas import tpu as pltpu
from jax.sharding import Mesh, PartitionSpec as P

EPSILON = 1e-06
BLOCK = 256
RING = 4
SWAP = [(0, 1), (1, 0)]
BF16 = jnp.bfloat16
F32 = jnp.float32


def shift(value, place, step):
    pairs = []
    for c in range(2):
        for y in range(RING):
            for z in range(RING):
                to_y, to_z = y, z
                if (place == 1) == (c == 0):
                    to_y = (y + step) % RING
                else:
                    to_z = (z + step) % RING
                pairs.append((c * 16 + y * 4 + z, c * 16 + to_y * 4 + to_z))
    return lax.ppermute(value, ("c", "y", "z"), pairs)


def swap(value):
    return lax.ppermute(value, "c", SWAP)


def block_at(core, d1, d2):
    y, z = lax.axis_index("y"), lax.axis_index("z")
    far_y = jnp.where(core == 0, d1, d2)
    far_z = jnp.where(core == 0, d2, d1)
    return ((y + far_y) % RING) * RING + (z + far_z) % RING


def together(*values):
    return lax.optimization_barrier(values)


def project_kernel(count, kind, at_ref, own_ref, arrived_ref, *refs):
    pieces, rest = refs[:count], refs[count:]
    if kind == "first":
        head_ref, pre_ref, states, stored = rest
    elif kind == "middle":
        base_ref, _, head_ref, pre_ref, states, stored = rest
    else:
        base_ref, counts_ref, _, head_ref, pre_ref, *outs, states, stored = rest
    half = count // 2
    blocks = 2 * half
    rows = arrived_ref.shape[0]
    width = 1024

    def store(k):
        row = pl.multiple_of(at_ref[0, k] * BLOCK, BLOCK)
        col = pl.multiple_of(at_ref[1, k] * width, width)
        return pltpu.make_async_copy(
            pieces[k // 2].at[pl.ds((k % 2) * BLOCK, BLOCK), :],
            head_ref.at[pl.ds(row, BLOCK), pl.ds(col, width)],
            stored.at[k],
        )

    for k in range(2 * blocks):
        store(k).start()
    for side in range(2):
        for k in range(blocks):
            col = pl.multiple_of(at_ref[0, side * blocks + k] * BLOCK, BLOCK)
            states[pl.ds(0, rows), pl.ds(k * BLOCK, BLOCK)] = own_ref[pl.ds(0, rows), pl.ds(col, BLOCK)]
            states[pl.ds(rows, rows), pl.ds(k * BLOCK, BLOCK)] = arrived_ref[:, pl.ds(col, BLOCK)]

        def strip(n, _, side=side):
            at_col = pl.multiple_of(n * BLOCK, BLOCK)
            out_col = pl.multiple_of(at_ref[1, side * blocks] * width + at_col, BLOCK)
            total = None
            for i in range(half):
                product = jnp.dot(
                    states[:, pl.ds(i * 512, 512)],
                    pieces[side * half + i][:, pl.ds(at_col, BLOCK)],
                    preferred_element_type=F32,
                )
                total = product if total is None else total + product
            if kind != "first":
                total = total + base_ref[:, pl.ds(out_col, BLOCK)]
            pre_ref[:, pl.ds(out_col, BLOCK)] = total
            return 0

        lax.fori_loop(0, width // BLOCK, strip, 0)
    if kind == "last":
        contrast(counts_ref, pre_ref, *outs)
    for k in range(2 * blocks):
        store(k).wait()


def contrast(counts_ref, pre_ref, inverse_ref, emb_ref, mixing_ref, first_ref, grad_ref):
    rows = counts_ref.shape[0]
    width = pre_ref.shape[1]
    scale = 16.0 / width
    chunk = 32

    def normalize(i, _):
        at = pl.ds(pl.multiple_of(i * chunk, chunk), chunk)
        values = pre_ref[at, :]
        inverse = lax.rsqrt(jnp.mean(values * values, axis=-1, keepdims=True) + EPSILON)
        emb_ref[at, :] = (values * inverse).astype(BF16)

        @pl.when(i < 2 * rows // chunk)
        def _():
            inverse_ref[at, :] = jnp.broadcast_to(inverse, (chunk, 128))

        return 0

    lax.fori_loop(0, pre_ref.shape[0] // chunk, normalize, 0)
    query = emb_ref[pl.ds(0, rows), :]
    passage = emb_ref[pl.ds(rows, rows), :]
    fetched = emb_ref[pl.ds(2 * rows, 2 * rows), :]
    positive = (
        jnp.sum(query.astype(F32) * passage.astype(F32), axis=1, keepdims=True) * scale
    )
    table = dot(query, fetched, ((1,), (1,))) * scale
    counts = counts_ref[...]
    top = jnp.maximum(
        positive, jnp.max(jnp.where(counts > 0, table, -1e30), axis=1, keepdims=True)
    )
    raised = jnp.where(counts > 0, jnp.exp(jnp.where(counts > 0, table - top, 0.0)), 0.0)
    raised_positive = jnp.exp(positive - top)
    whole = raised_positive + jnp.sum(raised * counts, axis=1, keepdims=True)
    first = (raised_positive / whole - 1.0).astype(BF16).astype(F32)
    mixing = ((raised / whole).astype(BF16).astype(F32) * counts).astype(BF16)
    first_ref[...] = jnp.broadcast_to(first, (rows, 128))
    mixing_ref[...] = mixing
    grad_ref[...] = dot(mixing, query, ((0,), (0,))).astype(BF16)


def vmem(count):
    return [pl.BlockSpec(memory_space=pltpu.VMEM)] * count


def project(kind, at, both_states, arrived, pieces, *more):
    count = len(pieces)
    rows = arrived.shape[0]
    half = rows // 2
    anywhere = pl.BlockSpec(memory_space=pl.ANY)
    ins = [pl.BlockSpec(memory_space=pltpu.SMEM)] + vmem(2 + count)
    outs = [anywhere] + vmem(1)
    types = [
        jax.ShapeDtypeStruct((4096, 2048), BF16),
        jax.ShapeDtypeStruct((2 * rows, 2048), F32),
    ]
    aliases = {}
    if kind != "first":
        ins += vmem(1 if kind == "middle" else 2) + [anywhere]
        aliases = {3 + count: 1, len(ins) - 1: 0}
    if kind == "last":
        outs += vmem(5)
        for shape, dtype in (
            ((rows, 128), F32),
            ((2 * rows, 2048), BF16),
            ((half, rows), BF16),
            ((half, 128), F32),
            ((rows, 2048), BF16),
        ):
            types.append(jax.ShapeDtypeStruct(shape, dtype))
    return pl.pallas_call(
        lambda *refs: project_kernel(count, kind, *refs),
        in_specs=ins,
        out_specs=outs,
        out_shape=types,
        scratch_shapes=[
            pltpu.VMEM((2 * rows, count // 2 * 512), BF16),
            pltpu.SemaphoreType.DMA((2 * count,)),
        ],
        input_output_aliases=aliases,
        compiler_params=pltpu.CompilerParams(vmem_limit_bytes=28 * 1024 * 1024),
        name="project_" + kind,
    )(at, both_states, arrived, *pieces, *more)


def slopes_kernel(part, cols_ref, pre_ref, inverse_ref, first_ref, emb_ref, left_ref, right_ref, out_ref, keep_ref, send_ref, grad_ref):
    rows, chunk = out_ref.shape[0], 32
    width = pre_ref.shape[1]
    depth = left_ref.shape[1]
    right = right_ref[pl.ds(2 * rows, depth), :] if part == 0 else right_ref[...]
    grad_ref[...] = jnp.dot(left_ref[...], right, preferred_element_type=F32)

    def some(i, _):
        at = pl.ds(pl.multiple_of(i * chunk, chunk), chunk)
        mine = pl.ds(pl.multiple_of(part * rows + i * chunk, chunk), chunk)
        other = pl.ds(pl.multiple_of((1 - part) * rows + i * chunk, chunk), chunk)
        grad = first_ref[at, :1] * emb_ref[other, :].astype(F32) + grad_ref[at, :]
        values = pre_ref[mine, :]
        inverse = inverse_ref[mine, :1]
        along = jnp.mean(grad * values, axis=-1, keepdims=True)
        out_ref[at, :] = (inverse * grad - values * (inverse * inverse * inverse * along)).astype(BF16)
        return 0

    lax.fori_loop(0, rows // chunk, some, 0)
    for k in range(width // BLOCK // 2):
        for row, ref in ((0, keep_ref), (1, send_ref)):
            col = pl.multiple_of(cols_ref[row, k] * BLOCK, BLOCK)
            ref[:, pl.ds(k * BLOCK, BLOCK)] = out_ref[:, pl.ds(col, BLOCK)]


def slopes_of(part, cols, pre, inverse, first, emb, left, right):
    rows = first.shape[0]
    width = pre.shape[1]
    return pl.pallas_call(
        lambda *refs: slopes_kernel(part, *refs),
        in_specs=[pl.BlockSpec(memory_space=pltpu.SMEM)] + vmem(6),
        out_specs=vmem(3),
        out_shape=[
            jax.ShapeDtypeStruct((rows, width), BF16),
            jax.ShapeDtypeStruct((rows, width // 2), BF16),
            jax.ShapeDtypeStruct((rows, width // 2), BF16),
        ],
        scratch_shapes=[pltpu.VMEM((rows, width), F32)],
        compiler_params=pltpu.CompilerParams(vmem_limit_bytes=16 * 1024 * 1024),
        name="slopes_of",
    )(cols, pre, inverse, first, emb, left, right)


def input_grad_kernel(slopes_ref, head_ref, out_ref):
    out_ref[...] = dot(slopes_ref[...], head_ref[...], ((1,), (1,))).astype(BF16)


def input_grad(slopes, head):
    rows, width = slopes.shape
    depth = head.shape[0]
    return pl.pallas_call(
        input_grad_kernel,
        grid=(depth // 512,),
        in_specs=[
            pl.BlockSpec((rows, width), lambda k: (0, 0)),
            pl.BlockSpec((512, width), lambda k: (k, 0)),
        ],
        out_specs=pl.BlockSpec((rows, 512), lambda k: (0, k)),
        out_shape=jax.ShapeDtypeStruct((rows, depth), BF16),
        compiler_params=pltpu.CompilerParams(vmem_limit_bytes=16 * 1024 * 1024),
        name="input_grad",
    )(slopes, pltpu.with_memory_space_constraint(head, pltpu.HBM))


def partial_kernel(outs, adds, at_ref, states_ref, slopes_ref, *refs):
    for k in range(outs * 2):
        row = pl.multiple_of(at_ref[k] * BLOCK, BLOCK)
        part = pl.ds(k % 2 * BLOCK, BLOCK)
        total = jnp.dot(
            states_ref[pl.ds(row, BLOCK), :], slopes_ref[...], preferred_element_type=F32
        ) * (1.0 / 128.0)
        for ref in refs[k // 2 * adds : (k // 2 + 1) * adds]:
            total = total + ref[part, :].astype(F32)
        refs[outs * adds + k // 2][part, :] = total.astype(BF16)


def head_partial(states, slopes, at, adds):
    outs, width = len(adds), slopes.shape[1]
    return pl.pallas_call(
        lambda *refs: partial_kernel(outs, len(adds[0]), *refs),
        in_specs=[pl.BlockSpec(memory_space=pltpu.SMEM)] + vmem(2 + outs * len(adds[0])),
        out_specs=vmem(outs),
        out_shape=[jax.ShapeDtypeStruct((2 * BLOCK, width), BF16)] * outs,
        compiler_params=pltpu.CompilerParams(vmem_limit_bytes=16 * 1024 * 1024),
        name="head_partial",
    )(at, states, slopes, *[value for some in adds for value in some])


def add(*values):
    total = values[0].astype(F32)
    for value in values[1:]:
        total = total + value.astype(F32)
    return total.astype(BF16)


def scatter_head(states, slopes, core, beside, given):
    def part(d1s, d2s, adds):
        at = [block_at(core, d1, d2) for d1, some in zip(d1s, d2s) for d2 in some]
        return head_partial(states, slopes, jnp.stack(at).astype(jnp.int32), adds)

    a, b = (2, 1), (-1, 0)
    far_a, far_b = part((2, 2), (a, b), ((), ()))
    far_a, far_b = shift(far_a, 1, 1), shift(far_b, 1, -1)
    up_b, down_a = part((1, -1), (b, a), ((), ()))
    up_b, down_a, given = together(up_b, down_a, given)
    up_b, down_a = shift(up_b, 1, 1), shift(down_a, 1, -1)
    extra = beside(given)
    far_a, far_b, extra = together(far_a, far_b, extra)
    up_a, down_b = part((1, -1), (a, b), ((far_a,), (far_b,)))
    up_a, down_b = shift(up_a, 1, 1), shift(down_b, 1, -1)
    mine_a, mine_b = part((0, 0), (a, b), ((down_a,), (up_b,)))
    up_a, down_b, mine_a, mine_b = together(up_a, down_b, mine_a, mine_b)
    half = BLOCK // 2
    far, up = mine_a[:BLOCK], mine_a[BLOCK:]
    down, mine = mine_b[:BLOCK], mine_b[BLOCK:]
    up_far, up_up = up_a[:BLOCK], up_a[BLOCK:]
    down_down, down_mine = down_b[:BLOCK], down_b[BLOCK:]
    far_a = shift(add(far[:half], up_far[:half]), 2, 1)
    far_b = shift(add(far[half:], up_far[half:]), 2, -1)
    up_b = shift(add(up[half:], up_up[half:]), 2, 1)
    down_a = shift(add(down[:half], down_down[:half]), 2, -1)
    far_a, far_b, up_b, down_a = together(far_a, far_b, up_b, down_a)
    up_a = shift(add(up[:half], up_up[:half], far_a), 2, 1)
    down_b = shift(add(down[half:], down_down[half:], far_b), 2, -1)
    up_a, down_b = together(up_a, down_b)
    total = jnp.concatenate(
        [
            add(mine[:half], down_mine[:half], down_a, up_a),
            add(mine[half:], down_mine[half:], up_b, down_b),
        ],
        axis=0,
    )
    arrived = together(
        *[
            lax.ppermute(
                total[:, step * BLOCK : (step + 1) * BLOCK],
                "x",
                [(i, (i + step) % RING) for i in range(RING)],
            )
            for step in (1, 2, 3)
        ]
    )
    out = total[:, :BLOCK].astype(F32)
    for value in arrived:
        out = out + value.astype(F32)
    return out, extra


def dot(a, b, contract=((1,), (0,))):
    return lax.dot_general(a, b, (contract, ((), ())), preferred_element_type=F32)


def per_device(queries, passages, head_weight, send_lists, neg_slots):
    core, x = lax.axis_index("c"), lax.axis_index("x")
    rows_dev, depth = queries.shape
    width = head_weight.shape[1]
    groups, capacity = send_lists.shape[2], send_lists.shape[3]
    slot_count = groups * capacity
    flat_lists = send_lists.reshape(slot_count)

    def places_of(*pieces):
        places = [(d1, d2) for d1s, d2 in pieces for d1 in d1s]
        at = [block_at(core, d1, d2) for d1, d2 in places] + [block_at(1 - core, d1, d2) for d1, d2 in places]
        side = [core] * len(places) + [1 - core] * len(places)
        return jnp.stack([jnp.stack(at), jnp.stack(side)]).astype(jnp.int32)

    a, b = (0, -1), (1, 2)
    states = jnp.concatenate([queries, passages], axis=0)
    owner = (flat_lists[None, :] == jnp.arange(rows_dev, dtype=jnp.int32)[:, None]).astype(BF16)
    own = lax.dynamic_slice_in_dim(head_weight, core * (width // 2), width // 2, axis=1)

    up, down = shift(own, 1, 1), shift(own, 1, -1)
    picked = dot(owner, passages, ((0,), (0,))).astype(BF16).reshape(groups, capacity, depth)
    up, down, picked = together(up, down, picked)
    arrived = lax.all_to_all(picked, ("x", "c"), split_axis=0, concat_axis=0, tiled=True)
    arrived = arrived.reshape(slot_count, depth)

    first = jnp.concatenate([own, up], axis=0)
    first_up, first_down = shift(first, 2, 1), shift(first, 2, -1)
    half = BLOCK // 2
    far_a, far_b = shift(up[:half], 1, 1), shift(down[half:], 1, -1)
    first_up, first_down, far_a, far_b = together(first_up, first_down, far_a, far_b)

    second = jnp.concatenate([down, far_a, far_b], axis=0)
    second_up, second_down = shift(second, 2, 1), shift(second, 2, -1)
    early = [first, second, first_up, first_down]
    early = early + [swap(piece) for piece in early]
    both_states = jnp.concatenate([states, swap(states)], axis=0)
    turned = both_states.T
    slot_ids = jnp.arange(slot_count, dtype=jnp.int32)[None, :]
    counts = jnp.zeros((rows_dev, slot_count), F32)
    for j in range(neg_slots.shape[1]):
        counts = counts + (neg_slots[:, j : j + 1] == slot_ids).astype(F32)
    second_up, second_down, arrived, first_up = together(second_up, second_down, arrived, first_up)

    first_far, second_far = shift(first_up, 2, 1), shift(second_down, 2, -1)
    head, pre = project(
        "first", places_of((a, 0), (b, 0), (a, -1), (a, 1)), both_states, arrived, early
    )
    middle = [second_up, second_down, swap(second_up), swap(second_down)]
    head, pre = project("middle", places_of((b, -1), (b, 1)), both_states, arrived, middle, pre, head)
    first_far, second_far, pre, counts, turned = together(first_far, second_far, pre, counts, turned)
    late = [first_far, second_far, swap(first_far), swap(second_far)]
    head, pre, inverse, emb, mixing, first, fetched_grad = project(
        "last", places_of((a, 2), (b, 2)), both_states, arrived, late, pre, counts, head
    )
    returned = lax.all_to_all(
        fetched_grad.reshape(groups, capacity, width),
        ("x", "c"),
        split_axis=0,
        concat_axis=0,
        tiled=True,
    ).reshape(slot_count, width)

    to_x = [(x + step) % RING for step in range(RING)]
    cols = jnp.stack(
        [jnp.stack([2 * to + core for to in to_x]), jnp.stack([2 * to + 1 - core for to in to_x])]
    ).astype(jnp.int32)
    query_dy, query_keep, query_send = slopes_of(0, cols, pre, inverse, first, emb, mixing, emb)
    query_other = swap(query_send)
    query_grads = input_grad(query_dy, head)
    returned, query_grads, query_other = lax.optimization_barrier((returned, query_grads, query_other))

    passage_dy, passage_keep, passage_send = slopes_of(
        1, cols, pre, inverse, first, emb, owner, returned
    )
    passage_other = swap(passage_send)
    slopes = jnp.concatenate([query_keep, passage_keep, query_other, passage_other], axis=0)
    head_grads, passage_grads = scatter_head(
        turned, slopes, core, lambda slopes: input_grad(slopes, head), passage_dy
    )
    return (query_grads, passage_grads, head_grads)


def solution(mesh):
    fine = Mesh(mesh.devices.reshape(4, 2, 4, 4), ("x", "c", "y", "z"))
    every = ("x", "c", "y", "z")
    return jax.shard_map(
        per_device,
        mesh=fine,
        in_specs=(
            P(every, None),
            P(every, None),
            P(("y", "z"), None),
            P(("x", "c"), ("y", "z"), None, None),
            P(every, None),
        ),
        out_specs=(P(every, None), P(every, None), P(("y", "z"), ("x", "c"))),
        check_vma=False,
    )
```

time: 255 us -> 256 us (level)
  other arithmetic: 5.98 us -> 23.7 us
  local copies, waits for them, and re-layouts: 29.9 us -> 45 us
  waiting for transfers between devices: 72.5 us -> 59.4 us
  Pallas kernels: 85.2 us -> 72.4 us
  starting transfers between devices: 54.3 us -> 48.6 us
    ppermute x22, waiting for transfers between devices: 61.5 us -> 38.4 us  [shift(): return lax.ppermute(value, ('c', 'y', 'z'), pairs)]
    pallas_call x12 -> x9, Pallas kernels: 70.1 us -> 48.3 us  [the longest x3 32.2 us: project(): pl.pallas_call(lambda *refs: project_kernel(count, kind, *refs), in_specs...]
    concatenate x2 -> x3, other arithmetic: 0.1 us -> 10.1 us  [the longest x1 7.8 us: per_device(): both_states = jnp.concatenate([states, swap(states)], axis=0)]
    pallas_call x2, Pallas kernels: 15.1 us -> 24 us  [input_grad(): pl.pallas_call(input_grad_kernel, grid=(depth // 512,), in_specs=[pl.Bloc...]
    transpose x0 -> x1, other arithmetic: none -> 8.09 us  [per_device(): turned = both_states.T]
    unnamed x49 -> x59, local copies, waits for them, and re-layouts: 25.3 us -> 32.3 us
    concatenate x1, local copies, waits for them, and re-layouts: 3.98 us -> 8.71 us  [per_device(): both_states = jnp.concatenate([states, swap(states)], axis=0)]
    ppermute x11, waiting for transfers between devices: 0.56 us -> 4.41 us  [swap(): return lax.ppermute(value, 'c', SWAP)]
  transfers between devices with their start and end apart: 38 -> 38, of which waited for: 19 -> 18; matrix products, arithmetic and copies ran while one was open for 7% -> 19% of each run, Pallas kernels for 23% -> 21%
where the time goes in v3:
time: 256 us; the launch traced here: 255 us
  Pallas kernels  72.4 us (28%)
  waiting for transfers between devices  59.4 us (23%)
  starting transfers between devices  48.6 us (19%)
  local copies, waits for them, and re-layouts  45 us (18%)
  other arithmetic  23.7 us (9%)
  matrix products  4.29 us (2%)
    ppermute x22, waiting for transfers between devices, shift(): return lax.ppermute(value, ('c', 'y', 'z'), pairs)  38.4 us
    ppermute x22, starting transfers between devices, shift(): return lax.ppermute(value, ('c', 'y', 'z'), pairs)  33.6 us
    unnamed x59, local copies, waits for them, and re-layouts  32.3 us
    pallas_call x3, Pallas kernels, project(): pl.pallas_call(lambda *refs: project_kernel(count, kind, *refs), in_specs...  32.2 us
    pallas_call x2, Pallas kernels, input_grad(): pl.pallas_call(input_grad_kernel, grid=(depth // 512,), in_specs=[pl.Bloc...  24 us
    pallas_call x4, Pallas kernels, head_partial(): pl.pallas_call(lambda *refs: partial_kernel(outs, len(adds[0]), *refs), i...  9.38 us
    all_to_all x1, waiting for transfers between devices, per_device(): lax.all_to_all(picked, ('x', 'c'), split_axis=0, concat_axis=0, tiled=True)  9.28 us
    concatenate x1, local copies, waits for them, and re-layouts, per_device(): both_states = jnp.concatenate([states, swap(states)], axis=0)  8.71 us
  transfers between devices with their start and end apart: 38, of which 18 were waited for; matrix products, arithmetic and copies ran while one was open for 19% of the time, Pallas kernels for 21%

profile of v3, /device:TPU:0, one launch (start us, length us, event | category | flops | bytes accessed | tf_op | source)
XLA Modules:
  0.0 255.0 jit_solution(16800328168112760658)
XLA Ops:
  6.0 3.2 %copy.14 = bf16[192,4096]{0,1:T(8,128)(2,1)S(1)} copy(bf16[192,4096]{1,0:T(8,128)(2,1)} %param.5) | data formatting | bytes 3145728 | tf_op args[0]
  9.1 4.2 %copy.15 = bf16[192,4096]{0,1:T(8,128)(2,1)} copy(bf16[192,4096]{1,0:T(8,128)(2,1)} %param.6) | data formatting | bytes 3145728 | tf_op args[1]
  13.4 4.3 %convolution_convert_fusion = bf16[384,4096]{1,0:T(8,128)(2,1)} fusion(bf16[192,4096]{1,0:T(8,128)(2,1)} %param.6, s32[384]{0:T(512)S(1)} %eq.458), kind=kOutput, calls=%fused_computation.1 | convolution fusion | flops 605626368 | bytes 4720128 | tf_op jit(solution)/shard_map/dot_general | solution.py:331
  26.9 4.4 %all-to-all-start = ((bf16[8,48,4096]{2,1,0:T(8,128)(2,1)}), bf16[8,48,4096]{2,1,0:T(8,128)(2,1)S(1)}, u32[]{:S(2)}, u32[]{:S(2)}) async-start(bf16[8,48,4096]{2,1,0:T(8,128)(2,1)} %bitcast.78), calls=%async_computation | async-start | bytes 6291456 | tf_op jit(solution)/shard_map/all_to_all | solution.py:356
  42.0 3.2 %collective-permute-start.8 = (bf16[512,1024]{1,0:T(8,128)(2,1)}, bf16[512,1024]{1,0:T(8,128)(2,1)}, u32[]{:S(2)}, u32[]{:S(2)}) collective-permute-start(bf16[512,1024]{1,0:T(8,128)(2,1)} %constant_dynamic-update-slice_fusion.refs_4_), channel_id=1, source_target_pairs={{0,3},{1,0},{2,1},{3,2},{4,7},{5,4},{6,5},{7,6},{8,11},{9,8},{10,9... | collective-permute-start | bytes 3145736 | tf_op jit(solution)/shard_map/ppermute | solution.py:27
  45.7 12.6 %collective-permute-done.7.refs_3_ = bf16[512,1024]{1,0:T(8,128)(2,1)} collective-permute-done((bf16[512,1024]{1,0:T(8,128)(2,1)}, bf16[512,1024]{1,0:T(8,128)(2,1)}, u32[]{:S(2)}, u32[]{:S(2)}) %collective-permute-start.7) | collective-permute-done | bytes 1048608 | tf_op jit(solution)/shard_map/ppermute | solution.py:27
  60.5 9.3 %all-to-all-done = bf16[8,48,4096]{2,1,0:T(8,128)(2,1)S(1)} async-done(((bf16[8,48,4096]{2,1,0:T(8,128)(2,1)}), bf16[8,48,4096]{2,1,0:T(8,128)(2,1)S(1)}, u32[]{:S(2)}, u32[]{:S(2)}) %all-to-all-start) | async-done | bytes 3145760 | tf_op jit(solution)/shard_map/all_to_all | solution.py:356
  72.1 7.8 %pad_maximum_fusion = bf16[768,4096]{0,1:T(8,128)(2,1)} fusion(bf16[384,4096]{0,1:T(8,128)(2,1)} %collective-permute-done, bf16[192,4096]{0,1:T(8,128)(2,1)} %copy.15, bf16[192,4096]{0,1:T(8,128)(2,1)} %copy-done.20), kind=kLoop, calls=%fused_computation | loop fusion | flops 18874368 | bytes 12582912 | tf_op jit(solution)/shard_map/concatenate | solution.py:369
  79.9 8.7 %copy.18.refs_1_ = bf16[768,4096]{1,0:T(8,128)(2,1)} copy(bf16[768,4096]{0,1:T(8,128)(2,1)} %pad_maximum_fusion) | data formatting | bytes 12582912 | tf_op jit(solution)/shard_map/concatenate | solution.py:369
  88.6 8.1 %fusion.7.refs_1_ = bf16[4096,768]{1,0:T(8,128)(2,1)} fusion(bf16[384,4096]{0,1:T(8,128)(2,1)} %collective-permute-done, bf16[192,4096]{0,1:T(8,128)(2,1)} %copy.15, bf16[192,4096]{0,1:T(8,128)(2,1)} %copy-done.20), kind=kLoop, calls=%fused_computation.62 | loop fusion | flops 18874368 | bytes 12582912 | tf_op jit(solution)/shard_map/transpose | solution.py:370
  96.7 12.6 %project_first.1 = (bf16[4096,2048]{1,0:T(8,128)(2,1)}, f32[768,2048]{1,0:T(8,128)S(1)}) custom-call(s32[2,16]{1,0:T(2,128)S(1)} %pad_add_fusion.2.refs_0_, bf16[768,4096]{1,0:T(8,128)(2,1)S(1)} %copy-done.2, bf16[384,4096]{1,0:T(8,128)(2,1)S(1)} %bitcast.74, bf16[512,1024]{1,0:T(8,128)(2,1)} %pad_maximum_fusion.2.refs_3_, ...), custom_call_target="tpu_custom_call" | custom-call | tf_op jit(solution)/shard_map/project_first/pallas_call | solution.py:167
  114.9 7.7 %project_middle.1 = (bf16[4096,2048]{1,0:T(8,128)(2,1)}, f32[768,2048]{1,0:T(8,128)S(1)}) custom-call(s32[2,8]{1,0:T(2,128)S(1)} %get-tuple-element.153.refs_0_, bf16[768,4096]{1,0:T(8,128)(2,1)S(1)} %copy-done.2, bf16[384,4096]{1,0:T(8,128)(2,1)S(1)} %bitcast.75, ...), custom_call_target="tpu_custom_call", output_to_operand_aliasing={{1}: (7, {}), {0}: (8, {})} | custom-call | tf_op jit(solution)/shard_map/project_middle/pallas_call | solution.py:167
  127.1 11.9 %project_last.1 = (bf16[4096,2048]{1,0:T(8,128)(2,1)}, f32[768,2048]{1,0:T(8,128)S(1)}, f32[384,128]{1,0:T(8,128)S(1)}, bf16[768,2048]{1,0:T(8,128)(2,1)S(1)}, b...) custom-call(s32[2,8]{1,0:T(2,128)S(1)} %get-tuple-element.154.refs_0, ...), custom_call_target="tpu_custom_call", output_to_operand_aliasing={{1}: (7, {}), {0}: (9, {})} | custom-call | tf_op jit(solution)/shard_map/project_last/pallas_call | solution.py:167
  145.9 4.6 %all-to-all-start.1 = ((bf16[8,48,2048]{2,1,0:T(8,128)(2,1)}), bf16[8,48,2048]{2,1,0:T(8,128)(2,1)}, u32[]{:S(2)}, u32[]{:S(2)}) async-start(bf16[8,48,2048]{2,1,0:T(8,128)(2,1)} %bitcast.77), calls=%async_computation.1 | async-start | bytes 3145728 | tf_op jit(solution)/shard_map/all_to_all | solution.py:388
  157.6 12.0 %input_grad.2 = bf16[192,4096]{1,0:T(8,128)(2,1)} custom-call(bf16[192,2048]{1,0:T(8,128)(2,1)S(1)} %get-tuple-element.91.slopes_ref, bf16[4096,2048]{1,0:T(8,128)(2,1)} %get-tuple-element.92.head_ref), custom_call_target="tpu_custom_call" | custom-call | tf_op jit(solution)/shard_map/input_grad/pallas_call | solution.py:232
  176.0 3.9 %slopes_of.3 = (bf16[192,2048]{1,0:T(8,128)(2,1)S(1)}, bf16[192,1024]{1,0:T(8,128)(2,1)S(1)}, bf16[192,1024]{1,0:T(8,128)(2,1)S(1)}) custom-call(s32[2,4]{1,0:T(2,128)S(1)} %pad_add_fusion.3.refs_0_, f32[768,2048]{1,0:T(8,128)S(1)} %copy-done.7, f32[384,128]{1,0:T(8,128)S(1)} %copy-done.13, f32[192,128]{1,0:T(8,128)S(1)} %copy-done.15, ...), custom_call_target="tpu_custom_call" | custom-call | tf_op jit(solution)/shard_map/slopes_of/pallas_call | solution.py:210
  192.2 12.0 %input_grad.3 = bf16[192,4096]{1,0:T(8,128)(2,1)} custom-call(bf16[192,2048]{1,0:T(8,128)(2,1)S(1)} %get-tuple-element.106.slopes_ref, bf16[4096,2048]{1,0:T(8,128)(2,1)} %get-tuple-element.92.head_ref), custom_call_target="tpu_custom_call" | custom-call | tf_op jit(solution)/shard_map/input_grad/pallas_call | solution.py:232
  206.7 3.1 %collective-permute-start.24 = (bf16[512,1024]{1,0:T(8,128)(2,1)S(1)}, bf16[512,1024]{1,0:T(8,128)(2,1)S(1)}, u32[]{:S(2)}, u32[]{:S(2)}) collective-permute-start(bf16[512,1024]{1,0:T(8,128)(2,1)S(1)} %get-tuple-element.111), channel_id=1, source_target_pairs={{0,12},{1,13},{2,14},{3,15},{4,0},{5,1},{6,2},{7,3},{8,4},{9,5},{1... | collective-permute-start | bytes 3145736 | tf_op jit(solution)/shard_map/ppermute | solution.py:27
  214.1 8.7 %collective-permute-done.23 = bf16[512,1024]{1,0:T(8,128)(2,1)S(1)} collective-permute-done((bf16[512,1024]{1,0:T(8,128)(2,1)S(1)}, bf16[512,1024]{1,0:T(8,128)(2,1)S(1)}, u32[]{:S(2)}, u32[]{:S(2)}) %collective-permute-start.23) | collective-permute-done | bytes 1048608 | tf_op jit(solution)/shard_map/ppermute | solution.py:27
  226.5 3.2 %collective-permute-start.28 = (bf16[128,1024]{1,0:T(8,128)(2,1)S(1)}, bf16[128,1024]{1,0:T(8,128)(2,1)S(1)}, u32[]{:S(2)}, u32[]{:S(2)}) collective-permute-start(bf16[128,1024]{1,0:T(8,128)(2,1)S(1)} %get-tuple-element.132), channel_id=1, source_target_pairs={{0,3},{1,0},{2,1},{3,2},{4,7},{5,4},{6,5},{7,6},{8,11},{9,8},{10,9... | collective-permute-start | bytes 786440 | tf_op jit(solution)/shard_map/ppermute | solution.py:27
  230.0 4.1 %collective-permute-done.27 = bf16[128,1024]{1,0:T(8,128)(2,1)S(1)} collective-permute-done((bf16[128,1024]{1,0:T(8,128)(2,1)S(1)}, bf16[128,1024]{1,0:T(8,128)(2,1)S(1)}, u32[]{:S(2)}, u32[]{:S(2)}) %collective-permute-start.27) | collective-permute-done | bytes 262176 | tf_op jit(solution)/shard_map/ppermute | solution.py:27
  234.0 3.2 %collective-permute-done.29 = bf16[128,1024]{1,0:T(8,128)(2,1)S(1)} collective-permute-done((bf16[128,1024]{1,0:T(8,128)(2,1)S(1)}, bf16[128,1024]{1,0:T(8,128)(2,1)S(1)}, u32[]{:S(2)}, u32[]{:S(2)}) %collective-permute-start.29) | collective-permute-done | bytes 262176 | tf_op jit(solution)/shard_map/ppermute | solution.py:27
  239.7 4.1 %collective-permute-done.32 = bf16[128,1024]{1,0:T(8,128)(2,1)S(1)} collective-permute-done((bf16[128,1024]{1,0:T(8,128)(2,1)S(1)}, bf16[128,1024]{1,0:T(8,128)(2,1)S(1)}, u32[]{:S(2)}, u32[]{:S(2)}) %collective-permute-start.32) | collective-permute-done | bytes 262176 | tf_op jit(solution)/shard_map/ppermute | solution.py:27
  249.3 4.1 %collective-permute-done.33 = bf16[256,256]{1,0:T(8,128)(2,1)S(1)} collective-permute-done((bf16[256,256]{1,0:T(8,128)(2,1)S(1)}, bf16[256,256]{1,0:T(8,128)(2,1)S(1)}, u32[]{:S(2)}, u32[]{:S(2)}) %collective-permute-start.33) | collective-permute-done | bytes 131104 | tf_op jit(solution)/shard_map/ppermute | solution.py:316
  (158 shorter events, 92.3 us)
Async XLA Ops:
  1.9 15.8 %collective-permute-start.1 = (bf16[256,1024]{1,0:T(8,128)(2,1)S(1)}, bf16[256,1024]{1,0:T(8,128)(2,1)}, u32[]{:S(2)}, u32[]{:S(2)}) collective-permute-start(bf16[256,1024]{1,0:T(8,128)(2,1)S(1)} %constant_dynamic-slice_fusion), channel_id=1, source_target_pairs={{0,4},{1,5},{2,6},{3,7},{4,8},{5,9},{6,10},{7,11},{8,12},{9,13},{1... | collective-permute-start | bytes 1572872 | tf_op jit(solution)/shard_map/ppermute | solution.py:27
  3.6 14.0 %collective-permute-start.2 = (bf16[256,1024]{1,0:T(8,128)(2,1)S(1)}, bf16[256,1024]{1,0:T(8,128)(2,1)S(1)}, u32[]{:S(2)}, u32[]{:S(2)}) collective-permute-start(bf16[256,1024]{1,0:T(8,128)(2,1)S(1)} %constant_dynamic-slice_fusion), channel_id=1, source_target_pairs={{0,12},{1,13},{2,14},{3,15},{4,0},{5,1},{6,2},{7,3},{8,4},{9,5},{1... | collective-permute-start | bytes 1572872 | tf_op jit(solution)/shard_map/ppermute | solution.py:27
  20.0 20.6 %collective-permute-start.3 = (bf16[512,1024]{1,0:T(8,128)(2,1)}, bf16[512,1024]{1,0:T(8,128)(2,1)}, u32[]{:S(2)}, u32[]{:S(2)}) collective-permute-start(bf16[512,1024]{1,0:T(8,128)(2,1)} %pad_maximum_fusion.2.refs_3_), channel_id=1, source_target_pairs={{0,1},{1,2},{2,3},{3,0},{4,5},{5,6},{6,7},{7,4},{8,9},{9,10},{10,1... | collective-permute-start | bytes 3145736 | tf_op jit(solution)/shard_map/ppermute | solution.py:27
  22.0 18.6 %collective-permute-start.4 = (bf16[512,1024]{1,0:T(8,128)(2,1)}, bf16[512,1024]{1,0:T(8,128)(2,1)}, u32[]{:S(2)}, u32[]{:S(2)}) collective-permute-start(bf16[512,1024]{1,0:T(8,128)(2,1)} %pad_maximum_fusion.2.refs_3_), channel_id=1, source_target_pairs={{0,3},{1,0},{2,1},{3,2},{4,7},{5,4},{6,5},{7,6},{8,11},{9,8},{10,9... | collective-permute-start | bytes 3145736 | tf_op jit(solution)/shard_map/ppermute | solution.py:27
  26.9 45.0 %collective-permute-start = (bf16[384,4096]{0,1:T(8,128)(2,1)}, bf16[384,4096]{0,1:T(8,128)(2,1)}, u32[]{:S(2)}, u32[]{:S(2)}) collective-permute-start(bf16[384,4096]{0,1:T(8,128)(2,1)} %pad_maximum_fusion.1), channel_id=1, source_target_pairs={{0,16},{16,0},{1,17},{17,1},{2,18},{18,2},{3,19},{19,3},{4,20},{20... | collective-permute-start | bytes 9437192 | tf_op jit(solution)/shard_map/ppermute | solution.py:31
  26.9 42.8 %all-to-all-start = ((bf16[8,48,4096]{2,1,0:T(8,128)(2,1)}), bf16[8,48,4096]{2,1,0:T(8,128)(2,1)S(1)}, u32[]{:S(2)}, u32[]{:S(2)}) async-start(bf16[8,48,4096]{2,1,0:T(8,128)(2,1)} %bitcast.78), calls=%async_computation | async-start | bytes 6291456 | tf_op jit(solution)/shard_map/all_to_all | solution.py:356
  42.0 16.3 %collective-permute-start.7 = (bf16[512,1024]{1,0:T(8,128)(2,1)}, bf16[512,1024]{1,0:T(8,128)(2,1)}, u32[]{:S(2)}, u32[]{:S(2)}) collective-permute-start(bf16[512,1024]{1,0:T(8,128)(2,1)} %constant_dynamic-update-slice_fusion.refs_4_), channel_id=1, source_target_pairs={{0,1},{1,2},{2,3},{3,0},{4,5},{5,6},{6,7},{7,4},{8,9},{9,10},{10,1... | collective-permute-start | bytes 3145736 | tf_op jit(solution)/shard_map/ppermute | solution.py:27
  42.0 17.9 %collective-permute-start.8 = (bf16[512,1024]{1,0:T(8,128)(2,1)}, bf16[512,1024]{1,0:T(8,128)(2,1)}, u32[]{:S(2)}, u32[]{:S(2)}) collective-permute-start(bf16[512,1024]{1,0:T(8,128)(2,1)} %constant_dynamic-update-slice_fusion.refs_4_), channel_id=1, source_target_pairs={{0,3},{1,0},{2,1},{3,2},{4,7},{5,4},{6,5},{7,6},{8,11},{9,8},{10,9... | collective-permute-start | bytes 3145736 | tf_op jit(solution)/shard_map/ppermute | solution.py:27
  45.2 24.5 %collective-permute-start.13 = (bf16[512,1024]{1,0:T(8,128)(2,1)}, bf16[512,1024]{1,0:T(8,128)(2,1)}, u32[]{:S(2)}, u32[]{:S(2)}) collective-permute-start(bf16[512,1024]{1,0:T(8,128)(2,1)} %pad_maximum_fusion.2.refs_3_), channel_id=1, source_target_pairs={{0,16},{16,0},{1,17},{17,1},{2,18},{18,2},{3,19},{19,3},{4,20},{20... | collective-permute-start | bytes 3145736 | tf_op jit(solution)/shard_map/ppermute | solution.py:31
  45.2 24.5 %collective-permute-start.14 = (bf16[512,1024]{1,0:T(8,128)(2,1)}, bf16[512,1024]{1,0:T(8,128)(2,1)}, u32[]{:S(2)}, u32[]{:S(2)}) collective-permute-start(bf16[512,1024]{1,0:T(8,128)(2,1)} %constant_dynamic-update-slice_fusion.refs_4_), channel_id=1, source_target_pairs={{0,16},{16,0},{1,17},{17,1},{2,18},{18,2},{3,19},{19,3},{4,20},{20... | collective-permute-start | bytes 3145736 | tf_op jit(solution)/shard_map/ppermute | solution.py:31
  58.3 13.5 %collective-permute-start.15 = (bf16[512,1024]{1,0:T(8,128)(2,1)}, bf16[512,1024]{1,0:T(8,128)(2,1)}, u32[]{:S(2)}, u32[]{:S(2)}) collective-permute-start(bf16[512,1024]{1,0:T(8,128)(2,1)} %collective-permute-done.3.refs_5_), channel_id=1, source_target_pairs={{0,16},{16,0},{1,17},{17,1},{2,18},{18,2},{3,19},{19,3},{4,20},{20... | collective-permute-start | bytes 3145736 | tf_op jit(solution)/shard_map/ppermute | solution.py:31
  59.9 36.9 %collective-permute-start.16 = (bf16[512,1024]{1,0:T(8,128)(2,1)}, bf16[512,1024]{1,0:T(8,128)(2,1)}, u32[]{:S(2)}, u32[]{:S(2)}) collective-permute-start(bf16[512,1024]{1,0:T(8,128)(2,1)} %collective-permute-done.4.refs_6_), channel_id=1, source_target_pairs={{0,16},{16,0},{1,17},{17,1},{2,18},{18,2},{3,19},{19,3},{4,20},{20... | collective-permute-start | bytes 3145736 | tf_op jit(solution)/shard_map/ppermute | solution.py:31
  69.7 42.4 %collective-permute-start.12 = (bf16[512,1024]{1,0:T(8,128)(2,1)}, bf16[512,1024]{1,0:T(8,128)(2,1)}, u32[]{:S(2)}, u32[]{:S(2)}) collective-permute-start(bf16[512,1024]{1,0:T(8,128)(2,1)} %collective-permute-done.8.refs_4_), channel_id=1, source_target_pairs={{0,16},{16,0},{1,17},{17,1},{2,18},{18,2},{3,19},{19,3},{4,20},{20... | collective-permute-start | bytes 3145736 | tf_op jit(solution)/shard_map/ppermute | solution.py:31
  69.8 52.9 %collective-permute-start.10 = (bf16[512,1024]{1,0:T(8,128)(2,1)}, bf16[512,1024]{1,0:T(8,128)(2,1)}, u32[]{:S(2)}, u32[]{:S(2)}) collective-permute-start(bf16[512,1024]{1,0:T(8,128)(2,1)} %collective-permute-done.8.refs_4_), channel_id=1, source_target_pairs={{0,3},{1,0},{2,1},{3,2},{4,7},{5,4},{6,5},{7,6},{8,11},{9,8},{10,9... | collective-permute-start | bytes 3145736 | tf_op jit(solution)/shard_map/ppermute | solution.py:27
  71.9 40.2 %collective-permute-start.11 = (bf16[512,1024]{1,0:T(8,128)(2,1)}, bf16[512,1024]{1,0:T(8,128)(2,1)}, u32[]{:S(2)}, u32[]{:S(2)}) collective-permute-start(bf16[512,1024]{1,0:T(8,128)(2,1)} %collective-permute-done.7.refs_3_), channel_id=1, source_target_pairs={{0,16},{16,0},{1,17},{17,1},{2,18},{18,2},{3,19},{19,3},{4,20},{20... | collective-permute-start | bytes 3145736 | tf_op jit(solution)/shard_map/ppermute | solution.py:31
  71.9 50.8 %collective-permute-start.9 = (bf16[512,1024]{1,0:T(8,128)(2,1)}, bf16[512,1024]{1,0:T(8,128)(2,1)}, u32[]{:S(2)}, u32[]{:S(2)}) collective-permute-start(bf16[512,1024]{1,0:T(8,128)(2,1)} %collective-permute-done.3.refs_5_), channel_id=1, source_target_pairs={{0,1},{1,2},{2,3},{3,0},{4,5},{5,6},{6,7},{7,4},{8,9},{9,10},{10,1... | collective-permute-start | bytes 3145736 | tf_op jit(solution)/shard_map/ppermute | solution.py:27
  145.9 26.1 %all-to-all-start.1 = ((bf16[8,48,2048]{2,1,0:T(8,128)(2,1)}), bf16[8,48,2048]{2,1,0:T(8,128)(2,1)}, u32[]{:S(2)}, u32[]{:S(2)}) async-start(bf16[8,48,2048]{2,1,0:T(8,128)(2,1)} %bitcast.77), calls=%async_computation.1 | async-start | bytes 3145728 | tf_op jit(solution)/shard_map/all_to_all | solution.py:388
  157.2 12.5 %collective-permute-start.19 = (bf16[192,1024]{1,0:T(8,128)(2,1)S(1)}, bf16[192,1024]{1,0:T(8,128)(2,1)}, u32[]{:S(2)}, u32[]{:S(2)}) collective-permute-start(bf16[192,1024]{1,0:T(8,128)(2,1)S(1)} %get-tuple-element.93), channel_id=1, source_target_pairs={{0,16},{16,0},{1,17},{17,1},{2,18},{18,2},{3,19},{19,3},{4,20},{20... | collective-permute-start | bytes 1179656 | tf_op jit(solution)/shard_map/ppermute | solution.py:31
  184.3 19.9 %collective-permute-start.21 = (bf16[512,1024]{1,0:T(8,128)(2,1)S(1)}, bf16[512,1024]{1,0:T(8,128)(2,1)S(1)}, u32[]{:S(2)}, u32[]{:S(2)}) collective-permute-start(bf16[512,1024]{1,0:T(8,128)(2,1)S(1)} %get-tuple-element.101), channel_id=1, source_target_pairs={{0,4},{1,5},{2,6},{3,7},{4,8},{5,9},{6,10},{7,11},{8,12},{9,13},{1... | collective-permute-start | bytes 3145736 | tf_op jit(solution)/shard_map/ppermute | solution.py:27
  185.7 18.5 %collective-permute-start.22 = (bf16[512,1024]{1,0:T(8,128)(2,1)S(1)}, bf16[512,1024]{1,0:T(8,128)(2,1)S(1)}, u32[]{:S(2)}, u32[]{:S(2)}) collective-permute-start(bf16[512,1024]{1,0:T(8,128)(2,1)S(1)} %get-tuple-element.102), channel_id=1, source_target_pairs={{0,12},{1,13},{2,14},{3,15},{4,0},{5,1},{6,2},{7,3},{8,4},{9,5},{1... | collective-permute-start | bytes 3145736 | tf_op jit(solution)/shard_map/ppermute | solution.py:27
  190.1 21.6 %collective-permute-start.25 = (bf16[512,1024]{1,0:T(8,128)(2,1)S(1)}, bf16[512,1024]{1,0:T(8,128)(2,1)S(1)}, u32[]{:S(2)}, u32[]{:S(2)}) collective-permute-start(bf16[512,1024]{1,0:T(8,128)(2,1)S(1)} %get-tuple-element.112), channel_id=1, source_target_pairs={{0,12},{1,13},{2,14},{3,15},{4,0},{5,1},{6,2},{7,3},{8,4},{9,5},{1... | collective-permute-start | bytes 3145736 | tf_op jit(solution)/shard_map/ppermute | solution.py:27
  191.6 20.1 %collective-permute-start.26 = (bf16[512,1024]{1,0:T(8,128)(2,1)S(1)}, bf16[512,1024]{1,0:T(8,128)(2,1)S(1)}, u32[]{:S(2)}, u32[]{:S(2)}) collective-permute-start(bf16[512,1024]{1,0:T(8,128)(2,1)S(1)} %get-tuple-element.113), channel_id=1, source_target_pairs={{0,4},{1,5},{2,6},{3,7},{4,8},{5,9},{6,10},{7,11},{8,12},{9,13},{1... | collective-permute-start | bytes 3145736 | tf_op jit(solution)/shard_map/ppermute | solution.py:27
  206.5 16.3 %collective-permute-start.23 = (bf16[512,1024]{1,0:T(8,128)(2,1)S(1)}, bf16[512,1024]{1,0:T(8,128)(2,1)S(1)}, u32[]{:S(2)}, u32[]{:S(2)}) collective-permute-start(bf16[512,1024]{1,0:T(8,128)(2,1)S(1)} %get-tuple-element.110), channel_id=1, source_target_pairs={{0,4},{1,5},{2,6},{3,7},{4,8},{5,9},{6,10},{7,11},{8,12},{9,13},{1... | collective-permute-start | bytes 3145736 | tf_op jit(solution)/shard_map/ppermute | solution.py:27
  206.7 16.2 %collective-permute-start.24 = (bf16[512,1024]{1,0:T(8,128)(2,1)S(1)}, bf16[512,1024]{1,0:T(8,128)(2,1)S(1)}, u32[]{:S(2)}, u32[]{:S(2)}) collective-permute-start(bf16[512,1024]{1,0:T(8,128)(2,1)S(1)} %get-tuple-element.111), channel_id=1, source_target_pairs={{0,12},{1,13},{2,14},{3,15},{4,0},{5,1},{6,2},{7,3},{8,4},{9,5},{1... | collective-permute-start | bytes 3145736 | tf_op jit(solution)/shard_map/ppermute | solution.py:27
  (40 other events, 268.4 us)

commit v4 on v3

--- a/solution.py
+++ b/solution.py
@@ -42,17 +42,46 @@
     return lax.optimization_barrier(values)
 
 
-def project_kernel(count, kind, at_ref, own_ref, arrived_ref, *refs):
-    pieces, rest = refs[:count], refs[count:]
-    if kind == "first":
-        head_ref, pre_ref, states, stored = rest
-    elif kind == "middle":
-        base_ref, _, head_ref, pre_ref, states, stored = rest
-    else:
-        base_ref, counts_ref, _, head_ref, pre_ref, *outs, states, stored = rest
+def turn_kernel(*refs):
+    turned_ref = refs[-1]
+    rows = refs[0].shape[0]
+
+    def block(k, _):
+        at = pl.ds(pl.multiple_of(k * BLOCK, BLOCK), BLOCK)
+        part = jnp.concatenate([ref[:, at] for ref in refs[:-1]], axis=0)
+        turned_ref[at, :] = part.T
+        return 0
+
+    lax.fori_loop(0, refs[0].shape[1] // BLOCK, block, 0)
+
+
+def turn(*states):
+    rows, depth = states[0].shape
+    return pl.pallas_call(
+        turn_kernel,
+        in_specs=vmem(len(states)),
+        out_specs=vmem(1)[0],
+        out_shape=jax.ShapeDtypeStruct((depth, rows * len(states)), BF16),
+        compiler_params=pltpu.CompilerParams(vmem_limit_bytes=20 * 1024 * 1024),
+        name="turn",
+    )(*states)
+
+
+def project_kernel(xs, count, store_all, bases, finish, at_ref, *refs):
+    x_refs, refs = refs[:xs], refs[xs:]
+    pieces, refs = refs[:count], refs[count:]
+    base_refs, refs = refs[:bases], refs[bases:]
+    if finish:
+        counts_ref, refs = refs[0], refs[1:]
+    if store_all:
+        if bases:
+            refs = refs[1:]
+        head_ref, refs = refs[0], refs[1:]
+    outs = max(bases, 1)
+    pre_refs, refs = refs[:outs], refs[outs:]
+    states, stored = refs[-2:]
     half = count // 2
     blocks = 2 * half
-    rows = arrived_ref.shape[0]
     width = 1024
 
     def store(k):
@@ -64,13 +93,16 @@
             stored.at[k],
         )
 
-    for k in range(2 * blocks):
-        store(k).start()
+    if store_all:
+        for k in range(2 * blocks):
+            store(k).start()
     for side in range(2):
         for k in range(blocks):
             col = pl.multiple_of(at_ref[0, side * blocks + k] * BLOCK, BLOCK)
-            states[pl.ds(0, rows), pl.ds(k * BLOCK, BLOCK)] = own_ref[pl.ds(0, rows), pl.ds(col, BLOCK)]
-            states[pl.ds(rows, rows), pl.ds(k * BLOCK, BLOCK)] = arrived_ref[:, pl.ds(col, BLOCK)]
+            row = 0
+            for ref in x_refs:
+                states[pl.ds(row, ref.shape[0]), pl.ds(k * BLOCK, BLOCK)] = ref[:, pl.ds(col, BLOCK)]
+                row += ref.shape[0]
 
         def strip(n, _, side=side):
             at_col = pl.multiple_of(n * BLOCK, BLOCK)
@@ -83,19 +115,25 @@
                     preferred_element_type=F32,
                 )
                 total = product if total is None else total + product
-            if kind != "first":
-                total = total + base_ref[:, pl.ds(out_col, BLOCK)]
-            pre_ref[:, pl.ds(out_col, BLOCK)] = total
+            row = 0
+            for i, pre_ref in enumerate(pre_refs):
+                rows = pre_ref.shape[0]
+                part = total[row : row + rows]
+                if bases:
+                    part = part + base_refs[i][:, pl.ds(out_col, BLOCK)]
+                pre_ref[:, pl.ds(out_col, BLOCK)] = part
+                row += rows
             return 0
 
         lax.fori_loop(0, width // BLOCK, strip, 0)
-    if kind == "last":
-        contrast(counts_ref, pre_ref, *outs)
-    for k in range(2 * blocks):
-        store(k).wait()
-
-
-def contrast(counts_ref, pre_ref, inverse_ref, emb_ref, mixing_ref, first_ref, grad_ref):
+    if finish:
+        contrast(counts_ref, *pre_refs, *refs[:-2])
+    if store_all:
+        for k in range(2 * blocks):
+            store(k).wait()
+
+
+def contrast(counts_ref, pre_ref, arrived_ref, inverse_ref, emb_ref, mixing_ref, first_ref, grad_ref):
     rows = counts_ref.shape[0]
     width = pre_ref.shape[1]
     scale = 16.0 / width
@@ -103,17 +141,17 @@
 
     def normalize(i, _):
         at = pl.ds(pl.multiple_of(i * chunk, chunk), chunk)
+        after = pl.ds(pl.multiple_of(2 * rows + i * chunk, chunk), chunk)
         values = pre_ref[at, :]
         inverse = lax.rsqrt(jnp.mean(values * values, axis=-1, keepdims=True) + EPSILON)
         emb_ref[at, :] = (values * inverse).astype(BF16)
-
-        @pl.when(i < 2 * rows // chunk)
-        def _():
-            inverse_ref[at, :] = jnp.broadcast_to(inverse, (chunk, 128))
-
+        inverse_ref[at, :] = jnp.broadcast_to(inverse, (chunk, 128))
+        values = arrived_ref[at, :]
+        inverse = lax.rsqrt(jnp.mean(values * values, axis=-1, keepdims=True) + EPSILON)
+        emb_ref[after, :] = (values * inverse).astype(BF16)
         return 0
 
-    lax.fori_loop(0, pre_ref.shape[0] // chunk, normalize, 0)
+    lax.fori_loop(0, 2 * rows // chunk, normalize, 0)
     query = emb_ref[pl.ds(0, rows), :]
     passage = emb_ref[pl.ds(rows, rows), :]
     fetched = emb_ref[pl.ds(2 * rows, 2 * rows), :]
@@ -139,44 +177,52 @@
     return [pl.BlockSpec(memory_space=pltpu.VMEM)] * count
 
 
-def project(kind, at, both_states, arrived, pieces, *more):
+def near(shape, dtype):
+    return pltpu.VMEM(shape, dtype)
+
+
+def keep_near(*values):
+    return [pltpu.with_memory_space_constraint(value, pltpu.VMEM) for value in values]
+
+
+def project(at, xs, pieces, bases=(), head=None, store=True, counts=None):
     count = len(pieces)
-    rows = arrived.shape[0]
-    half = rows // 2
+    sizes = [base.shape[0] for base in bases] or [sum(x.shape[0] for x in xs)]
+    finish = counts is not None
     anywhere = pl.BlockSpec(memory_space=pl.ANY)
-    ins = [pl.BlockSpec(memory_space=pltpu.SMEM)] + vmem(2 + count)
-    outs = [anywhere] + vmem(1)
-    types = [
-        jax.ShapeDtypeStruct((4096, 2048), BF16),
-        jax.ShapeDtypeStruct((2 * rows, 2048), F32),
-    ]
-    aliases = {}
-    if kind != "first":
-        ins += vmem(1 if kind == "middle" else 2) + [anywhere]
-        aliases = {3 + count: 1, len(ins) - 1: 0}
-    if kind == "last":
+    ins = [pl.BlockSpec(memory_space=pltpu.SMEM)] + vmem(len(xs) + count + len(bases) + finish)
+    args = [at, *xs, *pieces, *keep_near(*bases)] + ([counts] if finish else [])
+    aliases = {1 + len(xs) + count + i: int(store) + i for i in range(len(bases))}
+    outs, types = vmem(len(sizes)), [near((size, 2048), F32) for size in sizes]
+    if store:
+        outs, types = [anywhere] + outs, [jax.ShapeDtypeStruct((4096, 2048), BF16)] + types
+        if bases:
+            aliases[len(args)] = 0
+            args.append(head)
+            ins.append(anywhere)
+    if finish:
+        rows = sizes[0]
         outs += vmem(5)
-        for shape, dtype in (
-            ((rows, 128), F32),
-            ((2 * rows, 2048), BF16),
-            ((half, rows), BF16),
-            ((half, 128), F32),
-            ((rows, 2048), BF16),
-        ):
-            types.append(jax.ShapeDtypeStruct(shape, dtype))
+        types += [
+            near((rows, 128), F32),
+            near((2 * rows, 2048), BF16),
+            near((rows // 2, rows), BF16),
+            near((rows // 2, 128), F32),
+            jax.ShapeDtypeStruct((rows, 2048), BF16),
+        ]
     return pl.pallas_call(
-        lambda *refs: project_kernel(count, kind, *refs),
+        lambda *refs: project_kernel(len(xs), count, store, len(bases), finish, *refs),
         in_specs=ins,
         out_specs=outs,
         out_shape=types,
         scratch_shapes=[
-            pltpu.VMEM((2 * rows, count // 2 * 512), BF16),
+            pltpu.VMEM((sum(sizes), count // 2 * 512), BF16),
             pltpu.SemaphoreType.DMA((2 * count,)),
         ],
         input_output_aliases=aliases,
-        compiler_params=pltpu.CompilerParams(vmem_limit_bytes=28 * 1024 * 1024),
-        name="project_" + kind,
-    )(at, both_states, arrived, *pieces, *more)
+        compiler_params=pltpu.CompilerParams(vmem_limit_bytes=24 * 1024 * 1024),
+        name="project",
+    )(*args)
 
 
 def slopes_kernel(part, cols_ref, pre_ref, inverse_ref, first_ref, emb_ref, left_ref, right_ref, out_ref, keep_ref, send_ref, grad_ref):
@@ -219,28 +265,32 @@
         scratch_shapes=[pltpu.VMEM((rows, width), F32)],
         compiler_params=pltpu.CompilerParams(vmem_limit_bytes=16 * 1024 * 1024),
         name="slopes_of",
-    )(cols, pre, inverse, first, emb, left, right)
-
-
-def input_grad_kernel(slopes_ref, head_ref, out_ref):
-    out_ref[...] = dot(slopes_ref[...], head_ref[...], ((1,), (1,))).astype(BF16)
-
-
-def input_grad(slopes, head):
+    )(cols, *keep_near(pre, inverse, first, emb), left, right)
+
+
+def input_grad_kernel(slopes_ref, head_ref, *refs):
+    refs[-1][...] = dot(slopes_ref[...], head_ref[...], ((1,), (1,))).astype(BF16)
+
+
+def input_grad(slopes, head, part, filled=None):
     rows, width = slopes.shape
     depth = head.shape[0]
+    steps = depth // 512 // 2
+    more = [] if filled is None else [filled]
     return pl.pallas_call(
         input_grad_kernel,
-        grid=(depth // 512,),
+        grid=(steps,),
         in_specs=[
             pl.BlockSpec((rows, width), lambda k: (0, 0)),
-            pl.BlockSpec((512, width), lambda k: (k, 0)),
-        ],
-        out_specs=pl.BlockSpec((rows, 512), lambda k: (0, k)),
+            pl.BlockSpec((512, width), lambda k: (k + part * steps, 0)),
+        ]
+        + [pl.BlockSpec(memory_space=pl.ANY)] * len(more),
+        out_specs=pl.BlockSpec((rows, 512), lambda k: (0, k + part * steps)),
         out_shape=jax.ShapeDtypeStruct((rows, depth), BF16),
+        input_output_aliases={2: 0} if more else {},
         compiler_params=pltpu.CompilerParams(vmem_limit_bytes=16 * 1024 * 1024),
         name="input_grad",
-    )(slopes, pltpu.with_memory_space_constraint(head, pltpu.HBM))
+    )(slopes, pltpu.with_memory_space_constraint(head, pltpu.HBM), *more)
 
 
 def partial_kernel(outs, adds, at_ref, states_ref, slopes_ref, *refs):
@@ -274,7 +324,7 @@
     return total.astype(BF16)
 
 
-def scatter_head(states, slopes, core, beside, given):
+def scatter_head(states, slopes, core, head, passage_dy):
     def part(d1s, d2s, adds):
         at = [block_at(core, d1, d2) for d1, some in zip(d1s, d2s) for d2 in some]
         return head_partial(states, slopes, jnp.stack(at).astype(jnp.int32), adds)
@@ -283,14 +333,16 @@
     far_a, far_b = part((2, 2), (a, b), ((), ()))
     far_a, far_b = shift(far_a, 1, 1), shift(far_b, 1, -1)
     up_b, down_a = part((1, -1), (b, a), ((), ()))
-    up_b, down_a, given = together(up_b, down_a, given)
+    up_b, down_a, passage_dy = together(up_b, down_a, passage_dy)
     up_b, down_a = shift(up_b, 1, 1), shift(down_a, 1, -1)
-    extra = beside(given)
+    extra = input_grad(passage_dy, head, 0)
     far_a, far_b, extra = together(far_a, far_b, extra)
     up_a, down_b = part((1, -1), (a, b), ((far_a,), (far_b,)))
     up_a, down_b = shift(up_a, 1, 1), shift(down_b, 1, -1)
     mine_a, mine_b = part((0, 0), (a, b), ((down_a,), (up_b,)))
-    up_a, down_b, mine_a, mine_b = together(up_a, down_b, mine_a, mine_b)
+    mine_a, mine_b, passage_dy = together(mine_a, mine_b, passage_dy)
+    extra = input_grad(passage_dy, head, 1, extra)
+    up_a, down_b, mine_a, mine_b, extra = together(up_a, down_b, mine_a, mine_b, extra)
     half = BLOCK // 2
     far, up = mine_a[:BLOCK], mine_a[BLOCK:]
     down, mine = mine_b[:BLOCK], mine_b[BLOCK:]
@@ -346,7 +398,6 @@
         return jnp.stack([jnp.stack(at), jnp.stack(side)]).astype(jnp.int32)
 
     a, b = (0, -1), (1, 2)
-    states = jnp.concatenate([queries, passages], axis=0)
     owner = (flat_lists[None, :] == jnp.arange(rows_dev, dtype=jnp.int32)[:, None]).astype(BF16)
     own = lax.dynamic_slice_in_dim(head_weight, core * (width // 2), width // 2, axis=1)
 
@@ -360,30 +411,37 @@
     first_up, first_down = shift(first, 2, 1), shift(first, 2, -1)
     half = BLOCK // 2
     far_a, far_b = shift(up[:half], 1, 1), shift(down[half:], 1, -1)
-    first_up, first_down, far_a, far_b = together(first_up, first_down, far_a, far_b)
+    slot_ids = jnp.arange(slot_count, dtype=jnp.int32)[None, :]
+    counts = jnp.zeros((rows_dev, slot_count), F32)
+    for j in range(neg_slots.shape[1]):
+        counts = counts + (neg_slots[:, j : j + 1] == slot_ids).astype(F32)
+    first_up, first_down, far_a, far_b, counts = together(first_up, first_down, far_a, far_b, counts)
 
     second = jnp.concatenate([down, far_a, far_b], axis=0)
     second_up, second_down = shift(second, 2, 1), shift(second, 2, -1)
     early = [first, second, first_up, first_down]
     early = early + [swap(piece) for piece in early]
-    both_states = jnp.concatenate([states, swap(states)], axis=0)
-    turned = both_states.T
-    slot_ids = jnp.arange(slot_count, dtype=jnp.int32)[None, :]
-    counts = jnp.zeros((rows_dev, slot_count), F32)
-    for j in range(neg_slots.shape[1]):
-        counts = counts + (neg_slots[:, j : j + 1] == slot_ids).astype(F32)
-    second_up, second_down, arrived, first_up = together(second_up, second_down, arrived, first_up)
+    early_at = places_of((a, 0), (b, 0), (a, -1), (a, 1))
+    head, pre = project(early_at, (queries, passages), early)
+    second_up, second_down, first_up, pre = together(second_up, second_down, first_up, pre)
 
     first_far, second_far = shift(first_up, 2, 1), shift(second_down, 2, -1)
-    head, pre = project(
-        "first", places_of((a, 0), (b, 0), (a, -1), (a, 1)), both_states, arrived, early
-    )
+    turned = turn(queries, passages, swap(queries), swap(passages))
     middle = [second_up, second_down, swap(second_up), swap(second_down)]
-    head, pre = project("middle", places_of((b, -1), (b, 1)), both_states, arrived, middle, pre, head)
-    first_far, second_far, pre, counts, turned = together(first_far, second_far, pre, counts, turned)
+    middle_at = places_of((b, -1), (b, 1))
+    head, pre = project(middle_at, (queries, passages), middle, (pre,), head)
+    pre, arrived = together(pre, arrived)
+    joined = early[:4] + middle[:2] + early[4:] + middle[2:]
+    joined_at = places_of((a, 0), (b, 0), (a, -1), (a, 1), (b, -1), (b, 1))
+    (arrived_pre,) = project(joined_at, (arrived,), joined, store=False)
     late = [first_far, second_far, swap(first_far), swap(second_far)]
-    head, pre, inverse, emb, mixing, first, fetched_grad = project(
-        "last", places_of((a, 2), (b, 2)), both_states, arrived, late, pre, counts, head
+    head, pre, _, inverse, emb, mixing, first, fetched_grad = project(
+        places_of((a, 2), (b, 2)),
+        (queries, passages, arrived),
+        late,
+        (pre, arrived_pre),
+        head,
+        counts=counts,
     )
     returned = lax.all_to_all(
         fetched_grad.reshape(groups, capacity, width),
@@ -399,7 +457,7 @@
     ).astype(jnp.int32)
     query_dy, query_keep, query_send = slopes_of(0, cols, pre, inverse, first, emb, mixing, emb)
     query_other = swap(query_send)
-    query_grads = input_grad(query_dy, head)
+    query_grads = input_grad(query_dy, head, 1, input_grad(query_dy, head, 0))
     returned, query_grads, query_other = lax.optimization_barrier((returned, query_grads, query_other))
 
     passage_dy, passage_keep, passage_send = slopes_of(
@@ -408,7 +466,7 @@
     passage_other = swap(passage_send)
     slopes = jnp.concatenate([query_keep, passage_keep, query_other, passage_other], axis=0)
     head_grads, passage_grads = scatter_head(
-        turned, slopes, core, lambda slopes: input_grad(slopes, head), passage_dy
+        turned, slopes, core, head, passage_dy
     )
     return (query_grads, passage_grads, head_grads)
 

time: 256 us -> 245 us (0.957)
  other arithmetic: 23.7 us -> 2.79 us
  Pallas kernels: 72.4 us -> 85.6 us
  waiting for transfers between devices: 59.4 us -> 54.4 us
    pallas_call x5 -> x9, Pallas kernels: 56.3 us -> 69.4 us  [the longest x4 37.7 us: project(): pl.pallas_call(lambda *refs: project_kernel(len(xs), count, store, len(ba...]
    concatenate x2 -> x0, other arithmetic: 10.6 us -> none  [the longest x1 7.8 us: per_device(): both_states = jnp.concatenate([states, swap(states)], axis=0)]
    unnamed x59 -> x77, local copies, waits for them, and re-layouts: 32.3 us -> 42.3 us
    ppermute x22, waiting for transfers between devices: 38.4 us -> 48.3 us  [shift(): return lax.ppermute(value, ('c', 'y', 'z'), pairs)]
    all_to_all x1, waiting for transfers between devices: 9.28 us -> 0.01 us  [per_device(): lax.all_to_all(picked, ('x', 'c'), split_axis=0, concat_axis=0, tiled=True)]
    concatenate x1 -> x0, local copies, waits for them, and re-layouts: 8.71 us -> none  [per_device(): both_states = jnp.concatenate([states, swap(states)], axis=0)]
    transpose x1 -> x0, other arithmetic: 8.09 us -> none  [per_device(): turned = both_states.T]
    ppermute x11 -> x12, waiting for transfers between devices: 4.41 us -> 0.03 us  [swap(): return lax.ppermute(value, 'c', SWAP)]
  transfers between devices with their start and end apart: 38 -> 39, of which waited for: 18 -> 19; matrix products, arithmetic and copies ran while one was open for 19% -> 4% of each run, Pallas kernels for 21% -> 34%
where the time goes in v4:
time: 245 us; the launch traced here: 244 us
  Pallas kernels  85.6 us (35%)
  waiting for transfers between devices  54.4 us (22%)
  starting transfers between devices  50.8 us (21%)
  local copies, waits for them, and re-layouts  44.5 us (18%)
  matrix products  4.11 us (2%)
  other arithmetic  2.79 us (1%)
    ppermute x22, waiting for transfers between devices, shift(): return lax.ppermute(value, ('c', 'y', 'z'), pairs)  48.3 us
    unnamed x77, local copies, waits for them, and re-layouts  42.3 us
    pallas_call x4, Pallas kernels, project(): pl.pallas_call(lambda *refs: project_kernel(len(xs), count, store, len(ba...  37.7 us
    ppermute x22, starting transfers between devices, shift(): return lax.ppermute(value, ('c', 'y', 'z'), pairs)  34.7 us
    pallas_call x4, Pallas kernels, input_grad(): pl.pallas_call(input_grad_kernel, grid=(steps,), in_specs=[pl.BlockSpec((...  26.8 us
    pallas_call x4, Pallas kernels, head_partial(): pl.pallas_call(lambda *refs: partial_kernel(outs, len(adds[0]), *refs), i...  9.56 us
    pallas_call x2, Pallas kernels, slopes_of(): pl.pallas_call(lambda *refs: slopes_kernel(part, *refs), in_specs=[pl.Blo...  6.66 us
    pallas_call x1, Pallas kernels, turn(): pl.pallas_call(turn_kernel, in_specs=vmem(len(states)), out_specs=vmem(1)...  4.91 us
  transfers between devices with their start and end apart: 39, of which 19 were waited for; matrix products, arithmetic and copies ran while one was open for 4% of the time, Pallas kernels for 34%

profile of v4, /device:TPU:0, one launch (start us, length us, event | category | flops | bytes accessed | tf_op | source)
XLA Modules:
  0.0 244.2 jit_solution(12469877115254226598)
XLA Ops:
  6.0 4.1 %convolution_convert_fusion = bf16[384,4096]{1,0:T(8,128)(2,1)} fusion(bf16[192,4096]{1,0:T(8,128)(2,1)} %refs_1_.7, s32[384]{0:T(512)S(1)} %eq.554), kind=kOutput, calls=%fused_computation | convolution fusion | flops 605626368 | bytes 4720128 | tf_op jit(solution)/shard_map/dot_general | solution.py:383
  21.9 5.8 %collective-permute-done.4 = bf16[128,1024]{1,0:T(8,128)(2,1)S(1)} collective-permute-done((bf16[128,1024]{1,0:T(8,128)(2,1)S(1)}, bf16[128,1024]{1,0:T(8,128)(2,1)S(1)}, u32[]{:S(2)}, u32[]{:S(2)}) %collective-permute-start.4) | collective-permute-done | bytes 262176 | tf_op jit(solution)/shard_map/ppermute | solution.py:27
  28.1 4.5 %collective-permute-done.2.refs_5_.refs_4_ = bf16[512,1024]{1,0:T(8,128)(2,1)S(1)} collective-permute-done((bf16[512,1024]{1,0:T(8,128)(2,1)S(1)}, bf16[512,1024]{1,0:T(8,128)(2,1)S(1)}, u32[]{:S(2)}, u32[]{:S(2)}) %collective-permute-start.2) | collective-permute-done | bytes 1048608 | tf_op jit(solution)/shard_map/ppermute | solution.py:27
  38.9 4.4 %all-to-all-start = ((bf16[8,48,4096]{2,1,0:T(8,128)(2,1)}), bf16[8,48,4096]{2,1,0:T(8,128)(2,1)}, u32[]{:S(2)}, u32[]{:S(2)}) async-start(bf16[8,48,4096]{2,1,0:T(8,128)(2,1)} %bitcast.73), calls=%async_computation | async-start | bytes 6291456 | tf_op jit(solution)/shard_map/all_to_all | solution.py:407
  52.7 7.7 %project.4 = (bf16[4096,2048]{1,0:T(8,128)(2,1)}, f32[384,2048]{1,0:T(8,128)S(1)}) custom-call(s32[2,16]{1,0:T(2,128)S(1)} %pad_add_fusion.2.refs_0_, bf16[192,4096]{1,0:T(8,128)(2,1)} %refs_0_.1, bf16[192,4096]{1,0:T(8,128)(2,1)S(1)} %copy-done.4, bf16[512,1024]{1,0:T(8,128)(2,1)S(1)} %copy-done.12, ...), custom_call_target="tpu_custom_call" | custom-call | tf_op jit(solution)/shard_map/project/pallas_call | solution.py:213
  64.3 12.4 %collective-permute-done.14.refs_4_ = bf16[512,1024]{1,0:T(8,128)(2,1)} collective-permute-done((bf16[512,1024]{1,0:T(8,128)(2,1)S(1)}, bf16[512,1024]{1,0:T(8,128)(2,1)}, u32[]{:S(2)}, u32[]{:S(2)}) %collective-permute-start.14) | collective-permute-done | bytes 1048608 | tf_op jit(solution)/shard_map/ppermute | solution.py:27
  78.7 5.8 %copy-done.2 = bf16[4096,2048]{1,0:T(8,128)(2,1)S(1)} copy-done((bf16[4096,2048]{1,0:T(8,128)(2,1)S(1)}, bf16[4096,2048]{1,0:T(8,128)(2,1)}, u32[]{:S(2)}) %copy-start.2) | copy-done | bytes 16777240
  85.8 6.4 %project.5 = (bf16[4096,2048]{1,0:T(8,128)(2,1)S(1)}, f32[384,2048]{1,0:T(8,128)S(1)}) custom-call(s32[2,8]{1,0:T(2,128)S(1)} %get-tuple-element.157.refs_0_, bf16[192,4096]{1,0:T(8,128)(2,1)} %refs_0_.1, bf16[192,4096]{1,0:T(8,128)(2,1)S(1)} %copy-done.5, ...), custom_call_target="tpu_custom_call", output_to_operand_aliasing={{1}: (7, {}), {0}: (8, {})} | custom-call | tf_op jit(solution)/shard_map/project/pallas_call | solution.py:213
  92.2 5.8 %copy-done.3 = bf16[4096,2048]{1,0:T(8,128)(2,1)} copy-done((bf16[4096,2048]{1,0:T(8,128)(2,1)}, bf16[4096,2048]{1,0:T(8,128)(2,1)S(1)}, u32[]{:S(2)}) %copy-start.3) | copy-done | bytes 16777240
  104.2 11.3 %project.6.refs_9_ = f32[384,2048]{1,0:T(8,128)S(1)} custom-call(s32[2,24]{1,0:T(2,128)S(1)} %pad_add_fusion.3.refs_0_, bf16[384,4096]{1,0:T(8,128)(2,1)} %bitcast.52.refs_1_.refs_3_, bf16[512,1024]{1,0:T(8,128)(2,1)S(1)} %copy-done.13, bf16[512,1024]{1,0:T(8,128)(2,1)} %constant_dynamic-update-slice_fusion.refs_4_.refs_3_, ...), custom_call_target="tpu_custom_call" | custom-call | tf_op jit(solution)/shard_map/project/pallas_call | solution.py:213
  115.5 12.3 %project.7 = (bf16[4096,2048]{1,0:T(8,128)(2,1)}, f32[384,2048]{1,0:T(8,128)S(1)}, f32[384,2048]{1,0:T(8,128)S(1)}, f32[384,128]{1,0:T(8,128)S(1)}, bf16[768,204...) custom-call(s32[2,8]{1,0:T(2,128)S(1)} %get-tuple-element.158.refs_0, ...), custom_call_target="tpu_custom_call", output_to_operand_aliasing={{1}: (8, {}), {2}: (9, {}), {0}: (11, {})} | custom-call | tf_op jit(solution)/shard_map/project/pallas_call | solution.py:213
  131.9 4.4 %all-to-all-start.1 = ((bf16[8,48,2048]{2,1,0:T(8,128)(2,1)}), bf16[8,48,2048]{2,1,0:T(8,128)(2,1)}, u32[]{:S(2)}, u32[]{:S(2)}) async-start(bf16[8,48,2048]{2,1,0:T(8,128)(2,1)} %bitcast.72), calls=%async_computation.1 | async-start | bytes 3145728 | tf_op jit(solution)/shard_map/all_to_all | solution.py:446
  142.7 6.7 %input_grad.4.refs_0_ = bf16[192,4096]{1,0:T(8,128)(2,1)} custom-call(bf16[192,2048]{1,0:T(8,128)(2,1)S(1)} %get-tuple-element.92.slopes_ref, bf16[4096,2048]{1,0:T(8,128)(2,1)} %get-tuple-element.93.head_ref), custom_call_target="tpu_custom_call" | custom-call | tf_op jit(solution)/shard_map/input_grad/pallas_call | solution.py:280
  149.4 6.7 %input_grad.5 = bf16[192,4096]{1,0:T(8,128)(2,1)} custom-call(bf16[192,2048]{1,0:T(8,128)(2,1)S(1)} %get-tuple-element.92.slopes_ref, bf16[4096,2048]{1,0:T(8,128)(2,1)} %get-tuple-element.93.head_ref, bf16[192,4096]{1,0:T(8,128)(2,1)} %input_grad.4.refs_0_), custom_call_target="tpu_custom_call", output_to_operand_aliasing={{}: (2, {})} | custom-call | tf_op jit(solution)/shard_map/input_grad/pallas_call | solution.py:280
  160.8 3.8 %slopes_of.3 = (bf16[192,2048]{1,0:T(8,128)(2,1)S(1)}, bf16[192,1024]{1,0:T(8,128)(2,1)S(1)}, bf16[192,1024]{1,0:T(8,128)(2,1)S(1)}) custom-call(s32[2,4]{1,0:T(2,128)S(1)} %pad_add_fusion.4.refs_0_, f32[384,2048]{1,0:T(8,128)S(1)} %get-tuple-element.87.refs_1_, f32[384,128]{1,0:T(8,128)S(1)} %copy-done.28, f32[192,128]{1,0:T(8,128)S(1)} %copy-done.30, ...), custom_call_target="tpu_custom_call" | custom-call | tf_op jit(solution)/shard_map/slopes_of/pallas_call | solution.py:256
  164.8 4.9 %turn.1.refs_1_ = bf16[4096,768]{1,0:T(8,128)(2,1)S(1)} custom-call(bf16[192,4096]{1,0:T(8,128)(2,1)} %refs_0_.1, bf16[192,4096]{1,0:T(8,128)(2,1)S(1)} %copy-done.7, bf16[192,4096]{1,0:T(8,128)(2,1)} %collective-permute-done.19.refs_2_, bf16[192,4096]{1,0:T(8,128)(2,1)} %collective-permute-done.20.refs_3_), custom_call_target="tpu_custom_call" | custom-call | tf_op jit(solution)/shard_map/turn/pallas_call | solution.py:60
  181.2 6.7 %input_grad.6.refs_0_ = bf16[192,4096]{1,0:T(8,128)(2,1)} custom-call(bf16[192,2048]{1,0:T(8,128)(2,1)S(1)} %get-tuple-element.117.slopes_ref, bf16[4096,2048]{1,0:T(8,128)(2,1)} %get-tuple-element.93.head_ref), custom_call_target="tpu_custom_call" | custom-call | tf_op jit(solution)/shard_map/input_grad/pallas_call | solution.py:280
  195.5 5.4 %collective-permute-done.26.refs_3_ = bf16[512,1024]{1,0:T(8,128)(2,1)S(1)} collective-permute-done((bf16[512,1024]{1,0:T(8,128)(2,1)S(1)}, bf16[512,1024]{1,0:T(8,128)(2,1)S(1)}, u32[]{:S(2)}, u32[]{:S(2)}) %collective-permute-start.26) | collective-permute-done | bytes 1048608 | tf_op jit(solution)/shard_map/ppermute | solution.py:27
  203.3 6.7 %input_grad.7 = bf16[192,4096]{1,0:T(8,128)(2,1)} custom-call(bf16[192,2048]{1,0:T(8,128)(2,1)S(1)} %get-tuple-element.117.slopes_ref, bf16[4096,2048]{1,0:T(8,128)(2,1)} %get-tuple-element.93.head_ref, bf16[192,4096]{1,0:T(8,128)(2,1)} %input_grad.6.refs_0_), custom_call_target="tpu_custom_call", output_to_operand_aliasing={{}: (2, {})} | custom-call | tf_op jit(solution)/shard_map/input_grad/pallas_call | solution.py:280
  215.7 3.2 %collective-permute-start.29 = (bf16[128,1024]{1,0:T(8,128)(2,1)S(1)}, bf16[128,1024]{1,0:T(8,128)(2,1)S(1)}, u32[]{:S(2)}, u32[]{:S(2)}) collective-permute-start(bf16[128,1024]{1,0:T(8,128)(2,1)S(1)} %get-tuple-element.136), channel_id=1, source_target_pairs={{0,3},{1,0},{2,1},{3,2},{4,7},{5,4},{6,5},{7,6},{8,11},{9,8},{10,9... | collective-permute-start | bytes 786440 | tf_op jit(solution)/shard_map/ppermute | solution.py:27
  219.2 4.0 %collective-permute-done.28 = bf16[128,1024]{1,0:T(8,128)(2,1)S(1)} collective-permute-done((bf16[128,1024]{1,0:T(8,128)(2,1)S(1)}, bf16[128,1024]{1,0:T(8,128)(2,1)S(1)}, u32[]{:S(2)}, u32[]{:S(2)}) %collective-permute-start.28) | collective-permute-done | bytes 262176 | tf_op jit(solution)/shard_map/ppermute | solution.py:27
  223.3 3.2 %collective-permute-done.30 = bf16[128,1024]{1,0:T(8,128)(2,1)S(1)} collective-permute-done((bf16[128,1024]{1,0:T(8,128)(2,1)S(1)}, bf16[128,1024]{1,0:T(8,128)(2,1)S(1)}, u32[]{:S(2)}, u32[]{:S(2)}) %collective-permute-start.30) | collective-permute-done | bytes 262176 | tf_op jit(solution)/shard_map/ppermute | solution.py:27
  228.9 4.1 %collective-permute-done.33 = bf16[128,1024]{1,0:T(8,128)(2,1)S(1)} collective-permute-done((bf16[128,1024]{1,0:T(8,128)(2,1)S(1)}, bf16[128,1024]{1,0:T(8,128)(2,1)S(1)}, u32[]{:S(2)}, u32[]{:S(2)}) %collective-permute-start.33) | collective-permute-done | bytes 262176 | tf_op jit(solution)/shard_map/ppermute | solution.py:27
  239.2 3.3 %collective-permute-done.34 = bf16[256,256]{1,0:T(8,128)(2,1)S(1)} collective-permute-done((bf16[256,256]{1,0:T(8,128)(2,1)S(1)}, bf16[256,256]{1,0:T(8,128)(2,1)S(1)}, u32[]{:S(2)}, u32[]{:S(2)}) %collective-permute-start.34) | collective-permute-done | bytes 131104 | tf_op jit(solution)/shard_map/ppermute | solution.py:368
  (180 shorter events, 98.4 us)
Async XLA Ops:
  12.9 19.7 %collective-permute-start.2 = (bf16[512,1024]{1,0:T(8,128)(2,1)S(1)}, bf16[512,1024]{1,0:T(8,128)(2,1)S(1)}, u32[]{:S(2)}, u32[]{:S(2)}) collective-permute-start(bf16[512,1024]{1,0:T(8,128)(2,1)S(1)} %pad_maximum_fusion.refs_3_.refs_2_), channel_id=1, source_target_pairs={{0,1},{1,2},{2,3},{3,0},{4,5},{5,6},{6,7},{7,4},{8,9},{9,10},{10,1... | collective-permute-start | bytes 3145736 | tf_op jit(solution)/shard_map/ppermute | solution.py:27
  14.9 17.7 %collective-permute-start.3 = (bf16[512,1024]{1,0:T(8,128)(2,1)S(1)}, bf16[512,1024]{1,0:T(8,128)(2,1)S(1)}, u32[]{:S(2)}, u32[]{:S(2)}) collective-permute-start(bf16[512,1024]{1,0:T(8,128)(2,1)S(1)} %pad_maximum_fusion.refs_3_.refs_2_), channel_id=1, source_target_pairs={{0,3},{1,0},{2,1},{3,2},{4,7},{5,4},{6,5},{7,6},{8,11},{9,8},{10,9... | collective-permute-start | bytes 3145736 | tf_op jit(solution)/shard_map/ppermute | solution.py:27
  17.1 19.3 %collective-permute-start.8 = (bf16[512,1024]{1,0:T(8,128)(2,1)S(1)}, bf16[512,1024]{1,0:T(8,128)(2,1)S(1)}, u32[]{:S(2)}, u32[]{:S(2)}) collective-permute-start(bf16[512,1024]{1,0:T(8,128)(2,1)S(1)} %pad_maximum_fusion.refs_3_.refs_2_), channel_id=1, source_target_pairs={{0,16},{16,0},{1,17},{17,1},{2,18},{18,2},{3,19},{19,3},{4,20},{20... | collective-permute-start | bytes 3145736 | tf_op jit(solution)/shard_map/ppermute | solution.py:31
  34.1 11.1 %collective-permute-start.10 = (bf16[512,1024]{1,0:T(8,128)(2,1)S(1)}, bf16[512,1024]{1,0:T(8,128)(2,1)}, u32[]{:S(2)}, u32[]{:S(2)}) collective-permute-start(bf16[512,1024]{1,0:T(8,128)(2,1)S(1)} %collective-permute-done.2.refs_5_.refs_4_), channel_id=1, source_target_pairs={{0,16},{16,0},{1,17},{17,1},{2,18},{18,2},{3,19},{19,3},{4,20},{20... | collective-permute-start | bytes 3145736 | tf_op jit(solution)/shard_map/ppermute | solution.py:31
  34.6 10.6 %collective-permute-start.11 = (bf16[512,1024]{1,0:T(8,128)(2,1)S(1)}, bf16[512,1024]{1,0:T(8,128)(2,1)}, u32[]{:S(2)}, u32[]{:S(2)}) collective-permute-start(bf16[512,1024]{1,0:T(8,128)(2,1)S(1)} %collective-permute-done.3.refs_6_.refs_5_), channel_id=1, source_target_pairs={{0,16},{16,0},{1,17},{17,1},{2,18},{18,2},{3,19},{19,3},{4,20},{20... | collective-permute-start | bytes 3145736 | tf_op jit(solution)/shard_map/ppermute | solution.py:31
  34.6 25.8 %collective-permute-start.6 = (bf16[512,1024]{1,0:T(8,128)(2,1)}, bf16[512,1024]{1,0:T(8,128)(2,1)}, u32[]{:S(2)}, u32[]{:S(2)}) collective-permute-start(bf16[512,1024]{1,0:T(8,128)(2,1)} %constant_dynamic-update-slice_fusion.refs_4_.refs_3_), channel_id=1, source_target_pairs={{0,1},{1,2},{2,3},{3,0},{4,5},{5,6},{6,7},{7,4},{8,9},{9,10},{10,1... | collective-permute-start | bytes 3145736 | tf_op jit(solution)/shard_map/ppermute | solution.py:27
  37.4 23.0 %collective-permute-start.7 = (bf16[512,1024]{1,0:T(8,128)(2,1)}, bf16[512,1024]{1,0:T(8,128)(2,1)}, u32[]{:S(2)}, u32[]{:S(2)}) collective-permute-start(bf16[512,1024]{1,0:T(8,128)(2,1)} %constant_dynamic-update-slice_fusion.refs_4_.refs_3_), channel_id=1, source_target_pairs={{0,3},{1,0},{2,1},{3,2},{4,7},{5,4},{6,5},{7,6},{8,11},{9,8},{10,9... | collective-permute-start | bytes 3145736 | tf_op jit(solution)/shard_map/ppermute | solution.py:27
  38.9 59.1 %all-to-all-start = ((bf16[8,48,4096]{2,1,0:T(8,128)(2,1)}), bf16[8,48,4096]{2,1,0:T(8,128)(2,1)}, u32[]{:S(2)}, u32[]{:S(2)}) async-start(bf16[8,48,4096]{2,1,0:T(8,128)(2,1)} %bitcast.73), calls=%async_computation | async-start | bytes 6291456 | tf_op jit(solution)/shard_map/all_to_all | solution.py:407
  60.5 16.2 %collective-permute-start.14 = (bf16[512,1024]{1,0:T(8,128)(2,1)S(1)}, bf16[512,1024]{1,0:T(8,128)(2,1)}, u32[]{:S(2)}, u32[]{:S(2)}) collective-permute-start(bf16[512,1024]{1,0:T(8,128)(2,1)S(1)} %copy-done.15), channel_id=1, source_target_pairs={{0,1},{1,2},{2,3},{3,0},{4,5},{5,6},{6,7},{7,4},{8,9},{9,10},{10,1... | collective-permute-start | bytes 3145736 | tf_op jit(solution)/shard_map/ppermute | solution.py:27
  61.1 15.5 %collective-permute-start.15 = (bf16[512,1024]{1,0:T(8,128)(2,1)}, bf16[512,1024]{1,0:T(8,128)(2,1)}, u32[]{:S(2)}, u32[]{:S(2)}) collective-permute-start(bf16[512,1024]{1,0:T(8,128)(2,1)} %collective-permute-done.7.refs_4_.refs_7_), channel_id=1, source_target_pairs={{0,3},{1,0},{2,1},{3,2},{4,7},{5,4},{6,5},{7,6},{8,11},{9,8},{10,9... | collective-permute-start | bytes 3145736 | tf_op jit(solution)/shard_map/ppermute | solution.py:27
  63.8 14.1 %collective-permute-start.12 = (bf16[512,1024]{1,0:T(8,128)(2,1)}, bf16[512,1024]{1,0:T(8,128)(2,1)}, u32[]{:S(2)}, u32[]{:S(2)}) collective-permute-start(bf16[512,1024]{1,0:T(8,128)(2,1)} %collective-permute-done.6.refs_3_.refs_6_), channel_id=1, source_target_pairs={{0,16},{16,0},{1,17},{17,1},{2,18},{18,2},{3,19},{19,3},{4,20},{20... | collective-permute-start | bytes 3145736 | tf_op jit(solution)/shard_map/ppermute | solution.py:31
  63.8 14.9 %collective-permute-start.13 = (bf16[512,1024]{1,0:T(8,128)(2,1)}, bf16[512,1024]{1,0:T(8,128)(2,1)}, u32[]{:S(2)}, u32[]{:S(2)}) collective-permute-start(bf16[512,1024]{1,0:T(8,128)(2,1)} %collective-permute-done.7.refs_4_.refs_7_), channel_id=1, source_target_pairs={{0,16},{16,0},{1,17},{17,1},{2,18},{18,2},{3,19},{19,3},{4,20},{20... | collective-permute-start | bytes 3145736 | tf_op jit(solution)/shard_map/ppermute | solution.py:31
  76.6 38.9 %collective-permute-start.16 = (bf16[512,1024]{1,0:T(8,128)(2,1)}, bf16[512,1024]{1,0:T(8,128)(2,1)}, u32[]{:S(2)}, u32[]{:S(2)}) collective-permute-start(bf16[512,1024]{1,0:T(8,128)(2,1)} %collective-permute-done.14.refs_4_), channel_id=1, source_target_pairs={{0,16},{16,0},{1,17},{17,1},{2,18},{18,2},{3,19},{19,3},{4,20},{20... | collective-permute-start | bytes 3145736 | tf_op jit(solution)/shard_map/ppermute | solution.py:31
  76.6 38.9 %collective-permute-start.17 = (bf16[512,1024]{1,0:T(8,128)(2,1)}, bf16[512,1024]{1,0:T(8,128)(2,1)}, u32[]{:S(2)}, u32[]{:S(2)}) collective-permute-start(bf16[512,1024]{1,0:T(8,128)(2,1)} %collective-permute-done.15.refs_5_), channel_id=1, source_target_pairs={{0,16},{16,0},{1,17},{17,1},{2,18},{18,2},{3,19},{19,3},{4,20},{20... | collective-permute-start | bytes 3145736 | tf_op jit(solution)/shard_map/ppermute | solution.py:31
  77.2 87.6 %collective-permute-start.19 = (bf16[192,4096]{1,0:T(8,128)(2,1)}, bf16[192,4096]{1,0:T(8,128)(2,1)}, u32[]{:S(2)}, u32[]{:S(2)}) collective-permute-start(bf16[192,4096]{1,0:T(8,128)(2,1)} %refs_0_.1), channel_id=1, source_target_pairs={{0,16},{16,0},{1,17},{17,1},{2,18},{18,2},{3,19},{19,3},{4,20},{20... | collective-permute-start | bytes 4718600 | tf_op jit(solution)/shard_map/ppermute | solution.py:31
  77.9 86.9 %collective-permute-start.20 = (bf16[192,4096]{1,0:T(8,128)(2,1)}, bf16[192,4096]{1,0:T(8,128)(2,1)}, u32[]{:S(2)}, u32[]{:S(2)}) collective-permute-start(bf16[192,4096]{1,0:T(8,128)(2,1)} %refs_1_.7), channel_id=1, source_target_pairs={{0,16},{16,0},{1,17},{17,1},{2,18},{18,2},{3,19},{19,3},{4,20},{20... | collective-permute-start | bytes 4718600 | tf_op jit(solution)/shard_map/ppermute | solution.py:31
  131.9 26.1 %all-to-all-start.1 = ((bf16[8,48,2048]{2,1,0:T(8,128)(2,1)}), bf16[8,48,2048]{2,1,0:T(8,128)(2,1)}, u32[]{:S(2)}, u32[]{:S(2)}) async-start(bf16[8,48,2048]{2,1,0:T(8,128)(2,1)} %bitcast.72), calls=%async_computation.1 | async-start | bytes 3145728 | tf_op jit(solution)/shard_map/all_to_all | solution.py:446
  142.2 13.9 %collective-permute-start.18 = (bf16[192,1024]{1,0:T(8,128)(2,1)S(1)}, bf16[192,1024]{1,0:T(8,128)(2,1)}, u32[]{:S(2)}, u32[]{:S(2)}) collective-permute-start(bf16[192,1024]{1,0:T(8,128)(2,1)S(1)} %get-tuple-element.94), channel_id=1, source_target_pairs={{0,16},{16,0},{1,17},{17,1},{2,18},{18,2},{3,19},{19,3},{4,20},{20... | collective-permute-start | bytes 1179656 | tf_op jit(solution)/shard_map/ppermute | solution.py:31
  173.3 16.1 %collective-permute-start.22 = (bf16[512,1024]{1,0:T(8,128)(2,1)S(1)}, bf16[512,1024]{1,0:T(8,128)(2,1)S(1)}, u32[]{:S(2)}, u32[]{:S(2)}) collective-permute-start(bf16[512,1024]{1,0:T(8,128)(2,1)S(1)} %get-tuple-element.101), channel_id=1, source_target_pairs={{0,4},{1,5},{2,6},{3,7},{4,8},{5,9},{6,10},{7,11},{8,12},{9,13},{1... | collective-permute-start | bytes 3145736 | tf_op jit(solution)/shard_map/ppermute | solution.py:27
  174.9 14.8 %collective-permute-start.23 = (bf16[512,1024]{1,0:T(8,128)(2,1)S(1)}, bf16[512,1024]{1,0:T(8,128)(2,1)S(1)}, u32[]{:S(2)}, u32[]{:S(2)}) collective-permute-start(bf16[512,1024]{1,0:T(8,128)(2,1)S(1)} %get-tuple-element.102), channel_id=1, source_target_pairs={{0,12},{1,13},{2,14},{3,15},{4,0},{5,1},{6,2},{7,3},{8,4},{9,5},{1... | collective-permute-start | bytes 3145736 | tf_op jit(solution)/shard_map/ppermute | solution.py:27
  179.1 21.8 %collective-permute-start.26 = (bf16[512,1024]{1,0:T(8,128)(2,1)S(1)}, bf16[512,1024]{1,0:T(8,128)(2,1)S(1)}, u32[]{:S(2)}, u32[]{:S(2)}) collective-permute-start(bf16[512,1024]{1,0:T(8,128)(2,1)S(1)} %get-tuple-element.111), channel_id=1, source_target_pairs={{0,12},{1,13},{2,14},{3,15},{4,0},{5,1},{6,2},{7,3},{8,4},{9,5},{1... | collective-permute-start | bytes 3145736 | tf_op jit(solution)/shard_map/ppermute | solution.py:27
  180.8 20.1 %collective-permute-start.27 = (bf16[512,1024]{1,0:T(8,128)(2,1)S(1)}, bf16[512,1024]{1,0:T(8,128)(2,1)S(1)}, u32[]{:S(2)}, u32[]{:S(2)}) collective-permute-start(bf16[512,1024]{1,0:T(8,128)(2,1)S(1)} %get-tuple-element.112), channel_id=1, source_target_pairs={{0,4},{1,5},{2,6},{3,7},{4,8},{5,9},{6,10},{7,11},{8,12},{9,13},{1... | collective-permute-start | bytes 3145736 | tf_op jit(solution)/shard_map/ppermute | solution.py:27
  192.1 19.7 %collective-permute-start.24 = (bf16[512,1024]{1,0:T(8,128)(2,1)S(1)}, bf16[512,1024]{1,0:T(8,128)(2,1)S(1)}, u32[]{:S(2)}, u32[]{:S(2)}) collective-permute-start(bf16[512,1024]{1,0:T(8,128)(2,1)S(1)} %get-tuple-element.109), channel_id=1, source_target_pairs={{0,4},{1,5},{2,6},{3,7},{4,8},{5,9},{6,10},{7,11},{8,12},{9,13},{1... | collective-permute-start | bytes 3145736 | tf_op jit(solution)/shard_map/ppermute | solution.py:27
  193.5 18.7 %collective-permute-start.25 = (bf16[512,1024]{1,0:T(8,128)(2,1)S(1)}, bf16[512,1024]{1,0:T(8,128)(2,1)S(1)}, u32[]{:S(2)}, u32[]{:S(2)}) collective-permute-start(bf16[512,1024]{1,0:T(8,128)(2,1)S(1)} %get-tuple-element.110), channel_id=1, source_target_pairs={{0,12},{1,13},{2,14},{3,15},{4,0},{5,1},{6,2},{7,3},{8,4},{9,5},{1... | collective-permute-start | bytes 3145736 | tf_op jit(solution)/shard_map/ppermute | solution.py:27
  (51 other events, 248.0 us)
